TPU v7x, 32 devices: a whole 2x2x4 slice. The times are simulated.
32 devices in a mesh: dp: 8 (over z, x), mp: 4 (over y, core).
Axes of the slice: x: 2, y: 2, z: 4, core: 2. Of those that a mesh axis runs over, the one named last changes fastest.
Arguments:
- tokens: bfloat16 [13824, 768], P('dp', 'mp'), may hold values from -6 to 6
- w_qkv: bfloat16 [768, 3, 768], P(None, None, 'mp'), may hold values from -0.21875 to 0.21875
- b_qkv: bfloat16 [3, 768], P(None, 'mp'), may hold values from -3 to 3
- freqs: float32 [2, 12, 32], P(None, 'mp'), may hold values from -0.8 to 0.8
- w_out: bfloat16 [768, 768], P('mp'), may hold values from -0.875 to 0.875
- b_out: bfloat16 [768], P('mp'), may hold values from -2 to 2
- norm1_gain: bfloat16 [768], P('mp'), may hold values from 0.5 to 1.5
- norm1_bias: bfloat16 [768], P('mp'), may hold values from -2 to 2
- norm2_gain: bfloat16 [768], P('mp'), may hold values from 0.5 to 1.5
- norm2_bias: bfloat16 [768], P('mp'), may hold values from -2 to 2
- w_up: bfloat16 [768, 3072], P(None, 'mp'), may hold values from -0.21875 to 0.21875
- b_up: bfloat16 [3072], P('mp'), may hold values from -3 to 3
- w_down: bfloat16 [3072, 768], P('mp'), may hold values from -0.109375 to 0.109375
- b_down: bfloat16 [768], P('mp'), may hold values from -2 to 2
- cotangent: bfloat16 [13824, 768], P('dp', 'mp'), may hold values from -6 to 6
- keep_mask: int32 [13824], P('dp'), may hold values from 0 to 1, as said below
- coords: int32 [2, 13824], P(None, 'dp'), may hold values from 0 to 23, as said below
- block_group: int32 [8], P('dp'), may hold values from 0 to 1, as said below
Outputs:
- block_out: bfloat16 [13824, 768], P('dp', 'mp')
- input_grad: float32 [13824, 768], P('dp', 'mp')
- grad_w_qkv: float32 [768, 3, 768], P(None, None, 'mp')
- grad_b_qkv: float32 [3, 768], P(None, 'mp')
- grad_freqs: float32 [2, 12, 32], P(None, 'mp')
- grad_w_out: float32 [768, 768], P('mp')
- grad_b_out: float32 [768], P('mp')
- grad_norm1_gain: float32 [768], P('mp')
- grad_norm1_bias: float32 [768], P('mp')
- grad_norm2_gain: float32 [768], P('mp')
- grad_norm2_bias: float32 [768], P('mp')
- grad_w_up: float32 [768, 3072], P(None, 'mp')
- grad_b_up: float32 [3072], P('mp')
- grad_w_down: float32 [3072, 768], P('mp')
- grad_b_down: float32 [768], P('mp')
Inputs may be any that keep to these rules, and one draw needn't show every extreme that they name: `keep_mask`: A block of group 0 holds 8 images of 196 slots one after another and then padding; a block of group 1 holds 3 images of 576 slots. Within each image the kept slots are its first ones, a quarter or more of its patches; padding is never kept; the first image of the first block of each group keeps all. `coords`: A kept slot holds the row and column of a patch of its image's grid (14 or 24 patches a side), each patch at most once per image; slots not kept hold 0. `block_group`: the group never falls from one block to the next, and both groups occur.
All inputs are finite; a program needn't handle non-finite values.
Results may differ from a plain program's by a relative error of at most 0.015.
The roundings to bfloat16 on the way count: a program that leaves them out, or rounds other values in their place, can miss the bound.
Values may be sent and summed in bfloat16 or wider, within the bound.
A program may use at most 128 MiB of HBM per device.

v0:
```python
import jax
import jax.numpy as jnp
from jax import lax
from jax.sharding import PartitionSpec as P

HEAD_DIM = 64
GRID_LO = 14
SLOTS = 576


norm_eps = 1e-06
root_half = 0.7071067811865476
inv_root_two_pi = 0.3989422804014327


def norm_forward(values, gain, shift_bias):
    row_mean = jnp.mean(values, axis=-1, keepdims=True)
    row_square = jnp.mean(values * values, axis=-1, keepdims=True)
    inverse = lax.rsqrt(row_square - row_mean * row_mean + norm_eps)
    normed = (values - row_mean) * inverse
    return (normed * gain + shift_bias, normed, inverse)


def norm_backward(grad_normed, normed, inverse, gain):
    scaled = grad_normed * gain
    return inverse * (
        scaled
        - jnp.mean(scaled, axis=-1, keepdims=True)
        - normed * jnp.mean(scaled * normed, axis=-1, keepdims=True)
    )


def rotate_pairs(vectors, cosine_table, sine_table):
    split_at = vectors.shape[-1] // 2
    front_part = vectors[..., :split_at]
    back_part = vectors[..., split_at:]
    return jnp.concatenate(
        [
            front_part * cosine_table - back_part * sine_table,
            front_part * sine_table + back_part * cosine_table,
        ],
        axis=-1,
    )


def rotate_back(grads, rotated, cosine_table, sine_table):
    split_at = grads.shape[-1] // 2
    grad_front = grads[..., :split_at]
    grad_rear = grads[..., split_at:]
    rot_front = rotated[..., :split_at]
    rot_rear = rotated[..., split_at:]
    unrotated = jnp.concatenate(
        [
            grad_front * cosine_table + grad_rear * sine_table,
            grad_rear * cosine_table - grad_front * sine_table,
        ],
        axis=-1,
    )
    return (unrotated, grad_rear * rot_front - grad_front * rot_rear)


def masked_scores(query_blk, key_all, segment_blk, segment_ids, key_keep):
    scale_factor = query_blk.shape[-1] ** (-0.5)
    scores = scale_factor * jnp.einsum(
        "qhd,khd->hqk", query_blk, key_all, preferred_element_type=jnp.float32
    )
    allowed = (segment_blk[:, None] == segment_ids[None, :]) & key_keep[None, :]
    return jnp.where(allowed[None], scores, -1e30)


def contract_rows(left_side, right_side):
    return lax.dot_general(
        left_side, right_side, (((0,), (0,)), ((), ())), preferred_element_type=jnp.float32
    )


def contract_cols(left_side, right_side):
    return lax.dot_general(
        left_side, right_side, (((1,), (1,)), ((), ())), preferred_element_type=jnp.float32
    )


def local(
    tokens,
    w_qkv,
    b_qkv,
    freqs,
    w_out,
    b_out,
    norm1_gain,
    norm1_bias,
    norm2_gain,
    norm2_bias,
    w_up,
    b_up,
    w_down,
    b_down,
    cotangent,
    keep_mask,
    coords,
    block_group,
):
    row_count, width_loc = tokens.shape
    heads_loc = freqs.shape[1]
    block_count = row_count // SLOTS
    column = lax.axis_index("mp") * width_loc
    keep_float = keep_mask.astype(jnp.float32)
    keep_col = keep_float[:, None]
    group_now = block_group[0]
    kept_total = jnp.sum(keep_float)
    low_flag = (group_now == 0).astype(jnp.float32)
    counts = lax.psum(jnp.stack([kept_total * low_flag, kept_total * (1.0 - low_flag)]), "dp")
    own_weight = jnp.where(group_now == 0, counts[0], counts[1]) / (counts[0] + counts[1])
    row_index = jnp.arange(row_count, dtype=jnp.int32)
    segment_size = jnp.where(group_now == 0, GRID_LO * GRID_LO, SLOTS).astype(jnp.int32)
    segment_ids = row_index // segment_size
    key_keep = keep_mask > 0
    whole_tokens, whole_cot, gain_one, bias_one, gain_two, bias_two, out_bias = (
        lax.all_gather(tokens, "mp", axis=1, tiled=True),
        lax.all_gather(cotangent, "mp", axis=1, tiled=True),
        lax.all_gather(norm1_gain, "mp", axis=0, tiled=True),
        lax.all_gather(norm1_bias, "mp", axis=0, tiled=True),
        lax.all_gather(norm2_gain, "mp", axis=0, tiled=True),
        lax.all_gather(norm2_bias, "mp", axis=0, tiled=True),
        lax.all_gather(b_out, "mp", axis=0, tiled=True),
    )
    stream = whole_tokens.astype(jnp.float32)
    normed_one_out, normed_one, inverse_one = norm_forward(
        stream, gain_one.astype(jnp.float32), bias_one.astype(jnp.float32)
    )
    normed_one_low = normed_one_out.astype(jnp.bfloat16)
    projected = jnp.einsum(
        "rd,dce->rce", normed_one_low, w_qkv, preferred_element_type=jnp.float32
    ) + b_qkv.astype(jnp.float32)
    coord_rows = coords[0].astype(jnp.float32)
    coord_cols = coords[1].astype(jnp.float32)
    angles = coord_rows[:, None, None] * freqs[0][None] + coord_cols[:, None, None] * freqs[1][None]
    cosine_table = jnp.cos(angles)
    sine_table = jnp.sin(angles)
    head_shape = (row_count, heads_loc, HEAD_DIM)
    query_rot = rotate_pairs(projected[:, 0].reshape(head_shape), cosine_table, sine_table)
    key_rot = rotate_pairs(projected[:, 1].reshape(head_shape), cosine_table, sine_table)
    query_low = query_rot.astype(jnp.bfloat16)
    key_low = key_rot.astype(jnp.bfloat16)
    value_low = projected[:, 2].astype(jnp.bfloat16).reshape(head_shape)
    block_shape = (block_count, SLOTS, heads_loc, HEAD_DIM)
    segment_blocks = segment_ids.reshape(block_count, SLOTS)

    def attend_block(inputs):
        query_blk, segment_blk = inputs
        scores = masked_scores(query_blk, key_low, segment_blk, segment_ids, key_keep)
        row_max = jnp.max(scores, axis=-1, keepdims=True)
        exponent = jnp.exp(scores - row_max)
        summed = jnp.sum(exponent, axis=-1, keepdims=True)
        attn_probs = (exponent / summed).astype(jnp.bfloat16)
        output = jnp.einsum(
            "hqk,khd->qhd", attn_probs, value_low, preferred_element_type=jnp.float32
        )
        return (output.astype(jnp.bfloat16), (row_max + jnp.log(summed))[..., 0])

    attended_blocks, log_total = lax.map(
        attend_block, (query_low.reshape(block_shape), segment_blocks)
    )
    attended = attended_blocks.reshape(row_count, width_loc)
    head_terms = jnp.dot(attended, w_out, preferred_element_type=jnp.float32)
    mid = stream + (lax.psum(head_terms, "mp") + out_bias.astype(jnp.float32))
    normed_two_out, normed_two, inverse_two = norm_forward(
        mid, gain_two.astype(jnp.float32), bias_two.astype(jnp.float32)
    )
    normed_two_low = normed_two_out.astype(jnp.bfloat16)
    mid_own = lax.dynamic_slice_in_dim(mid, column, width_loc, 1)
    hidden_pre = jnp.dot(normed_two_low, w_up, preferred_element_type=jnp.float32) + b_up.astype(
        jnp.float32
    )
    activated = jax.nn.gelu(hidden_pre, approximate=False).astype(jnp.bfloat16)
    mlp_terms = jnp.dot(activated, w_down, preferred_element_type=jnp.float32)
    mlp_own = lax.psum_scatter(
        mlp_terms.astype(jnp.bfloat16), "mp", scatter_dimension=1, tiled=True
    ).astype(jnp.float32)
    block_out = (keep_col * (mid_own + (mlp_own + b_down.astype(jnp.float32)))).astype(jnp.bfloat16)
    grad_out_full = keep_col * whole_cot.astype(jnp.float32)
    grad_out_own = keep_col * cotangent.astype(jnp.float32)
    grad_out_low = grad_out_full.astype(jnp.bfloat16)
    grad_b_down = jnp.sum(grad_out_own, axis=0)
    grad_w_down = contract_rows(activated, grad_out_low)
    grad_act = contract_cols(grad_out_low, w_down)
    derivative = 0.5 * (
        1.0 + lax.erf(hidden_pre * root_half)
    ) + hidden_pre * inv_root_two_pi * jnp.exp(-0.5 * hidden_pre * hidden_pre)
    grad_pre = (grad_act * derivative).astype(jnp.bfloat16)
    grad_b_up = jnp.sum(grad_pre.astype(jnp.float32), axis=0)
    grad_w_up = contract_rows(normed_two_low, grad_pre)
    norm_two_terms = contract_cols(grad_pre, w_up)
    grad_normed_two = lax.psum(norm_two_terms, "mp")
    grad_gain_two = lax.dynamic_slice_in_dim(
        jnp.sum(grad_normed_two * normed_two, axis=0), column, width_loc, 0
    )
    grad_bias_two = lax.dynamic_slice_in_dim(jnp.sum(grad_normed_two, axis=0), column, width_loc, 0)
    grad_mid = grad_out_full + norm_backward(
        grad_normed_two, normed_two, inverse_two, gain_two.astype(jnp.float32)
    )
    grad_mid_low = grad_mid.astype(jnp.bfloat16)
    grad_mid_own = lax.dynamic_slice_in_dim(grad_mid, column, width_loc, 1)
    grad_b_out = lax.dynamic_slice_in_dim(
        jnp.sum(grad_mid_low.astype(jnp.float32), axis=0), column, width_loc, 0
    )
    grad_w_out = contract_rows(attended, grad_mid_low)
    grad_attended = contract_cols(grad_mid_low, w_out).astype(jnp.bfloat16).reshape(block_shape)
    scale_factor = HEAD_DIM ** (-0.5)

    def back_block(carry, inputs):
        key_sum, value_sum = carry
        query_blk, segment_blk, grad_blk, log_blk = inputs
        scores = masked_scores(query_blk, key_low, segment_blk, segment_ids, key_keep)
        attn_probs = jnp.exp(scores - log_blk[..., None])
        grad_probs = jnp.einsum(
            "qhd,khd->hqk", grad_blk, value_low, preferred_element_type=jnp.float32
        )
        grad_scores = (
            attn_probs * (grad_probs - jnp.sum(attn_probs * grad_probs, axis=-1, keepdims=True))
        ).astype(jnp.bfloat16)
        grad_query = scale_factor * jnp.einsum(
            "hqk,khd->qhd", grad_scores, key_low, preferred_element_type=jnp.float32
        )
        key_sum = key_sum + scale_factor * jnp.einsum(
            "hqk,qhd->khd", grad_scores, query_blk, preferred_element_type=jnp.float32
        )
        value_sum = value_sum + jnp.einsum(
            "hqk,qhd->khd",
            attn_probs.astype(jnp.bfloat16),
            grad_blk,
            preferred_element_type=jnp.float32,
        )
        return ((key_sum, value_sum), grad_query.astype(jnp.bfloat16))

    empty_sum = jnp.zeros(head_shape, jnp.float32)
    (key_total, value_total), grad_query = lax.scan(
        back_block,
        (empty_sum, empty_sum),
        (query_low.reshape(block_shape), segment_blocks, grad_attended, log_total),
    )
    grad_key = key_total.astype(jnp.bfloat16)
    grad_value = value_total.astype(jnp.bfloat16)
    grad_query_raw, angle_query = rotate_back(
        grad_query.reshape(head_shape).astype(jnp.float32), query_rot, cosine_table, sine_table
    )
    grad_key_raw, angle_key = rotate_back(
        grad_key.astype(jnp.float32), key_rot, cosine_table, sine_table
    )
    grad_angle = angle_query + angle_key
    grad_freqs = jnp.stack(
        [
            jnp.sum(coord_rows[:, None, None] * grad_angle, axis=0),
            jnp.sum(coord_cols[:, None, None] * grad_angle, axis=0),
        ]
    )
    grad_projected = jnp.stack(
        [
            grad_query_raw.reshape(row_count, width_loc),
            grad_key_raw.reshape(row_count, width_loc),
            grad_value.reshape(row_count, width_loc).astype(jnp.float32),
        ],
        axis=1,
    ).astype(jnp.bfloat16)
    grad_b_qkv = jnp.sum(grad_projected.astype(jnp.float32), axis=0)
    grad_w_qkv = jnp.einsum(
        "rd,rce->dce", normed_one_low, grad_projected, preferred_element_type=jnp.float32
    )
    norm_one_terms = jnp.einsum(
        "rce,dce->rd", grad_projected, w_qkv, preferred_element_type=jnp.float32
    )
    grad_normed_one = lax.psum(norm_one_terms, "mp")
    grad_gain_one = lax.dynamic_slice_in_dim(
        jnp.sum(grad_normed_one * normed_one, axis=0), column, width_loc, 0
    )
    grad_bias_one = lax.dynamic_slice_in_dim(jnp.sum(grad_normed_one, axis=0), column, width_loc, 0)
    grad_stream = norm_backward(
        grad_normed_one, normed_one, inverse_one, gain_one.astype(jnp.float32)
    )
    input_grad = grad_mid_own + lax.dynamic_slice_in_dim(grad_stream, column, width_loc, 1)
    all_sums = lax.psum(
        (
            own_weight * grad_w_qkv,
            own_weight * grad_b_qkv,
            own_weight * grad_freqs,
            own_weight * grad_w_out,
            own_weight * grad_b_out,
            own_weight * grad_gain_one,
            own_weight * grad_bias_one,
            own_weight * grad_gain_two,
            own_weight * grad_bias_two,
            own_weight * grad_w_up,
            own_weight * grad_b_up,
            own_weight * grad_w_down,
            own_weight * grad_b_down,
        ),
        "dp",
    )
    return (
        block_out,
        input_grad,
        all_sums[0],
        all_sums[1],
        all_sums[2],
        all_sums[3],
        all_sums[4],
        all_sums[5],
        all_sums[6],
        all_sums[7],
        all_sums[8],
        all_sums[9],
        all_sums[10],
        all_sums[11],
        all_sums[12],
    )


def solution(mesh):
    return jax.shard_map(
        local,
        mesh=mesh,
        in_specs=(
            P("dp", "mp"),
            P(None, None, "mp"),
            P(None, "mp"),
            P(None, "mp", None),
            P("mp", None),
            P("mp"),
            P("mp"),
            P("mp"),
            P("mp"),
            P("mp"),
            P(None, "mp"),
            P("mp"),
            P("mp", None),
            P("mp"),
            P("dp", "mp"),
            P("dp"),
            P(None, "dp"),
            P("dp"),
        ),
        out_specs=(
            P("dp", "mp"),
            P("dp", "mp"),
            P(None, None, "mp"),
            P(None, "mp"),
            P(None, "mp", None),
            P("mp", None),
            P("mp"),
            P("mp"),
            P("mp"),
            P("mp"),
            P("mp"),
            P(None, "mp"),
            P("mp"),
            P("mp", None),
            P("mp"),
        ),
        check_vma=False,
    )
```

profile of v0, /device:TPU:0, one launch (start us, length us, event | category | flops | bytes accessed | tf_op | source)
XLA Modules:
  0.0 870.7 jit_solution(13086328898767809821)
XLA Ops:
  16.2 13.9 %all-reduce.7 = (bf16[768]{0:T(1024)(128)(2,1)S(1)}, bf16[768]{0:T(1024)(128)(2,1)S(1)}, bf16[768]{0:T(1024)(128)(2,1)}, bf16[768]{0:T(1024)(128)(2,1)}, bf16[768]{0:T(1024)(128)(2,1)}) all-reduce(bf16[768]{0:T(1024)(128)(2,1)S(1)} %dynamic-update-slice.1, ...), channel_id=1, replica_groups=mesh['dp'=8,'mp'=4] {'mp'}, use_global_device_ids=true, to_apply=%add.1 | all-reduce | flops 3840 | bytes 15360
  32.7 6.1 all-gather.3.cloned.1.call-done
  38.8 4.6 copy.55
  43.4 2.6 convert_reduce_fusion
  46.1 4.3 fusion.74
  52.2 3.8 fusion.82
  60.1 76.1 %while.28 = (s32[]{:T(128)}, bf16[3,576,3,64]{1,3,2,0:T(8,128)(2,1)}, f32[3,3,576]{2,1,0:T(4,128)}, s32[3,576]{1,0:T(4,128)S(1)}, pred[1728]{0:T(1024)(128)(4,1)...) while((s32[]{:T(128)}, ...), condition=%wide.region_5.6_spmd.clone, body=%wide.region_2.5_spmd.clone.sunk | while | flops 802357056 | bytes 42155340 | solution.py:161
  61.2 8.1 fusion.139
  69.3 6.7 fusion.140
  76.0 9.0 %fusion.141 = bf16[3,576,3,64]{1,3,2,0:T(8,128)(2,1)} fusion(bf16[3,576,3,64]{1,3,2,0:T(8,128)(2,1)} %get-tuple-element.589, s32[]{:T(128)S(6)} %copy.84, bf16[1728,3,64]{0,2,1:T(8,128)(2,1)S(1)} %get-tuple-element.606, f32[3,576,1728]{2,1,0:T(8,128)} %get-tuple-element.560, f32[3,576]{1,0:T(4,128)S(1)} %fusion.140, ...), kind=kOutput, calls=%fused_computation.11.clone.1 | convolution fusion | flops 397246464 | bytes 14304772 | tf_op jit(solution)/shard_map/while/body/eval_jaxpr/hqk,khd->qhd/dot_general | solution.py:156
  86.5 8.1 fusion.139
  94.6 6.7 fusion.140
  101.3 9.0 %fusion.141 = bf16[3,576,3,64]{1,3,2,0:T(8,128)(2,1)} fusion(bf16[3,576,3,64]{1,3,2,0:T(8,128)(2,1)} %get-tuple-element.589, s32[]{:T(128)S(6)} %copy.84, bf16[1728,3,64]{0,2,1:T(8,128)(2,1)S(1)} %get-tuple-element.606, f32[3,576,1728]{2,1,0:T(8,128)} %get-tuple-element.560, f32[3,576]{1,0:T(4,128)S(1)} %fusion.140, ...), kind=kOutput, calls=%fused_computation.11.clone.1 | convolution fusion | flops 397246464 | bytes 14304772 | tf_op jit(solution)/shard_map/while/body/eval_jaxpr/hqk,khd->qhd/dot_general | solution.py:156
  111.8 8.1 fusion.139
  119.9 6.7 fusion.140
  126.6 9.0 %fusion.141 = bf16[3,576,3,64]{1,3,2,0:T(8,128)(2,1)} fusion(bf16[3,576,3,64]{1,3,2,0:T(8,128)(2,1)} %get-tuple-element.589, s32[]{:T(128)S(6)} %copy.84, bf16[1728,3,64]{0,2,1:T(8,128)(2,1)S(1)} %get-tuple-element.606, f32[3,576,1728]{2,1,0:T(8,128)} %get-tuple-element.560, f32[3,576]{1,0:T(4,128)S(1)} %fusion.140, ...), kind=kOutput, calls=%fused_computation.11.clone.1 | convolution fusion | flops 397246464 | bytes 14304772 | tf_op jit(solution)/shard_map/while/body/eval_jaxpr/hqk,khd->qhd/dot_general | solution.py:156
  136.8 2.7 copy.57
  139.5 2.4 reshape.258
  142.0 3.3 fusion.92
  146.1 5.0 copy.59
  151.1 98.1 %all-reduce.13.cloned.1.call-done = f32[1728,768]{1,0:T(8,128)} async-done(((f32[1728,768]{1,0:T(8,128)}), f32[1728,768]{1,0:T(8,128)}) %all-reduce.13.cloned.1.call-update) | async-done | bytes 5308432 | tf_op jit(solution)/shard_map/psum | solution.py:166
  249.2 4.5 fusion.88
  254.9 14.8 %fusion.51 = (bf16[1728,768]{1,0:T(8,128)(2,1)}, f32[1728,768]{1,0:T(8,128)S(1)}) fusion(f32[768]{0:T(1024)S(1)} %convert_element_type.171, bf16[1728,768]{1,0:T(8,128)(2,1)S(1)} %add_convert_fusion, bf16[768,768]{1,0:T(8,128)(2,1)S(1)} %copy-done), kind=kOutput, calls=%fused_computation.70 | convolution fusion | flops 2126020608 | bytes 11799552 | tf_op jit(solution)/shard_map/dot_general | solution.py:172
  269.8 4.9 convert_reduce_fusion.1
  276.2 4.6 fusion.93
  283.5 21.8 %psum.122 = f32[2]{0:T(128)} all-reduce(f32[2]{0:T(128)S(1)} %pad_maximum_fusion.5), channel_id=1, replica_groups=mesh['dp'=8,'mp'=4] {'dp'}, use_global_device_ids=true, to_apply=%region_20.21 | all-reduce | flops 2 | bytes 16 | tf_op jit(solution)/shard_map/psum | solution.py:112
  305.3 6.0 fusion.67
  311.4 73.3 %all-reduce.15.cloned.1.call-done = f32[1728,768]{1,0:T(8,128)} async-done(((f32[1728,768]{1,0:T(8,128)}), f32[1728,768]{1,0:T(8,128)}) %all-reduce.15.cloned.1.call-update) | async-done | bytes 5308432 | tf_op jit(solution)/shard_map/psum | solution.py:194
  384.8 6.1 multiply_reduce_fusion.1
  391.2 5.4 convert_reduce_fusion.2
  396.6 2.4 copy-done.3
  400.8 2.5 reshape.259
  405.2 82.9 %while.29 = (s32[]{:T(128)}, f32[1728,3,64]{0,2,1:T(8,128)S(1)}, f32[1728,3,64]{0,2,1:T(8,128)}, bf16[3,576,3,64]{1,3,2,0:T(8,128)(2,1)}, bf16[3,576,3,64]{1,3,2...) while((s32[]{:T(128)}, f32[1728,3,64]{0,2,1:T(8,128)S(1)}, ...), condition=%wide.region_15.16_spmd.clone, body=%wide.region_13.15_spmd.clone.sunk | while | flops 1959702272 | bytes 119148544 | solution.py:237
  407.7 3.2 fusion.151
  410.9 3.6 fusion.153
  414.5 6.7 multiply_reduce_fusion.11
  421.2 6.9 multiply_convert_fusion.3
  428.1 2.6 fusion.154
  430.7 2.2 fusion.152
  435.3 3.2 fusion.151
  438.5 3.6 fusion.153
  442.1 6.7 multiply_reduce_fusion.11
  448.8 6.8 multiply_convert_fusion.3
  455.7 2.6 fusion.154
  458.3 2.2 fusion.152
  462.9 3.2 fusion.151
  466.1 3.6 fusion.153
  469.7 6.7 multiply_reduce_fusion.11
  476.4 6.8 multiply_convert_fusion.3
  483.3 2.6 fusion.154
  489.6 3.0 copy.62
  492.6 3.6 reshape.260
  496.3 5.5 subtract_add_fusion
  501.8 2.8 multiply_reduce_fusion.9
  505.1 4.7 convolution_bitcast_fusion
  513.7 7.4 convolution_multiply_fusion.3
  521.1 5.9 convolution_multiply_fusion.2
  536.5 2.6 multiply_reduce_fusion.7
  540.3 73.5 %all-reduce.17.cloned.1.call-done = f32[1728,768]{1,0:T(8,128)} async-done(((f32[1728,768]{1,0:T(8,128)}), f32[1728,768]{1,0:T(8,128)}) %all-reduce.17.cloned.1.call-update) | async-done | bytes 5308432 | tf_op jit(solution)/shard_map/psum | solution.py:272
  613.7 7.5 fusion.86
  621.4 39.9 %all-reduce.5 = (f32[3,192]{1,0:T(4,128)}, f32[2,3,32]{2,1,0:T(4,128)S(1)}, f32[192]{0:T(256)}, f32[192]{0:T(256)}, f32[192]{0:T(256)}, /*index=5*/f32[192]{0:T(256)}, f32[192]{0:T(256)}, f32[768]{0:T(1024)}, f32[192]{0:T(256)}) all-reduce(f32[3,192]{1,0:T(4,128)S(1)} %broadcast_multiply_fusion.9, ...), channel_id=1, replica_groups=mesh['dp'=8,'mp'=4] {'dp'}, use_global_device_ids=true, to_apply=%region_23.24 | all-reduce | flops 2688 | bytes 21504 | tf_op jit(solution)/shard_map/psum | solution.py:281
  661.9 4.5 fusion.70
  668.0 187.8 %all-reduce.19.cloned.1.call-done = (f32[768,3,192]{0,2,1:T(8,128)}, f32[192,768]{1,0:T(8,128)}, f32[768,768]{1,0:T(8,128)}, f32[768,768]{1,0:T(8,128)}) async-done(((f32[768,3,192]{0,2,1:T(8,128)}, f32[192,768]{1,0:T(8,128)}, f32[768,768]{1,0:T(8,128)}, f32[768,768]{1,0:T(8,128)}), (f32[768,3,192]{0,2,1:T(8,128)}, f32[192,768]{1,0:T(8,128)}, f32[768,768]{1,0:T(8,128)}, ...) | async-done | bytes 7077904 | tf_op jit(solution)/shard_map/psum | solution.py:281
  855.8 2.9 copy.110
  (252 shorter events, 60.1 us)
Async XLA Ops:
  7.2 247.7 %copy-start = (bf16[768,768]{1,0:T(8,128)(2,1)S(1)}, bf16[768,768]{1,0:T(8,128)(2,1)}, u32[]{:S(2)}) copy-start(bf16[768,768]{1,0:T(8,128)(2,1)} %param.32) | copy-start | bytes 3538948
  7.2 38.9 %copy-start.53 = (bf16[768,3,192]{0,2,1:T(8,128)(2,1)S(1)}, bf16[768,3,192]{0,2,1:T(8,128)(2,1)}, u32[]{:S(2)}) copy-start(bf16[768,3,192]{0,2,1:T(8,128)(2,1)} %param.23) | copy-start | bytes 2654212
  7.2 31.6 %all-gather.3.cloned.1.call-start = ((), (), s32[]{:S(2)}) async-start(), calls=%async_computation.1 | async-start | bytes 3440640 | tf_op jit(solution)/shard_map/all_gather | solution.py:119
  7.9 138.1 %all-gather.5.cloned.1.call-start = ((), (), s32[]{:S(2)}) async-start(), calls=%async_computation.3 | async-start | bytes 3440640 | tf_op jit(solution)/shard_map/all_gather | solution.py:120
  8.7 240.5 %all-reduce.13.cloned.1.call-start = ((), (), s32[]{:S(2)}) async-start(), calls=%async_computation.2 | async-start | bytes 10616832 | tf_op jit(solution)/shard_map/psum | solution.py:166
  30.1 20.3 %copy-start.44 = (f32[768]{0:T(1024)}, f32[768]{0:T(1024)S(1)}, u32[]{:S(2)}) copy-start(f32[768]{0:T(1024)S(1)} %convert_element_type.159) | copy-start | bytes 9220
  30.9 19.6 %copy-start.42 = (f32[768]{0:T(1024)}, f32[768]{0:T(1024)S(1)}, u32[]{:S(2)}) copy-start(f32[768]{0:T(1024)S(1)} %convert_element_type.158) | copy-start | bytes 9220
  32.7 18.4 %copy-start.22 = (f32[1728]{0:T(1024)}, f32[1728]{0:T(1024)S(1)}, u32[]{:S(2)}) copy-start(f32[1728]{0:T(1024)S(1)} %get-tuple-element.320) | copy-start | bytes 20740
  32.7 18.4 %copy-start.24 = (f32[1728]{0:T(1024)}, f32[1728]{0:T(1024)S(1)}, u32[]{:S(2)}) copy-start(f32[1728]{0:T(1024)S(1)} %get-tuple-element.321) | copy-start | bytes 20740
  32.7 18.4 %copy-start.36 = (f32[3,32]{1,0:T(4,128)}, f32[3,32]{1,0:T(4,128)S(1)}, u32[]{:S(2)}) copy-start(f32[3,32]{1,0:T(4,128)S(1)} %get-tuple-element.427) | copy-start | bytes 1156
  32.7 18.4 %copy-start.38 = (f32[3,32]{1,0:T(4,128)}, f32[3,32]{1,0:T(4,128)S(1)}, u32[]{:S(2)}) copy-start(f32[3,32]{1,0:T(4,128)S(1)} %get-tuple-element.428) | copy-start | bytes 1156
  46.1 4.4 copy-start.34
  46.1 4.4 copy-start.40
  51.1 4.8 copy-start.9
  60.1 81.9 %copy-start.21 = (bf16[192,768]{1,0:T(8,128)(2,1)S(1)}, bf16[192,768]{1,0:T(8,128)(2,1)}, u32[]{:S(2)}) copy-start(bf16[192,768]{1,0:T(8,128)(2,1)} %param.26) | copy-start | bytes 884740
  136.2 9.1 %copy-start.5 = (bf16[1728,3,64]{0,2,1:T(8,128)(2,1)}, bf16[1728,3,64]{0,2,1:T(8,128)(2,1)S(1)}, u32[]{:S(2)}) copy-start(bf16[1728,3,64]{0,2,1:T(8,128)(2,1)S(1)} %get-tuple-element.687) | copy-start | bytes 1990660
  142.0 3.3 copy-start.12
  145.4 239.4 %all-reduce.15.cloned.1.call-start = ((), (), s32[]{:S(2)}) async-start(), calls=%async_computation.4 | async-start | bytes 10616832 | tf_op jit(solution)/shard_map/psum | solution.py:194
  146.0 123.8 %copy-start.29 = (f32[1728]{0:T(1024)}, f32[1728]{0:T(1024)S(1)}, u32[]{:S(2)}) copy-start(f32[1728]{0:T(1024)S(1)} %convert_element_type.156) | copy-start | bytes 20740
  253.7 16.1 %copy-start.2 = (f32[1728,768]{1,0:T(8,128)}, f32[1728,768]{1,0:T(8,128)S(1)}, u32[]{:S(2)}) copy-start(f32[1728,768]{1,0:T(8,128)S(1)} %get-tuple-element.391) | copy-start | bytes 15925252
  253.7 16.0 %copy-start.26 = (f32[1728]{0:T(1024)}, f32[1728]{0:T(1024)S(1)}, u32[]{:S(2)}) copy-start(f32[1728]{0:T(1024)S(1)} %get-tuple-element.416) | copy-start | bytes 20740
  254.9 14.8 %copy-start.16 = (bf16[1728,768]{1,0:T(8,128)(2,1)}, bf16[1728,768]{1,0:T(8,128)(2,1)S(1)}, u32[]{:S(2)}) copy-start(bf16[1728,768]{1,0:T(8,128)(2,1)S(1)} %add_convert_fusion) | copy-start | bytes 7962628
  254.9 14.8 %copy-start.10 = (bf16[1728,768]{1,0:T(8,128)(2,1)S(1)}, bf16[1728,768]{1,0:T(8,128)(2,1)}, u32[]{:S(2)}) copy-start(bf16[1728,768]{1,0:T(8,128)(2,1)} %copy.59) | copy-start | bytes 7962628
  254.9 14.8 %copy-start.52 = (bf16[768,768]{1,0:T(8,128)(2,1)S(1)}, bf16[768,768]{1,0:T(8,128)(2,1)}, u32[]{:S(2)}) copy-start(bf16[768,768]{1,0:T(8,128)(2,1)} %param.34) | copy-start | bytes 3538948
  274.7 1.5 copy-start.56
  280.8 254.3 %reduce-scatter.4.cloned.1.call-start = ((), (), s32[]{:S(2)}) async-start(), calls=%async_computation.6 | async-start | bytes 3440640
  305.3 79.5 %copy-start.27 = (f32[1728]{0:T(1024)S(1)}, f32[1728]{0:T(1024)}, u32[]{:S(2)}) copy-start(f32[1728]{0:T(1024)} %copy-done.26) | copy-start | bytes 20740
  311.4 79.5 %copy-start.30 = (f32[1728]{0:T(1024)S(1)}, f32[1728]{0:T(1024)}, u32[]{:S(2)}) copy-start(f32[1728]{0:T(1024)} %copy-done.29) | copy-start | bytes 20740
  311.4 302.4 %all-reduce.17.cloned.1.call-start = ((), (), s32[]{:S(2)}) async-start(), calls=%async_computation.5 | async-start | bytes 10616832 | tf_op jit(solution)/shard_map/psum | solution.py:272
  384.8 6.1 copy-start.7
  384.8 6.4 copy-start.11
  396.6 2.4 copy-start.3
  407.7 3.2 copy-start.14
  407.7 3.2 copy-start.19
  414.5 6.8 copy-start.20
  421.2 6.9 copy-start.6
  435.3 3.2 copy-start.14
  435.3 3.2 copy-start.19
  442.1 6.8 copy-start.20
  448.8 6.8 copy-start.6
  462.9 3.2 copy-start.14
  462.9 3.2 copy-start.19
  469.7 6.8 copy-start.20
  476.4 6.8 copy-start.6
  488.1 8.2 copy-start.23
  488.1 8.2 copy-start.25
  488.1 8.2 copy-start.37
  488.1 8.2 copy-start.39
  501.8 3.3 copy-start.54
  509.8 11.3 %copy-start.31 = (f32[1728]{0:T(1024)S(1)}, f32[1728]{0:T(1024)}, u32[]{:S(2)}) copy-start(f32[1728]{0:T(1024)} %copy-done.29) | copy-start | bytes 20740
  509.8 346.0 %all-reduce.19.cloned.1.call-start = ((), (), s32[]{:S(2)}) async-start(), calls=%async_computation.7 | async-start | bytes 14155776 | tf_op jit(solution)/shard_map/psum | solution.py:281
  513.7 7.4 copy-start.57
  521.1 6.0 copy-start.4
  521.1 6.0 copy-start.35
  521.1 5.9 copy-start.41
  521.1 5.9 copy-start.43
  521.1 5.9 copy-start.45
  521.1 9.4 %slice-start = ((s8[5308416]{0:T(1024)(128)(4,1)}), s8[4194304]{0:T(1024)(128)(4,1)S(1)}, s32[]{:S(2)}) async-start(s8[5308416]{0:T(1024)(128)(4,1)} %bitcast.139), calls=%async_computation.8 | async-start | bytes 8388608
  527.0 3.5 slice-start.1
  527.1 3.5 copy-start.13
  530.5 1.6 copy-start.15
  855.8 4.9 copy-start.18
  855.8 6.3 copy-start.17
  855.8 7.7 copy-start.1
  (11 other events, 7.9 us)
Sparse Core Ops, SparseCore 0:
  9.6 29.1 all-gather.2
  40.4 26.4 all-gather.4
  145.5 103.6 all-reduce.12
  280.9 103.7 all-reduce.14
  387.2 35.6 reduce-scatter.3
  509.9 103.7 all-reduce.16
  619.3 236.4 all-reduce.18
where the time goes:
time: 878 us; the launch traced here: 871 us
  waiting for transfers between devices  440 us (50%)
  matrix products  168 us (19%)
  other arithmetic  105 us (12%)
  blocking collectives  75.6 us (9%)
  local copies, waits for them, and re-layouts  60.4 us (7%)
  between operations  20.6 us (2%)
    psum x1, waiting for transfers between devices, local(): lax.psum((own_weight * grad_w_qkv, own_weight * grad_b_qkv, own_weight *...  188 us
    psum x1, waiting for transfers between devices, local(): mid = stream + (lax.psum(head_terms, 'mp') + out_bias.astype(jnp.float32))  98.1 us
    psum x1, waiting for transfers between devices, local(): grad_normed_one = lax.psum(norm_one_terms, 'mp')  73.5 us
    psum x1, waiting for transfers between devices, local(): grad_normed_two = lax.psum(norm_two_terms, 'mp')  73.3 us
    psum x1, blocking collectives, local(): lax.psum((own_weight * grad_w_qkv, own_weight * grad_b_qkv, own_weight *...  39.9 us
    dot_general x6, matrix products, masked_scores(): jnp.einsum('qhd,khd->hqk', query_blk, key_all, preferred_element_type=jnp...  33.8 us
    unnamed x135, local copies, waits for them, and re-layouts  28.1 us
    dot_general x3, matrix products, attend_block(): jnp.einsum('hqk,khd->qhd', attn_probs, value_low, preferred_element_type=...  26.9 us
  transfers between devices with their start and end apart: 7, of which 5 were waited for; matrix products, arithmetic and copies ran while one was open for 33% of the time, Pallas kernels for 0%

commit v1 on v0

--- a/solution.py
+++ b/solution.py
@@ -1,11 +1,373 @@
+import functools
+
 import jax
 import jax.numpy as jnp
 from jax import lax
+from jax.experimental import pallas as pl
+from jax.experimental.pallas import tpu as pltpu
 from jax.sharding import PartitionSpec as P
 
 HEAD_DIM = 64
 GRID_LO = 14
 SLOTS = 576
+
+MESH = pl.DeviceIdType.MESH
+MIB = 1024 * 1024
+F32 = jnp.float32
+BF16 = jnp.bfloat16
+NT = (((1,), (1,)), ((), ()))
+TN = (((0,), (0,)), ((), ()))
+NN = (((1,), (0,)), ((), ()))
+
+ROWS = 1728
+TILE = 192
+TILES = ROWS // TILE
+NARROW = 608
+WIDE = 768
+GATHER_ROWS = 288
+GATHERS = ROWS // GATHER_ROWS
+
+
+class Refs:
+    pass
+
+
+def dot(left, right, dims=NN):
+    return lax.dot_general(left, right, dims, preferred_element_type=F32)
+
+
+def remote(src, dst, send, recv, device):
+    return pltpu.make_async_remote_copy(
+        src_ref=src, dst_ref=dst, send_sem=send, recv_sem=recv, device_id=device, device_id_type=MESH
+    )
+
+
+def place():
+    spot = Refs()
+    spot.dp = lax.axis_index("dp")
+    spot.mp = lax.axis_index("mp")
+    spot.y = spot.mp // 2
+    spot.c = spot.mp % 2
+    spot.sib_mp = 2 * spot.y + 1 - spot.c
+    spot.yp_mp = 2 * (1 - spot.y) + spot.c
+    spot.diag_mp = 2 * (1 - spot.y) + 1 - spot.c
+    spot.sib = (spot.dp, spot.sib_mp)
+    spot.yp = (spot.dp, spot.yp_mp)
+    return spot
+
+
+def greet(devices):
+    barrier = pltpu.get_barrier_semaphore()
+    for device in devices:
+        pl.semaphore_signal(barrier, inc=1, device_id=device, device_id_type=MESH)
+    pl.semaphore_wait(barrier, len(devices))
+
+
+def sin_cos(angle):
+    turns = jnp.floor(angle * 0.6366197723675814 + 0.5)
+    rest = angle - turns * 1.5703125
+    rest = rest - turns * 4.837512969970703e-4
+    rest = rest - turns * 7.549789948768648e-8
+    square = rest * rest
+    sine = rest + rest * square * (
+        -1.6666654611e-1 + square * (8.3321608736e-3 + square * -1.9515295891e-4)
+    )
+    cosine = (
+        1.0
+        - 0.5 * square
+        + square
+        * square
+        * (4.166664568298827e-2 + square * (-1.388731625493765e-3 + square * 2.443315711809948e-5))
+    )
+    quarter = turns - 4.0 * jnp.floor(turns * 0.25)
+    odd = (quarter == 1.0) | (quarter == 3.0)
+    sine_sign = jnp.where(quarter >= 2.0, -1.0, 1.0)
+    cosine_sign = jnp.where((quarter == 1.0) | (quarter == 2.0), -1.0, 1.0)
+    return (
+        jnp.where(odd, cosine, sine) * sine_sign,
+        jnp.where(odd, sine, cosine) * cosine_sign,
+    )
+
+
+def front_lanes(shape):
+    return lax.broadcasted_iota(jnp.int32, shape, 1) % HEAD_DIM < HEAD_DIM // 2
+
+
+def swap_halves(values):
+    width = values.shape[1]
+    half = HEAD_DIM // 2
+    return jnp.where(
+        front_lanes(values.shape),
+        pltpu.roll(values, width - half, 1),
+        pltpu.roll(values, half, 1),
+    )
+
+
+def start_gather(r, spot):
+    own = pltpu.make_async_copy(r.tok, r.tokp.at[spot.mp], r.own_sem)
+    own.start()
+    for i in range(GATHERS):
+        rows = pl.ds(i * GATHER_ROWS, GATHER_ROWS)
+        remote(
+            r.tok.at[rows], r.tokp.at[spot.mp, rows], r.ty_send.at[i], r.ty_recv.at[i], spot.yp
+        ).start()
+    remote(r.tok, r.tokp.at[spot.mp], r.tc_send, r.tc_recv, spot.sib).start()
+    remote(r.small, r.smallp.at[spot.mp], r.sm_send.at[0], r.sm_recv.at[0], spot.yp).start()
+    remote(r.small, r.smallp.at[spot.mp], r.sm_send.at[1], r.sm_recv.at[1], spot.sib).start()
+
+
+def angle_tables(r):
+    step = 144
+
+    def block(i, carry):
+        rows = pl.ds(pl.multiple_of(i * step, 16), step)
+        angle = r.info[rows, 0:1] * r.freq[0:1, :] + r.info[rows, 1:2] * r.freq[1:2, :]
+        sine, cosine = sin_cos(angle)
+        r.cos[rows, :] = cosine
+        r.sin[rows, :] = jnp.where(front_lanes(sine.shape), -sine, sine)
+        return carry
+
+    lax.fori_loop(0, ROWS // step, block, 0)
+
+
+def project(r, i):
+    rows = pl.ds(pl.multiple_of(i * GATHER_ROWS, 16), GATHER_ROWS)
+    values = jnp.concatenate([r.tokp[j, rows, :].astype(F32) for j in range(4)], axis=1)
+    r.tokf[rows, :] = values.astype(BF16)
+    mean = jnp.mean(values, axis=1, keepdims=True)
+    square = jnp.mean(values * values, axis=1, keepdims=True)
+    inverse = lax.rsqrt(square - mean * mean + norm_eps)
+    h1 = ((values - mean) * inverse * r.smallf[0:1, :] + r.smallf[1:2, :]).astype(BF16)
+    r.h1[rows, :] = h1
+    projected = dot(h1, r.wqkv[...]) + r.bqkv[0:1, :]
+    front = projected[:, :384]
+    turned = (front * r.cos[rows, :] + swap_halves(front) * r.sin[rows, :]).astype(BF16)
+    r.qk[rows, :] = turned
+    value = projected[:, 384:].astype(BF16)
+    for h in range(3):
+        r.q3[h, rows, :] = turned[:, 64 * h : 64 * h + 64]
+        r.k3[h, rows, :] = turned[:, 192 + 64 * h : 256 + 64 * h]
+        r.v3[h, rows, :] = value[:, 64 * h : 64 * h + 64]
+
+
+def gather_and_project(r, spot):
+    angle_tables(r)
+    pltpu.make_async_copy(r.tok, r.tokp.at[spot.mp], r.own_sem).wait()
+    from_sib = remote(r.tok, r.tokp.at[spot.mp], r.tc_send, r.tc_recv, spot.sib)
+    from_sib.wait()
+    small_y = remote(r.small, r.smallp.at[spot.mp], r.sm_send.at[0], r.sm_recv.at[0], spot.yp)
+    small_c = remote(r.small, r.smallp.at[spot.mp], r.sm_send.at[1], r.sm_recv.at[1], spot.sib)
+    small_y.wait()
+    small_c.wait()
+    on = r.smallp.at[spot.yp_mp]
+    small_f = remote(on, on, r.sm_send.at[2], r.sm_recv.at[2], spot.sib)
+    small_f.start()
+    small_f.wait()
+    r.smallp[spot.mp] = r.small[...]
+    r.smallf[...] = jnp.concatenate([r.smallp[j] for j in range(4)], axis=1)
+
+    def y_copy(i):
+        rows = pl.ds(pl.multiple_of(i * GATHER_ROWS, 16), GATHER_ROWS)
+        return remote(
+            r.tok.at[rows], r.tokp.at[spot.mp, rows], r.ty_send.at[i], r.ty_recv.at[i], spot.yp
+        )
+
+    def forward(i):
+        rows = pl.ds(pl.multiple_of(i * GATHER_ROWS, 16), GATHER_ROWS)
+        piece = r.tokp.at[spot.yp_mp, rows]
+        return remote(piece, piece, r.tf_send.at[i], r.tf_recv.at[i], spot.sib)
+
+    y_copy(0).wait()
+    forward(0).start()
+
+    def chunk(i, carry):
+        @pl.when(i + 1 < GATHERS)
+        def _():
+            y_copy(i + 1).wait()
+            forward(i + 1).start()
+
+        forward(i).wait()
+        project(r, i)
+        return carry
+
+    lax.fori_loop(0, GATHERS, chunk, 0)
+
+
+def tile_of(n):
+    return n
+
+
+def narrow_tile(n):
+    tile = n + (n + 5) // 8 + (n + 3) // 8
+    third = tile // 3
+    return (tile, third * 576 - 32 * (third // 2))
+
+
+def wide_tile(n):
+    return (3 + 3 * n, 384 + 576 * n)
+
+
+def attend_tile(r, tile, start, width):
+    rows = pl.ds(pl.multiple_of(tile * TILE, 16), TILE)
+    window = pl.ds(pl.multiple_of(start, 16), width)
+    allowed = r.info[rows, 4:5] == r.kseg[tile, 0:1, :width]
+    mask = jnp.where(allowed, 0.0, -1e30)
+    outs = []
+    logs = []
+    for h in range(3):
+        query = r.q3[h, rows, :] * BF16(0.125)
+        scores = dot(query, r.k3[h, window, :], NT) + mask
+        top = jnp.max(scores, axis=1, keepdims=True)
+        exponent = jnp.exp(scores - top)
+        total = jnp.sum(exponent, axis=1, keepdims=True)
+        probs = (exponent * (1.0 / total)).astype(BF16)
+        outs.append(dot(probs, r.v3[h, window, :]))
+        logs.append(top + jnp.log(total))
+    r.att[r.spot.mp, rows, :] = jnp.concatenate(outs, axis=1).astype(BF16)
+    lane = lax.broadcasted_iota(jnp.int32, (TILE, 128), 1)
+    r.lse[rows, :] = jnp.where(lane == 0, logs[0], jnp.where(lane == 1, logs[1], logs[2]))
+
+
+def attend(r, spot):
+    def copies(tile):
+        rows = pl.ds(pl.multiple_of(tile * TILE, 16), TILE)
+        piece = r.att.at[spot.mp, rows]
+        other = r.att.at[spot.yp_mp, rows]
+        return (
+            remote(piece, piece, r.ac_send.at[tile], r.ac_recv.at[tile], spot.sib),
+            remote(piece, piece, r.ay_send.at[tile], r.ay_recv.at[tile], spot.yp),
+            remote(other, other, r.af_send.at[tile], r.af_recv.at[tile], spot.sib),
+        )
+
+    def send(tile):
+        to_sib, to_y, _ = copies(tile)
+        to_y.start()
+        to_sib.start()
+
+    def pass_on(tile):
+        _, to_y, onward = copies(tile)
+        to_y.wait()
+        onward.start()
+
+    def narrow(n, carry):
+        @pl.when(n >= 2)
+        def _():
+            pass_on(narrow_tile(n - 2)[0])
+
+        tile, start = narrow_tile(n)
+        attend_tile(r, tile, start, NARROW)
+        send(tile)
+        return carry
+
+    lax.fori_loop(0, 7, narrow, 0)
+
+    def wide(n, carry):
+        pass_on(narrow_tile(n + 5)[0])
+        tile, start = wide_tile(n)
+        attend_tile(r, tile, start, WIDE)
+        send(tile)
+        return carry
+
+    lax.fori_loop(0, 2, wide, 0)
+    for n in range(2):
+        pass_on(wide_tile(n)[0])
+    for tile in range(TILES):
+        to_sib, _, onward = copies(tile)
+        to_sib.wait()
+        onward.wait()
+
+
+def call_kernel(kernel, ins, outs, scratch, collective_id, limit):
+    names = list(ins) + list(outs) + list(scratch)
+
+    def body(*refs):
+        r = Refs()
+        for name, ref in zip(names, refs, strict=True):
+            setattr(r, name, ref)
+        r.spot = place()
+        kernel(r, r.spot)
+
+    spaces = {"vmem": pltpu.VMEM, "any": pl.ANY, "smem": pltpu.SMEM}
+    results = pl.pallas_call(
+        body,
+        out_shape=[jax.ShapeDtypeStruct(shape, dtype) for shape, dtype, _ in outs.values()],
+        in_specs=[pl.BlockSpec(memory_space=spaces[space]) for _, space in ins.values()],
+        out_specs=[pl.BlockSpec(memory_space=spaces[space]) for _, _, space in outs.values()],
+        scratch_shapes=list(scratch.values()),
+        compiler_params=pltpu.CompilerParams(
+            collective_id=collective_id, has_side_effects=True, vmem_limit_bytes=limit * MIB
+        ),
+    )(*[array for array, _ in ins.values()])
+    return dict(zip(outs, results, strict=True))
+
+
+def dma(*shape):
+    return pltpu.SemaphoreType.DMA(shape) if shape else pltpu.SemaphoreType.DMA
+
+
+def kernel_a(r, spot):
+    greet([spot.sib, spot.yp])
+    start_gather(r, spot)
+    gather_and_project(r, spot)
+    attend(r, spot)
+
+
+def run_a(tokens, small, wqkv, bqkv, freq, info, kseg):
+    ins = {
+        "tok": (tokens, "vmem"),
+        "small": (small, "vmem"),
+        "wqkv": (wqkv, "vmem"),
+        "bqkv": (bqkv, "vmem"),
+        "freq": (freq, "vmem"),
+        "info": (info, "vmem"),
+        "kseg": (kseg, "vmem"),
+    }
+    outs = {
+        "tokf": ((ROWS, 768), BF16, "vmem"),
+        "h1": ((ROWS, 768), BF16, "vmem"),
+        "qk": ((ROWS, 384), BF16, "vmem"),
+        "q3": ((3, ROWS, 64), BF16, "vmem"),
+        "k3": ((3, ROWS, 64), BF16, "vmem"),
+        "v3": ((3, ROWS, 64), BF16, "vmem"),
+        "cos": ((ROWS, 384), F32, "vmem"),
+        "sin": ((ROWS, 384), F32, "vmem"),
+        "smallf": ((8, 768), F32, "vmem"),
+        "att": ((4, ROWS, 192), BF16, "vmem"),
+        "lse": ((ROWS, 128), F32, "vmem"),
+    }
+    scratch = {
+        "tokp": pltpu.VMEM((4, ROWS, 192), BF16),
+        "smallp": pltpu.VMEM((4, 8, 192), F32),
+        "own_sem": dma(),
+        "ty_send": dma(GATHERS),
+        "ty_recv": dma(GATHERS),
+        "tf_send": dma(GATHERS),
+        "tf_recv": dma(GATHERS),
+        "tc_send": dma(),
+        "tc_recv": dma(),
+        "sm_send": dma(3),
+        "sm_recv": dma(3),
+        "ac_send": dma(TILES),
+        "ac_recv": dma(TILES),
+        "ay_send": dma(TILES),
+        "ay_recv": dma(TILES),
+        "af_send": dma(TILES),
+        "af_recv": dma(TILES),
+    }
+    return call_kernel(kernel_a, ins, outs, scratch, 1, 56)
+
+
+def key_windows(key_segment):
+    starts = []
+    for tile in range(TILES):
+        if tile % 3 == 0 and tile:
+            starts.append(384 + 576 * (tile // 3 - 1))
+        else:
+            starts.append(576 * (tile // 3) - 32 * (tile // 6))
+    padded = jnp.pad(key_segment, (0, WIDE), constant_values=-3.0)
+    return jnp.broadcast_to(
+        jnp.stack([padded[s : s + WIDE] for s in starts])[:, None, :], (TILES, 8, WIDE)
+    )
 
 
 norm_eps = 1e-06
@@ -115,53 +477,46 @@
     segment_size = jnp.where(group_now == 0, GRID_LO * GRID_LO, SLOTS).astype(jnp.int32)
     segment_ids = row_index // segment_size
     key_keep = keep_mask > 0
-    whole_tokens, whole_cot, gain_one, bias_one, gain_two, bias_two, out_bias = (
-        lax.all_gather(tokens, "mp", axis=1, tiled=True),
-        lax.all_gather(cotangent, "mp", axis=1, tiled=True),
-        lax.all_gather(norm1_gain, "mp", axis=0, tiled=True),
-        lax.all_gather(norm1_bias, "mp", axis=0, tiled=True),
-        lax.all_gather(norm2_gain, "mp", axis=0, tiled=True),
-        lax.all_gather(norm2_bias, "mp", axis=0, tiled=True),
-        lax.all_gather(b_out, "mp", axis=0, tiled=True),
-    )
+    segment_float = segment_ids.astype(jnp.float32)
+    key_segment = jnp.where(key_keep, segment_float, -1.0)
+    info = jnp.stack(
+        [coords[0].astype(F32), coords[1].astype(F32), keep_float, key_segment, segment_float]
+        + [keep_float] * 3,
+        axis=1,
+    )
+    small = jnp.stack(
+        [
+            part.astype(F32)
+            for part in (norm1_gain, norm1_bias, norm2_gain, norm2_bias, b_out, b_down, b_out, b_out)
+        ]
+    )
+    wqkv_flat = w_qkv.reshape(w_qkv.shape[0], 3 * width_loc)
+    bqkv_flat = jnp.broadcast_to(b_qkv.reshape(1, 3 * width_loc).astype(F32), (8, 3 * width_loc))
+    half_freqs = jnp.concatenate([freqs, freqs], axis=2).reshape(2, width_loc)
+    freq = jnp.pad(jnp.concatenate([half_freqs, half_freqs], axis=1), ((0, 6), (0, 0)))
+    a = run_a(tokens, small, wqkv_flat, bqkv_flat, freq, info, key_windows(key_segment))
+    whole_tokens = a["tokf"]
+    gain_one, bias_one, gain_two, bias_two, out_bias = (a["smallf"][n] for n in range(5))
+    whole_cot = lax.all_gather(cotangent, "mp", axis=1, tiled=True)
     stream = whole_tokens.astype(jnp.float32)
-    normed_one_out, normed_one, inverse_one = norm_forward(
-        stream, gain_one.astype(jnp.float32), bias_one.astype(jnp.float32)
-    )
-    normed_one_low = normed_one_out.astype(jnp.bfloat16)
-    projected = jnp.einsum(
-        "rd,dce->rce", normed_one_low, w_qkv, preferred_element_type=jnp.float32
-    ) + b_qkv.astype(jnp.float32)
+    normed_one_low = a["h1"]
+    _, normed_one, inverse_one = norm_forward(stream, gain_one, bias_one)
     coord_rows = coords[0].astype(jnp.float32)
     coord_cols = coords[1].astype(jnp.float32)
     angles = coord_rows[:, None, None] * freqs[0][None] + coord_cols[:, None, None] * freqs[1][None]
     cosine_table = jnp.cos(angles)
     sine_table = jnp.sin(angles)
     head_shape = (row_count, heads_loc, HEAD_DIM)
-    query_rot = rotate_pairs(projected[:, 0].reshape(head_shape), cosine_table, sine_table)
-    key_rot = rotate_pairs(projected[:, 1].reshape(head_shape), cosine_table, sine_table)
-    query_low = query_rot.astype(jnp.bfloat16)
-    key_low = key_rot.astype(jnp.bfloat16)
-    value_low = projected[:, 2].astype(jnp.bfloat16).reshape(head_shape)
+    query_low = a["qk"][:, :width_loc].reshape(head_shape)
+    key_low = a["qk"][:, width_loc:].reshape(head_shape)
+    query_rot, key_rot = query_low.astype(F32), key_low.astype(F32)
+    value_low = a["v3"].transpose(1, 0, 2)
     block_shape = (block_count, SLOTS, heads_loc, HEAD_DIM)
     segment_blocks = segment_ids.reshape(block_count, SLOTS)
-
-    def attend_block(inputs):
-        query_blk, segment_blk = inputs
-        scores = masked_scores(query_blk, key_low, segment_blk, segment_ids, key_keep)
-        row_max = jnp.max(scores, axis=-1, keepdims=True)
-        exponent = jnp.exp(scores - row_max)
-        summed = jnp.sum(exponent, axis=-1, keepdims=True)
-        attn_probs = (exponent / summed).astype(jnp.bfloat16)
-        output = jnp.einsum(
-            "hqk,khd->qhd", attn_probs, value_low, preferred_element_type=jnp.float32
-        )
-        return (output.astype(jnp.bfloat16), (row_max + jnp.log(summed))[..., 0])
-
-    attended_blocks, log_total = lax.map(
-        attend_block, (query_low.reshape(block_shape), segment_blocks)
-    )
-    attended = attended_blocks.reshape(row_count, width_loc)
+    attended = lax.dynamic_index_in_dim(a["att"], lax.axis_index("mp"), 0, False)
+    log_total = (
+        a["lse"][:, :heads_loc].reshape(block_count, SLOTS, heads_loc).transpose(0, 2, 1)
+    )
     head_terms = jnp.dot(attended, w_out, preferred_element_type=jnp.float32)
     mid = stream + (lax.psum(head_terms, "mp") + out_bias.astype(jnp.float32))
     normed_two_out, normed_two, inverse_two = norm_forward(

time: 878 us -> 846 us (0.964)
  Pallas kernels: 0 us -> 72.3 us
  matrix products: 168 us -> 115 us
  other arithmetic: 105 us -> 84.2 us
  waiting for transfers between devices: 440 us -> 421 us
  blocking collectives: 75.6 us -> 60.8 us
    pallas_call x0 -> x1, Pallas kernels: none -> 72.3 us  [call_kernel(): pl.pallas_call(body, out_shape=[jax.ShapeDtypeStruct(shape, dtype) for sh...]
    dot_general x3 -> x0, matrix products: 26.9 us -> none  [attend_block(): jnp.einsum('hqk,khd->qhd', attn_probs, value_low, preferred_element_type=...]
    dot_general x6 -> x3, matrix products: 33.8 us -> 8.7 us  [masked_scores(): jnp.einsum('qhd,khd->hqk', query_blk, key_all, preferred_element_type=jnp...]
    reduce_sum x6 -> x1, other arithmetic: 27.9 us -> 5.66 us  [norm_forward(): row_square = jnp.mean(values * values, axis=-1, keepdims=True)]
    psum x1, waiting for transfers between devices: 73.5 us -> 52.2 us  [local(): grad_normed_one = lax.psum(norm_one_terms, 'mp')]
    unnamed x1 -> x0, blocking collectives: 13.9 us -> none
    unnamed x135 -> x95, local copies, waits for them, and re-layouts: 28.1 us -> 32.6 us
  transfers between devices with their start and end apart: 7 -> 6, of which waited for: 5 -> 5; matrix products, arithmetic and copies ran while one was open for 33% -> 25% of each run, Pallas kernels for 0% -> 0%
where the time goes in v1:
time: 846 us; the launch traced here: 839 us
  waiting for transfers between devices  421 us (50%)
  matrix products  115 us (14%)
  other arithmetic  84.2 us (10%)
  Pallas kernels  72.3 us (9%)
  local copies, waits for them, and re-layouts  64 us (8%)
  blocking collectives  60.8 us (7%)
  between operations  19.5 us (2%)
    psum x1, waiting for transfers between devices, local(): lax.psum((own_weight * grad_w_qkv, own_weight * grad_b_qkv, own_weight *...  188 us
    psum x1, waiting for transfers between devices, local(): mid = stream + (lax.psum(head_terms, 'mp') + out_bias.astype(jnp.float32))  103 us
    psum x1, waiting for transfers between devices, local(): grad_normed_two = lax.psum(norm_two_terms, 'mp')  75.8 us
    pallas_call x1, Pallas kernels, call_kernel(): pl.pallas_call(body, out_shape=[jax.ShapeDtypeStruct(shape, dtype) for sh...  72.3 us
    psum x1, waiting for transfers between devices, local(): grad_normed_one = lax.psum(norm_one_terms, 'mp')  52.2 us
    psum x1, blocking collectives, local(): lax.psum((own_weight * grad_w_qkv, own_weight * grad_b_qkv, own_weight *...  39.8 us
    unnamed x95, local copies, waits for them, and re-layouts  32.6 us
    psum x1, blocking collectives, local(): lax.psum(jnp.stack([kept_total * low_flag, kept_total * (1.0 - low_flag)]...  21 us
  transfers between devices with their start and end apart: 6, of which 5 were waited for; matrix products, arithmetic and copies ran while one was open for 25% of the time, Pallas kernels for 0%

profile of v1, /device:TPU:0, one launch (start us, length us, event | category | flops | bytes accessed | tf_op | source)
XLA Modules:
  0.0 838.7 jit_solution(6893585333815612935)
XLA Ops:
  9.3 2.0 fusion.70
  19.9 2.3 copy.93.refs_0_
  22.2 2.2 copy.94.refs_2_
  26.4 72.3 %shard_map.289 = (bf16[1728,768]{1,0:T(8,128)(2,1)}, bf16[1728,768]{1,0:T(8,128)(2,1)}, bf16[1728,384]{1,0:T(8,128)(2,1)}, bf16[3,1728,64]{2,1,0:T(8,128)(2,1)},...) custom-call(bf16[1728,192]{1,0:T(8,128)(2,1)} %copy.93.refs_0_, ...), custom_call_target="tpu_custom_call" | custom-call | tf_op jit(solution)/shard_map/pallas_call | solution.py:291
  98.8 4.4 fusion.59
  105.1 102.7 %all-reduce.9.cloned.1.call-done = f32[1728,768]{1,0:T(8,128)} async-done(((f32[1728,768]{1,0:T(8,128)}), f32[1728,768]{1,0:T(8,128)}) %all-reduce.9.cloned.1.call-update) | async-done | bytes 5308432 | tf_op jit(solution)/shard_map/psum | solution.py:521
  207.8 5.7 fusion.42
  213.4 2.3 copy-done.2
  218.4 15.7 %fusion.36 = (bf16[1728,768]{1,0:T(8,128)(2,1)}, f32[1728,768]{1,0:T(8,128)}) fusion(f32[768]{0:T(1024)S(1)} %convert_element_type.192, bf16[1728,768]{1,0:T(8,128)(2,1)S(1)} %add_convert_fusion, bf16[768,768]{1,0:T(8,128)(2,1)S(1)} %copy-done), kind=kOutput, calls=%fused_computation.47 | convolution fusion | flops 2126020608 | bytes 11799552 | tf_op jit(solution)/shard_map/dot_general | solution.py:527
  234.1 1.8 all-gather.2.cloned.1.call-done
  235.9 4.6 copy.97
  240.5 6.9 convert_reduce_fusion.1
  248.8 4.6 fusion.82
  255.6 1.7 copy.103
  257.3 3.7 slice_convert_fusion
  261.0 3.1 copy.105
  266.8 4.3 reshape.272
  271.1 3.5 copy.101
  275.4 6.0 fusion.52
  281.4 75.8 %all-reduce.11.cloned.1.call-done = f32[1728,768]{1,0:T(8,128)} async-done(((f32[1728,768]{1,0:T(8,128)}), f32[1728,768]{1,0:T(8,128)}) %all-reduce.11.cloned.1.call-update) | async-done | bytes 5308432 | tf_op jit(solution)/shard_map/psum | solution.py:549
  357.2 6.1 multiply_reduce_fusion.1
  363.7 5.4 convert_reduce_fusion.2
  369.0 2.3 copy-done.3
  371.4 1.9 convolution_convert_fusion.1
  373.2 3.3 reshape.260
  376.5 2.4 copy.102
  378.9 78.0 %while.15 = (s32[]{:T(128)}, f32[1728,3,64]{0,2,1:T(8,128)S(1)}, f32[1728,3,64]{0,2,1:T(8,128)}, bf16[3,576,3,64]{1,3,2,0:T(8,128)(2,1)}, bf16[3,576,3,64]{1,3,2...) while((s32[]{:T(128)}, f32[1728,3,64]{0,2,1:T(8,128)S(1)}, ...), condition=%wide.region_11.12_spmd.clone, body=%wide.region_9.11_spmd.clone.sunk | while | flops 1959702272 | bytes 116469728 | solution.py:592
  380.3 2.9 fusion.127
  383.2 3.6 fusion.129
  386.8 6.8 multiply_reduce_fusion.11
  393.6 6.8 multiply_convert_fusion.3
  400.4 2.6 fusion.130
  403.0 2.2 fusion.128
  406.2 2.9 fusion.127
  409.1 3.6 fusion.129
  412.7 6.8 multiply_reduce_fusion.11
  419.5 6.8 multiply_convert_fusion.3
  426.2 2.6 fusion.130
  428.8 2.2 fusion.128
  432.0 2.9 fusion.127
  435.0 3.6 fusion.129
  438.5 6.8 multiply_reduce_fusion.11
  445.3 6.8 multiply_convert_fusion.3
  452.1 2.6 fusion.130
  454.7 2.2 fusion.128
  458.4 3.0 copy.104
  461.4 3.6 reshape.267
  465.2 5.1 add_convert_fusion.2
  470.4 2.9 multiply_reduce_fusion.9
  473.7 4.6 convolution_bitcast_fusion
  479.8 21.0 %psum.122 = f32[2]{0:T(128)S(1)} all-reduce(f32[2]{0:T(128)S(1)} %pad_maximum_fusion.4), channel_id=1, replica_groups=mesh['dp'=8,'mp'=4] {'dp'}, use_global_device_ids=true, to_apply=%region_16.17 | all-reduce | flops 2 | bytes 16 | tf_op jit(solution)/shard_map/psum | solution.py:474
  504.0 6.6 convolution_multiply_fusion.3
  510.6 5.9 convolution_multiply_fusion.2
  516.5 1.8 fusion.83
  519.6 2.8 convolution_multiply_fusion.4
  525.4 2.6 multiply_reduce_fusion.7
  529.9 52.2 %all-reduce.13.cloned.1.call-done = f32[1728,768]{1,0:T(8,128)} async-done(((f32[1728,768]{1,0:T(8,128)}), f32[1728,768]{1,0:T(8,128)}) %all-reduce.13.cloned.1.call-update) | async-done | bytes 5308432 | tf_op jit(solution)/shard_map/psum | solution.py:627
  582.1 7.5 fusion.77
  589.6 39.8 %all-reduce.2 = (f32[3,192]{1,0:T(4,128)}, f32[2,3,32]{2,1,0:T(4,128)S(1)}, f32[192]{0:T(256)}, f32[192]{0:T(256)}, f32[192]{0:T(256)}, /*index=5*/f32[192]{0:T(256)}, f32[192]{0:T(256)}, f32[768]{0:T(1024)}, f32[192]{0:T(256)}) all-reduce(f32[3,192]{1,0:T(4,128)S(1)} %broadcast_multiply_fusion.9, ...), channel_id=1, replica_groups=mesh['dp'=8,'mp'=4] {'dp'}, use_global_device_ids=true, to_apply=%region_19.20 | all-reduce | flops 2688 | bytes 21504 | tf_op jit(solution)/shard_map/psum | solution.py:636
  630.0 4.5 fusion.55
  634.6 1.6 copy.108
  636.2 187.8 %all-reduce.15.cloned.1.call-done = (f32[768,3,192]{0,2,1:T(8,128)}, f32[192,768]{1,0:T(8,128)}, f32[768,768]{1,0:T(8,128)}, f32[768,768]{1,0:T(8,128)}) async-done(((f32[768,3,192]{0,2,1:T(8,128)}, f32[192,768]{1,0:T(8,128)}, f32[768,768]{1,0:T(8,128)}, f32[768,768]{1,0:T(8,128)}), (f32[768,3,192]{0,2,1:T(8,128)}, f32[192,768]{1,0:T(8,128)}, f32[768,768]{1,0:T(8,128)}, ...) | async-done | bytes 7077904 | tf_op jit(solution)/shard_map/psum | solution.py:636
  824.0 2.9 copy.141
  826.9 1.9 copy.142
  (189 shorter events, 39.0 us)
Async XLA Ops:
  7.2 211.2 %copy-start = (bf16[768,768]{1,0:T(8,128)(2,1)S(1)}, bf16[768,768]{1,0:T(8,128)(2,1)}, u32[]{:S(2)}) copy-start(bf16[768,768]{1,0:T(8,128)(2,1)} %param.30) | copy-start | bytes 3538948
  7.2 91.5 %copy-start.13 = (bf16[192,768]{1,0:T(8,128)(2,1)S(1)}, bf16[192,768]{1,0:T(8,128)(2,1)}, u32[]{:S(2)}) copy-start(bf16[192,768]{1,0:T(8,128)(2,1)} %param.24) | copy-start | bytes 884740
  7.2 200.5 %all-reduce.9.cloned.1.call-start = ((), (), s32[]{:S(2)}) async-start(), calls=%async_computation.1 | async-start | bytes 10616832 | tf_op jit(solution)/shard_map/psum | solution.py:521
  9.3 354.0 %copy-start.16 = (f32[1728]{0:T(1024)}, f32[1728]{0:T(1024)S(1)}, u32[]{:S(2)}) copy-start(f32[1728]{0:T(1024)S(1)} %convert_element_type.180) | copy-start | bytes 20740
  12.1 91.0 %copy-start.34 = (f32[192]{0:T(256)}, f32[192]{0:T(256)S(1)}, u32[]{:S(2)}) copy-start(f32[192]{0:T(256)S(1)} %convert_element_type.181) | copy-start | bytes 2308
  103.1 1.3 copy-start.36
  103.1 1.3 copy-start.32
  103.1 132.8 %all-gather.2.cloned.1.call-start = ((), (), s32[]{:S(2)}) async-start(), calls=%async_computation.2 | async-start | bytes 3440640 | tf_op jit(solution)/shard_map/all_gather | solution.py:500
  103.9 253.3 %all-reduce.11.cloned.1.call-start = ((), (), s32[]{:S(2)}) async-start(), calls=%async_computation.3 | async-start | bytes 10616832 | tf_op jit(solution)/shard_map/psum | solution.py:549
  105.1 108.4 %copy-start.23 = (f32[768]{0:T(1024)}, f32[768]{0:T(1024)S(1)}, u32[]{:S(2)}) copy-start(f32[768]{0:T(1024)S(1)} %get-tuple-element.270) | copy-start | bytes 9220
  213.4 2.3 copy-start.2
  213.4 3.4 copy-start.18
  216.9 1.5 copy-start.8
  234.1 6.4 copy-start.38
  247.3 1.5 copy-start.39
  253.4 0.7 copy-start.31
  253.4 1.8 copy-start.15
  253.5 270.5 %reduce-scatter.4.cloned.1.call-start = ((), (), s32[]{:S(2)}) async-start(), calls=%async_computation.5 | async-start | bytes 3440640
  261.0 13.8 %copy-start.25 = (s32[2,1728]{1,0:T(2,128)S(1)}, s32[2,1728]{1,0:T(2,128)}, u32[]{:S(2)}) copy-start(s32[2,1728]{1,0:T(2,128)} %param.36) | copy-start | bytes 41476
  275.4 81.8 %copy-start.19 = (f32[1728]{0:T(1024)S(1)}, f32[1728]{0:T(1024)}, u32[]{:S(2)}) copy-start(f32[1728]{0:T(1024)} %copy-done.18) | copy-start | bytes 20740
  275.4 81.8 %copy-start.24 = (f32[768]{0:T(1024)S(1)}, f32[768]{0:T(1024)}, u32[]{:S(2)}) copy-start(f32[768]{0:T(1024)} %copy-done.23) | copy-start | bytes 9220
  281.4 300.7 %all-reduce.13.cloned.1.call-start = ((), (), s32[]{:S(2)}) async-start(), calls=%async_computation.4 | async-start | bytes 10616832 | tf_op jit(solution)/shard_map/psum | solution.py:627
  357.2 6.1 copy-start.4
  357.2 6.4 copy-start.5
  369.0 2.3 copy-start.3
  369.0 9.9 %copy-start.20 = (pred[1728]{0:T(1024)(128)(4,1)S(1)}, pred[1728]{0:T(1024)(128)(4,1)}, u32[]{:S(2)}) copy-start(pred[1728]{0:T(1024)(128)(4,1)} %get-tuple-element.459) | copy-start | bytes 5188
  380.2 2.9 copy-start.6
  380.3 2.9 copy-start.11
  386.8 6.8 copy-start.12
  406.1 2.9 copy-start.6
  406.1 2.9 copy-start.11
  412.6 6.8 copy-start.12
  432.0 2.9 copy-start.6
  432.0 2.9 copy-start.11
  438.5 6.8 copy-start.12
  456.9 8.2 copy-start.21
  456.9 8.2 copy-start.22
  456.9 8.2 copy-start.28
  457.0 8.2 copy-start.29
  470.3 3.4 copy-start.14
  478.3 32.2 %copy-start.17 = (f32[1728]{0:T(1024)S(1)}, f32[1728]{0:T(1024)}, u32[]{:S(2)}) copy-start(f32[1728]{0:T(1024)} %copy-done.16) | copy-start | bytes 20740
  478.4 345.6 %all-reduce.15.cloned.1.call-start = ((), (), s32[]{:S(2)}) async-start(), calls=%async_computation.6 | async-start | bytes 14155776 | tf_op jit(solution)/shard_map/psum | solution.py:636
  504.0 6.6 copy-start.40
  510.6 5.9 copy-start.37
  516.4 3.1 slice-start
  516.4 3.1 slice-start.1
  519.6 2.9 copy-start.7
  522.4 0.7 copy-start.26
  522.4 0.7 copy-start.27
  522.4 0.7 copy-start.33
  522.4 2.9 copy-start.35
  522.5 59.6 %copy-start.30 = (f32[768]{0:T(1024)S(1)}, f32[768]{0:T(1024)}, u32[]{:S(2)}) copy-start(f32[768]{0:T(1024)} %get-tuple-element.268) | copy-start | bytes 9220
  823.9 4.9 copy-start.10
  823.9 6.3 copy-start.9
  823.9 7.7 copy-start.1
Sparse Core Ops, SparseCore 0:
  103.3 104.4 all-reduce.8
  209.4 26.4 all-gather.1
  253.6 103.5 all-reduce.10
  359.6 35.6 reduce-scatter.3
  478.5 103.5 all-reduce.12
  587.5 236.4 all-reduce.14

commit v2 on v1

v2 whole, which is shorter than its diff:
```python
import functools

import jax
import jax.numpy as jnp
from jax import lax
from jax.experimental import pallas as pl
from jax.experimental.pallas import tpu as pltpu
from jax.sharding import PartitionSpec as P

HEAD_DIM = 64
GRID_LO = 14
SLOTS = 576

MESH = pl.DeviceIdType.MESH
MIB = 1024 * 1024
VM = pltpu.VMEM
F32 = jnp.float32
BF16 = jnp.bfloat16
NT = (((1,), (1,)), ((), ()))
TN = (((0,), (0,)), ((), ()))
NN = (((1,), (0,)), ((), ()))

ROWS = 1728
TILE = 192
TILES = ROWS // TILE
NARROW = 608
WIDE = 768
GATHER_ROWS = 288
GATHERS = ROWS // GATHER_ROWS


class Refs:
    pass


def dot(left, right, dims=NN):
    return lax.dot_general(left, right, dims, preferred_element_type=F32)


def remote(src, dst, send, recv, device):
    return pltpu.make_async_remote_copy(
        src_ref=src, dst_ref=dst, send_sem=send, recv_sem=recv, device_id=device, device_id_type=MESH
    )


def place():
    spot = Refs()
    spot.dp = lax.axis_index("dp")
    spot.mp = lax.axis_index("mp")
    spot.y = spot.mp // 2
    spot.c = spot.mp % 2
    spot.sib_mp = 2 * spot.y + 1 - spot.c
    spot.yp_mp = 2 * (1 - spot.y) + spot.c
    spot.diag_mp = 2 * (1 - spot.y) + 1 - spot.c
    spot.sib = (spot.dp, spot.sib_mp)
    spot.yp = (spot.dp, spot.yp_mp)
    return spot


def greet(devices):
    barrier = pltpu.get_barrier_semaphore()
    for device in devices:
        pl.semaphore_signal(barrier, inc=1, device_id=device, device_id_type=MESH)
    pl.semaphore_wait(barrier, len(devices))


def sin_cos(angle):
    turns = jnp.floor(angle * 0.6366197723675814 + 0.5)
    rest = angle - turns * 1.5703125
    rest = rest - turns * 4.837512969970703e-4
    rest = rest - turns * 7.549789948768648e-8
    square = rest * rest
    sine = rest + rest * square * (
        -1.6666654611e-1 + square * (8.3321608736e-3 + square * -1.9515295891e-4)
    )
    cosine = (
        1.0
        - 0.5 * square
        + square
        * square
        * (4.166664568298827e-2 + square * (-1.388731625493765e-3 + square * 2.443315711809948e-5))
    )
    quarter = turns - 4.0 * jnp.floor(turns * 0.25)
    odd = (quarter == 1.0) | (quarter == 3.0)
    sine_sign = jnp.where(quarter >= 2.0, -1.0, 1.0)
    cosine_sign = jnp.where((quarter == 1.0) | (quarter == 2.0), -1.0, 1.0)
    return (
        jnp.where(odd, cosine, sine) * sine_sign,
        jnp.where(odd, sine, cosine) * cosine_sign,
    )


def front_lanes(shape):
    return lax.broadcasted_iota(jnp.int32, shape, 1) % HEAD_DIM < HEAD_DIM // 2


def swap_halves(values):
    width = values.shape[1]
    half = HEAD_DIM // 2
    return jnp.where(
        front_lanes(values.shape),
        pltpu.roll(values, width - half, 1),
        pltpu.roll(values, half, 1),
    )


def start_gather(r, spot):
    own = pltpu.make_async_copy(r.tok, r.tokp.at[spot.mp], r.own_sem)
    own.start()
    for i in range(GATHERS):
        rows = pl.ds(i * GATHER_ROWS, GATHER_ROWS)
        remote(
            r.tok.at[rows], r.tokp.at[spot.mp, rows], r.ty_send.at[i], r.ty_recv.at[i], spot.yp
        ).start()
    remote(r.tok, r.tokp.at[spot.mp], r.tc_send, r.tc_recv, spot.sib).start()
    remote(r.small, r.smallp.at[spot.mp], r.sm_send.at[0], r.sm_recv.at[0], spot.yp).start()
    remote(r.small, r.smallp.at[spot.mp], r.sm_send.at[1], r.sm_recv.at[1], spot.sib).start()


def angle_tables(r):
    step = 144

    def block(i, carry):
        rows = pl.ds(pl.multiple_of(i * step, 16), step)
        angle = r.info[rows, 0:1] * r.freq[0:1, :] + r.info[rows, 1:2] * r.freq[1:2, :]
        sine, cosine = sin_cos(angle)
        r.cos[rows, :] = cosine
        r.sin[rows, :] = jnp.where(front_lanes(sine.shape), -sine, sine)
        return carry

    lax.fori_loop(0, ROWS // step, block, 0)


def project(r, i):
    rows = pl.ds(pl.multiple_of(i * GATHER_ROWS, 16), GATHER_ROWS)
    values = jnp.concatenate([r.tokp[j, rows, :].astype(F32) for j in range(4)], axis=1)
    r.tokf[rows, :] = values.astype(BF16)
    mean = jnp.mean(values, axis=1, keepdims=True)
    square = jnp.mean(values * values, axis=1, keepdims=True)
    inverse = lax.rsqrt(square - mean * mean + norm_eps)
    h1 = ((values - mean) * inverse * r.smallf[0:1, :] + r.smallf[1:2, :]).astype(BF16)
    r.h1[rows, :] = h1
    projected = dot(h1, r.wqkv[...]) + r.bqkv[0:1, :]
    front = projected[:, :384]
    turned = (front * r.cos[rows, :] + swap_halves(front) * r.sin[rows, :]).astype(BF16)
    r.qk[rows, :] = turned
    value = projected[:, 384:].astype(BF16)
    for h in range(3):
        r.q3[h, rows, :] = turned[:, 64 * h : 64 * h + 64]
        r.k3[h, rows, :] = turned[:, 192 + 64 * h : 256 + 64 * h]
        r.v3[h, rows, :] = value[:, 64 * h : 64 * h + 64]


def gather_and_project(r, spot):
    angle_tables(r)
    pltpu.make_async_copy(r.tok, r.tokp.at[spot.mp], r.own_sem).wait()
    from_sib = remote(r.tok, r.tokp.at[spot.mp], r.tc_send, r.tc_recv, spot.sib)
    from_sib.wait()
    small_y = remote(r.small, r.smallp.at[spot.mp], r.sm_send.at[0], r.sm_recv.at[0], spot.yp)
    small_c = remote(r.small, r.smallp.at[spot.mp], r.sm_send.at[1], r.sm_recv.at[1], spot.sib)
    small_y.wait()
    small_c.wait()
    on = r.smallp.at[spot.yp_mp]
    small_f = remote(on, on, r.sm_send.at[2], r.sm_recv.at[2], spot.sib)
    small_f.start()
    small_f.wait()
    r.smallp[spot.mp] = r.small[...]
    r.smallf[...] = jnp.concatenate([r.smallp[j] for j in range(4)], axis=1)

    def y_copy(i):
        rows = pl.ds(pl.multiple_of(i * GATHER_ROWS, 16), GATHER_ROWS)
        return remote(
            r.tok.at[rows], r.tokp.at[spot.mp, rows], r.ty_send.at[i], r.ty_recv.at[i], spot.yp
        )

    def forward(i):
        rows = pl.ds(pl.multiple_of(i * GATHER_ROWS, 16), GATHER_ROWS)
        piece = r.tokp.at[spot.yp_mp, rows]
        return remote(piece, piece, r.tf_send.at[i], r.tf_recv.at[i], spot.sib)

    y_copy(0).wait()
    forward(0).start()

    def chunk(i, carry):
        @pl.when(i + 1 < GATHERS)
        def _():
            y_copy(i + 1).wait()
            forward(i + 1).start()

        forward(i).wait()
        project(r, i)
        return carry

    lax.fori_loop(0, GATHERS, chunk, 0)


def narrow_tile(n):
    tile = n + (n + 5) // 8 + (n + 3) // 8
    third = tile // 3
    return (tile, third * 576 - 32 * (third // 2))


def wide_tile(n):
    return (3 + 3 * n, 384 + 576 * n)


def attend_tile(r, tile, start, width):
    rows = pl.ds(pl.multiple_of(tile * TILE, 16), TILE)
    window = pl.ds(pl.multiple_of(start, 16), width)
    allowed = r.info[rows, 4:5] == r.kseg[tile, 0:1, :width]
    mask = jnp.where(allowed, 0.0, -1e30)
    outs = []
    logs = []
    for h in range(3):
        query = r.q3[h, rows, :] * BF16(0.125)
        scores = dot(query, r.k3[h, window, :], NT) + mask
        top = jnp.max(scores, axis=1, keepdims=True)
        exponent = jnp.exp(scores - top)
        total = jnp.sum(exponent, axis=1, keepdims=True)
        probs = (exponent * (1.0 / total)).astype(BF16)
        outs.append(dot(probs, r.v3[h, window, :]))
        logs.append(top + jnp.log(total))
    r.att[r.spot.mp, rows, :] = jnp.concatenate(outs, axis=1).astype(BF16)
    lane = lax.broadcasted_iota(jnp.int32, (TILE, 128), 1)
    r.lse[rows, :] = jnp.where(lane == 0, logs[0], jnp.where(lane == 1, logs[1], logs[2]))


def attend(r, spot):
    def copies(tile):
        rows = pl.ds(pl.multiple_of(tile * TILE, 16), TILE)
        piece = r.att.at[spot.mp, rows]
        other = r.att.at[spot.yp_mp, rows]
        return (
            remote(piece, piece, r.ac_send.at[tile], r.ac_recv.at[tile], spot.sib),
            remote(piece, piece, r.ay_send.at[tile], r.ay_recv.at[tile], spot.yp),
            remote(other, other, r.af_send.at[tile], r.af_recv.at[tile], spot.sib),
        )

    def send(tile):
        to_sib, to_y, _ = copies(tile)
        to_y.start()
        to_sib.start()

    def pass_on(tile):
        _, to_y, onward = copies(tile)
        to_y.wait()
        onward.start()

    def narrow(n, carry):
        @pl.when(n >= 2)
        def _():
            pass_on(narrow_tile(n - 2)[0])

        tile, start = narrow_tile(n)
        attend_tile(r, tile, start, NARROW)
        send(tile)
        return carry

    lax.fori_loop(0, 7, narrow, 0)

    def wide(n, carry):
        pass_on(narrow_tile(n + 5)[0])
        tile, start = wide_tile(n)
        attend_tile(r, tile, start, WIDE)
        send(tile)
        return carry

    lax.fori_loop(0, 2, wide, 0)
    for n in range(2):
        pass_on(wide_tile(n)[0])
    for tile in range(TILES):
        to_sib, _, onward = copies(tile)
        to_sib.wait()
        onward.wait()


def call_kernel(kernel, ins, outs, scratch, collective_id, limit, dp_bits):
    names = list(ins) + list(outs) + list(scratch)

    def body(*refs):
        r = Refs()
        for name, ref in zip(names, refs, strict=True):
            setattr(r, name, ref)
        r.spot = place()
        r.dp_bits = dp_bits
        kernel(r, r.spot)

    results = pl.pallas_call(
        body,
        out_shape=[jax.ShapeDtypeStruct(shape, dtype) for shape, dtype, _ in outs.values()],
        in_specs=[pl.BlockSpec(memory_space=space) for _, space in ins.values()],
        out_specs=[pl.BlockSpec(memory_space=space) for _, _, space in outs.values()],
        scratch_shapes=list(scratch.values()),
        compiler_params=pltpu.CompilerParams(
            collective_id=collective_id, has_side_effects=True, vmem_limit_bytes=limit * MIB
        ),
    )(*[array for array, _ in ins.values()])
    named = Refs()
    for name, result in zip(outs, results, strict=True):
        setattr(named, name, result)
    return named


def dma(*shape):
    return pltpu.SemaphoreType.DMA(shape) if shape else pltpu.SemaphoreType.DMA


def dp_partner(spot, bit):
    mine = (spot.dp // (1 << bit)) % 2
    return spot.dp + (1 - 2 * mine) * (1 << bit)


def sum_counts(r, spot):
    total = r.cnt[...]
    for bit in range(r.dp_bits):
        r.cnts[bit] = total
        copy = remote(
            r.cnts.at[bit],
            r.cntr.at[bit],
            r.cn_send.at[bit],
            r.cn_recv.at[bit],
            (dp_partner(spot, bit), spot.mp),
        )
        copy.start()
        copy.wait()
        total = total + r.cntr[bit]
    low = total[:, 0:1]
    high = total[:, 1:2]
    own = jnp.where(r.cnt[:, 2:3] > 0.5, low, high) / (low + high)
    r.share[...] = jnp.broadcast_to(own, (8, 128))


def kernel_a(r, spot):
    greet([spot.sib, spot.yp] + [(dp_partner(spot, bit), spot.mp) for bit in range(r.dp_bits)])
    start_gather(r, spot)
    sum_counts(r, spot)
    gather_and_project(r, spot)
    attend(r, spot)


def run_a(tokens, small, wqkv, bqkv, freq, info, kseg, cnt, dp_bits):
    ins = dict(
        tok=(tokens, VM),
        small=(small, VM),
        wqkv=(wqkv, VM),
        bqkv=(bqkv, VM),
        freq=(freq, VM),
        info=(info, VM),
        kseg=(kseg, VM),
        cnt=(cnt, VM),
    )
    outs = dict(
        tokf=((ROWS, 768), BF16, VM),
        h1=((ROWS, 768), BF16, VM),
        qk=((ROWS, 384), BF16, VM),
        q3=((3, ROWS, 64), BF16, VM),
        k3=((3, ROWS, 64), BF16, VM),
        v3=((3, ROWS, 64), BF16, VM),
        cos=((ROWS, 384), F32, VM),
        sin=((ROWS, 384), F32, VM),
        smallf=((8, 768), F32, VM),
        att=((4, ROWS, 192), BF16, VM),
        lse=((ROWS, 128), F32, VM),
        share=((8, 128), F32, VM),
    )
    scratch = dict(
        cnts=pltpu.VMEM((dp_bits, 8, 128), F32),
        cntr=pltpu.VMEM((dp_bits, 8, 128), F32),
        cn_send=dma(dp_bits),
        cn_recv=dma(dp_bits),
        tokp=pltpu.VMEM((4, ROWS, 192), BF16),
        smallp=pltpu.VMEM((4, 8, 192), F32),
        own_sem=dma(),
        ty_send=dma(GATHERS),
        ty_recv=dma(GATHERS),
        tf_send=dma(GATHERS),
        tf_recv=dma(GATHERS),
        tc_send=dma(),
        tc_recv=dma(),
        sm_send=dma(3),
        sm_recv=dma(3),
        ac_send=dma(TILES),
        ac_recv=dma(TILES),
        ay_send=dma(TILES),
        ay_recv=dma(TILES),
        af_send=dma(TILES),
        af_recv=dma(TILES),
    )
    return call_kernel(kernel_a, ins, outs, scratch, 1, 56, dp_bits)


PART = ROWS // 4
SUB = 144
SUBS = PART // SUB


def part_order(spot, n):
    y = spot.y + (1 - n // 2) * (1 - 2 * spot.y)
    c = spot.c + (1 - n % 2) * (1 - 2 * spot.c)
    return 2 * y + c


def phi_parts(value):
    scaled = jnp.clip(value * root_half, -3.832506856900711, 3.832506856900711)
    square = scaled * scaled
    top = 0.00022905065861350646
    for factor in (
        0.0034082910107109506,
        0.050955695062380861,
        0.18520832239976145,
        1.128379143519084,
    ):
        top = top * square + factor
    low = -1.1791602954361697e-7
    for factor in (
        0.000023547966471313185,
        0.0010179625278914885,
        0.014070470171167667,
        0.11098505178285362,
        0.49746925110067538,
        1.0,
    ):
        low = low * square + factor
    error = scaled * top / low
    return (0.5 + 0.5 * error, inv_root_two_pi * jnp.exp(-0.5 * value * value))


def own_columns(spot, values):
    return pltpu.roll(values, (768 - 192 * spot.mp) % 768, 1)[:, :192]


def core_columns(spot, values):
    cut = [values[:, 192 * j : 192 * j + 192] for j in range(4)]
    mine = [jnp.where(spot.c == 0, cut[2 * y], cut[2 * y + 1]) for y in range(2)]
    other = [jnp.where(spot.c == 0, cut[2 * y + 1], cut[2 * y]) for y in range(2)]
    return (mine, other)


def part_rows(k, length=PART, offset=0):
    return pl.ds(pl.multiple_of(k * PART + offset, 16), length)


def b_gathers(r, spot):
    own = r.wof.at[pl.ds(pl.multiple_of(192 * spot.mp, 16), 192)]
    other = r.wof.at[pl.ds(pl.multiple_of(192 * spot.yp_mp, 16), 192)]
    moves = Refs()
    moves.cot_own = pltpu.make_async_copy(r.cot, r.cotp.at[spot.mp], r.own_sem.at[0])
    moves.wo_own = pltpu.make_async_copy(r.wout, own, r.own_sem.at[1])
    moves.wo_y = remote(r.wout, own, r.wo_send.at[0], r.wo_recv.at[0], spot.yp)
    moves.wo_c = remote(r.wout, own, r.wo_send.at[1], r.wo_recv.at[1], spot.sib)
    moves.wo_f = remote(other, other, r.wo_send.at[2], r.wo_recv.at[2], spot.sib)
    moves.cot_c = remote(r.cot, r.cotp.at[spot.mp], r.ct_send.at[0], r.ct_recv.at[0], spot.sib)
    moves.cot_y = remote(r.cot, r.cotp.at[spot.mp], r.ct_send.at[1], r.ct_recv.at[1], spot.yp)
    piece = r.cotp.at[spot.yp_mp]
    moves.cot_f = remote(piece, piece, r.ct_send.at[2], r.ct_recv.at[2], spot.sib)
    return moves


def mlp_forward(r, spot, k):
    rows = part_rows(k)
    terms = r.smallf[4:5, :]
    for j in range(4):
        terms = terms + dot(r.att[j, rows, :], r.wof[192 * j : 192 * j + 192, :])
    r.work[...] = r.tokf[rows, :].astype(F32) + terms

    def norm(i, carry):
        local = pl.ds(pl.multiple_of(i * 48, 16), 48)
        rows_now = pl.ds(pl.multiple_of(k * PART + i * 48, 16), 48)
        mid = r.work[local, :]
        r.midc[rows_now, :] = own_columns(spot, mid)
        mean = jnp.mean(mid, axis=1, keepdims=True)
        square = jnp.mean(mid * mid, axis=1, keepdims=True)
        inverse = lax.rsqrt(square - mean * mean + norm_eps)
        normed = (mid - mean) * inverse
        r.n2[local, :] = normed
        r.inv2[local, :] = jnp.broadcast_to(inverse, (48, 128))
        r.h2[rows_now, :] = (normed * r.smallf[2:3, :] + r.smallf[3:4, :]).astype(BF16)
        return carry

    lax.fori_loop(0, PART // 48, norm, 0)
    r.work[...] = dot(r.h2[rows, :], r.wup[...]) + r.bup[0:1, :]

    def gelu(i, carry):
        local = pl.ds(pl.multiple_of(i * 48, 16), 48)
        rows_now = pl.ds(pl.multiple_of(k * PART + i * 48, 16), 48)
        value = r.work[local, :]
        lower, density = phi_parts(value)
        r.act[rows_now, :] = (value * lower).astype(BF16)
        r.work[local, :] = lower + value * density
        return carry

    lax.fori_loop(0, PART // 48, gelu, 0)


def mlp_output(r, spot, k):
    rows = part_rows(k)
    mine, other = core_columns(spot, dot(r.act[rows, :], r.wdown[...]))
    for y in range(2):
        r.mown[y, rows, :] = mine[y]
        r.msend[y, rows, :] = other[y].astype(BF16)


def mlp_backward(r, spot, k):
    rows = part_rows(k)

    def cotangents(i, carry):
        rows_now = pl.ds(pl.multiple_of(k * PART + i * SUB, 16), SUB)
        values = jnp.concatenate([r.cotp[j, rows_now, :].astype(F32) for j in range(4)], axis=1)
        r.gout[rows_now, :] = (values * r.info[rows_now, 2:3]).astype(BF16)
        return carry

    lax.fori_loop(0, SUBS, cotangents, 0)
    g_pre = (dot(r.gout[rows, :], r.wdown[...], NT) * r.work[...]).astype(BF16)
    r.gpre[rows, :] = g_pre
    r.sums[0:1, :] += jnp.sum(g_pre.astype(F32), axis=0, keepdims=True)
    r.work[...] = dot(r.gpre[rows, :], r.wup[...], NT)


def kernel_b(r, spot):
    greet([spot.sib, spot.yp])
    moves = b_gathers(r, spot)
    for move in (moves.wo_own, moves.cot_own, moves.wo_y, moves.wo_c, moves.cot_y, moves.cot_c):
        move.start()
    r.sums[...] = jnp.zeros_like(r.sums)
    moves.wo_own.wait()
    moves.wo_y.wait()
    moves.wo_f.start()
    moves.wo_c.wait()
    moves.wo_f.wait()

    def reduce_copies():
        return (
            remote(r.ps.at[0], r.rb.at[0], r.rs_send.at[0], r.rs_recv.at[0], spot.sib),
            remote(r.ps.at[1], r.rb.at[1], r.rs_send.at[1], r.rs_recv.at[1], spot.yp),
            remote(r.ps.at[2], r.rb.at[2], r.rs_send.at[2], r.rs_recv.at[2], spot.sib),
        )

    def out_copy(n, k):
        piece = r.msend.at[:, part_rows(k)]
        return remote(
            piece, r.mrecv.at[:, part_rows(k)], r.mc_send.at[n], r.mc_recv.at[n], spot.sib
        )

    def part(n, carry):
        k = part_order(spot, n)
        mlp_forward(r, spot, k)
        mlp_output(r, spot, k)
        out_copy(n, k).start()

        @pl.when(n == 0)
        def _():
            moves.cot_own.wait()
            moves.cot_c.wait()
            moves.cot_y.wait()
            moves.cot_f.start()
            moves.cot_f.wait()

        mlp_backward(r, spot, k)

        @pl.when(n == 0)
        def _():
            r.ps[0] = r.work[...].astype(BF16)
            reduce_copies()[0].start()

        @pl.when(n == 1)
        def _():
            reduce_copies()[0].wait()
            r.ps[1] = (r.work[...] + r.rb[0].astype(F32)).astype(BF16)
            reduce_copies()[1].start()

        @pl.when(n == 2)
        def _():
            r.ps[2] = r.work[...].astype(BF16)
            reduce_copies()[2].start()

        return carry

    lax.fori_loop(0, 4, part, 0)
    reduce_copies()[1].wait()
    reduce_copies()[2].wait()

    def norm_back(i, carry):
        local = pl.ds(pl.multiple_of(i * 48, 16), 48)
        rows_now = pl.ds(pl.multiple_of(spot.mp * PART + i * 48, 16), 48)
        grad = r.work[local, :] + r.rb[2, local, :].astype(F32) + r.rb[1, local, :].astype(F32)
        normed = r.n2[local, :]
        r.sums[1:2, :] += jnp.sum(grad * normed, axis=0, keepdims=True)
        r.sums[2:3, :] += jnp.sum(grad, axis=0, keepdims=True)
        scaled = grad * r.smallf[2:3, :]
        first = jnp.mean(scaled, axis=1, keepdims=True)
        second = jnp.mean(scaled * normed, axis=1, keepdims=True)
        back = r.inv2[local, 0:1] * (scaled - first - normed * second)
        r.gatt[rows_now, :] = (r.gout[rows_now, :].astype(F32) + back).astype(BF16)
        return carry

    def spread(s):
        own = r.gatt.at[part_rows(spot.mp, SUB, s * SUB)]
        other = r.gatt.at[part_rows(spot.yp_mp, SUB, s * SUB)]
        return (
            remote(own, own, r.gy_send.at[s], r.gy_recv.at[s], spot.yp),
            remote(own, own, r.gc_send.at[s], r.gc_recv.at[s], spot.sib),
            remote(other, other, r.gf_send.at[s], r.gf_recv.at[s], spot.sib),
        )

    for s in range(SUBS):
        lax.fori_loop(3 * s, 3 * s + 3, norm_back, 0)
        to_y, to_sib, _ = spread(s)
        to_y.start()
        to_sib.start()

    r.gdn[...] = (dot(r.act[...], r.gout[...], TN) * r.share[0:1, 0:1]).astype(BF16)

    for n in range(4):
        out_copy(n, part_order(spot, n)).wait()

    def chip_sum(i, carry):
        rows_now = pl.ds(pl.multiple_of(i * SUB, 16), SUB)
        r.ysend[rows_now, :] = (
            r.mown[1 - spot.y, rows_now, :] + r.mrecv[1 - spot.y, rows_now, :].astype(F32)
        ).astype(BF16)
        return carry

    lax.fori_loop(0, ROWS // SUB, chip_sum, 0)
    out_y = remote(r.ysend, r.yrecv, r.my_send, r.my_recv, spot.yp)
    out_y.start()
    for s in range(SUBS):
        to_y, _, onward = spread(s)
        to_y.wait()
        onward.start()
    r.gup[...] = (dot(r.h2[...], r.gpre[...], TN) * r.share[0:1, 0:1]).astype(BF16)
    out_y.wait()
    bias = own_columns(spot, jnp.broadcast_to(r.smallb[0:1, :], (8, 768)))[0:1, :]

    def finish(i, carry):
        rows_now = pl.ds(pl.multiple_of(i * SUB, 16), SUB)
        total = (
            r.mown[spot.y, rows_now, :]
            + r.mrecv[spot.y, rows_now, :].astype(F32)
            + r.yrecv[rows_now, :].astype(F32)
        )
        keep = r.info[rows_now, 2:3]
        r.out[rows_now, :] = (keep * (r.midc[rows_now, :] + (total + bias))).astype(BF16)
        cot = r.cot[rows_now, :].astype(F32) * keep
        r.sums[3:4, :192] += jnp.sum(cot, axis=0, keepdims=True)
        return carry

    lax.fori_loop(0, ROWS // SUB, finish, 0)
    for s in range(SUBS):
        _, to_sib, onward = spread(s)
        to_sib.wait()
        onward.wait()


def run_b(a, cot, wout, wup, bup, wdown, info, dp_bits):
    ins = dict(
        att=(a.att, VM),
        tokf=(a.tokf, VM),
        cot=(cot, VM),
        wout=(wout, VM),
        wup=(wup, VM),
        bup=(bup, VM),
        wdown=(wdown, VM),
        info=(info, VM),
        smallf=(a.smallf, VM),
        smallb=(a.smallb, VM),
        share=(a.share, VM),
    )
    outs = dict(
        gatt=((ROWS, 768), BF16, VM),
        out=((ROWS, 192), BF16, VM),
        gdn=((768, 768), BF16, VM),
        gup=((768, 768), BF16, VM),
        sums=((8, 768), F32, VM),
    )
    scratch = dict(
        wof=pltpu.VMEM((768, 768), BF16),
        cotp=pltpu.VMEM((4, ROWS, 192), BF16),
        gout=pltpu.VMEM((ROWS, 768), BF16),
        h2=pltpu.VMEM((ROWS, 768), BF16),
        act=pltpu.VMEM((ROWS, 768), BF16),
        gpre=pltpu.VMEM((ROWS, 768), BF16),
        work=pltpu.VMEM((PART, 768), F32),
        n2=pltpu.VMEM((PART, 768), F32),
        inv2=pltpu.VMEM((PART, 128), F32),
        midc=pltpu.VMEM((ROWS, 192), F32),
        ps=pltpu.VMEM((3, PART, 768), BF16),
        rb=pltpu.VMEM((3, PART, 768), BF16),
        mown=pltpu.VMEM((2, ROWS, 192), F32),
        msend=pltpu.VMEM((2, ROWS, 192), BF16),
        mrecv=pltpu.VMEM((2, ROWS, 192), BF16),
        ysend=pltpu.VMEM((ROWS, 192), BF16),
        yrecv=pltpu.VMEM((ROWS, 192), BF16),
        own_sem=dma(2),
        wo_send=dma(3),
        wo_recv=dma(3),
        ct_send=dma(3),
        ct_recv=dma(3),
        rs_send=dma(3),
        rs_recv=dma(3),
        mc_send=dma(4),
        mc_recv=dma(4),
        my_send=dma(),
        my_recv=dma(),
        gy_send=dma(SUBS),
        gy_recv=dma(SUBS),
        gc_send=dma(SUBS),
        gc_recv=dma(SUBS),
        gf_send=dma(SUBS),
        gf_recv=dma(SUBS),
    )
    return call_kernel(kernel_b, ins, outs, scratch, 2, 60, dp_bits)


class Reduce:
    def __init__(self, spot, acc, arrive, res, order, send, recv):
        self.spot, self.acc, self.arrive, self.res = spot, acc, arrive, res
        self.send, self.recv = send, recv
        self.phases = []
        self.at = 0
        offset, size, held = 0, acc.shape[0], None
        used = 0
        gathers = []
        for bit in order:
            mine = (spot.dp // (1 << bit)) % 2
            start = 0 if held is None else held
            source = acc if held is None else arrive
            if (size // 2) % 16 == 0:
                size = size // 2
                keep, away = start + mine * size, start + (1 - mine) * size
                offset = offset + mine * size
                gathers.append(("gather", bit, res, offset, offset, size, 0))
            else:
                keep, away = start, start
            self.phases.append(("sum", bit, source, away, keep, size, used))
            held = used
            used += size
        self.own = (held, offset, size)
        self.sums = len(self.phases)
        self.phases += gathers[::-1]

    def copy(self):
        kind, bit, source, away, keep, size, used = self.phases[self.at]
        piece = source.at[pl.ds(pl.multiple_of(away, 16), size)]
        target = self.arrive.at[pl.ds(used, size)] if kind == "sum" else piece
        device = (dp_partner(self.spot, bit), self.spot.mp)
        return remote(piece, target, self.send.at[self.at], self.recv.at[self.at], device)

    def start(self):
        self.copy().start()

    def add(self):
        _, _, source, _, keep, size, used = self.phases[self.at]
        last = self.at == self.sums - 1
        step = 48 if size % 48 == 0 else 16

        def block(i, carry):
            rows = pl.ds(pl.multiple_of(keep + i * step, 16), step)
            new = pl.ds(pl.multiple_of(used + i * step, 16), step)
            total = (source[rows, :].astype(F32) + self.arrive[new, :].astype(F32)).astype(BF16)
            if last:
                self.res[pl.ds(pl.multiple_of(self.own[1] + i * step, 16), step), :] = total
            else:
                self.arrive[new, :] = total
            return carry

        lax.fori_loop(0, size // step, block, 0)

    def advance(self):
        if self.at >= len(self.phases):
            return
        self.copy().wait()
        if self.phases[self.at][0] == "sum":
            self.add()
        self.at += 1
        if self.at < len(self.phases):
            self.start()


def arrive_rows(rows, dp_bits):
    total = 0
    for _ in range(dp_bits):
        rows = rows // 2 if (rows // 2) % 16 == 0 else rows
        total += rows
    return total


def back_tile(r, spot, tile, start, width):
    rows = pl.ds(pl.multiple_of(tile * TILE, 16), TILE)
    window = pl.ds(pl.multiple_of(start, 16), width)
    g_att = dot(r.gatt[rows, :], r.wout[...], NT).astype(BF16)
    allowed = r.info[window, 3:4] == r.qseg[tile, 0:1, :]
    mask = jnp.where(allowed, 0.0, -1e30)
    logs = jnp.transpose(r.lse[rows, :])
    outs = []
    for h in range(3):
        query = r.q3[h, rows, :] * BF16(0.125)
        keys = r.k3[h, window, :]
        grad = g_att[:, 64 * h : 64 * h + 64]
        probs = jnp.exp(dot(keys, query, NT) + mask - logs[h : h + 1, :])
        g_probs = dot(r.v3[h, window, :], grad, NT)
        center = jnp.sum(probs * g_probs, axis=0, keepdims=True)
        g_scores = (probs * (g_probs - center)).astype(BF16)
        r.dv[h, window, :] += dot(probs.astype(BF16), grad)
        r.dk[h, window, :] += dot(g_scores, query)
        outs.append(dot(keys, g_scores, TN) * 0.125)
    r.dq[rows, :] = jnp.transpose(jnp.concatenate(outs, axis=0)).astype(BF16)


def unrotate(r):
    step = 144

    def block(i, carry):
        rows = pl.ds(pl.multiple_of(i * step, 16), step)
        parts = [r.dq[rows, :].astype(F32)]
        parts += [r.dk[h, rows, :].astype(BF16).astype(F32) for h in range(3)]
        grads = jnp.concatenate(parts, axis=1)
        rotated = r.qk[rows, :].astype(F32)
        plain = grads * r.cos[rows, :] - swap_halves(grads) * r.sin[rows, :]
        values = jnp.concatenate([r.dv[h, rows, :] for h in range(3)], axis=1)
        packed = jnp.concatenate([plain, values], axis=1).astype(BF16)
        r.gproj[rows, :] = packed
        turn = grads * swap_halves(rotated)
        turn = jnp.where(front_lanes(turn.shape), -turn, turn)
        r.sums[0:1, :576] += jnp.sum(packed.astype(F32), axis=0, keepdims=True)
        r.sums[1:2, :384] += jnp.sum(turn * r.info[rows, 0:1], axis=0, keepdims=True)
        r.sums[2:3, :384] += jnp.sum(turn * r.info[rows, 1:2], axis=0, keepdims=True)
        r.sums[3:4, :] += jnp.sum(r.gatt[rows, :].astype(F32), axis=0, keepdims=True)
        return carry

    lax.fori_loop(0, ROWS // step, block, 0)


def first_norm_back(r, spot, n):
    rows = part_rows(n)
    r.work[...] = dot(r.gproj[rows, :], r.wqkv[...], NT)

    def block(i, carry):
        local = pl.ds(pl.multiple_of(i * 48, 16), 48)
        rows_now = pl.ds(pl.multiple_of(n * PART + i * 48, 16), 48)
        values = r.tokf[rows_now, :].astype(F32)
        mean = jnp.mean(values, axis=1, keepdims=True)
        square = jnp.mean(values * values, axis=1, keepdims=True)
        inverse = lax.rsqrt(square - mean * mean + norm_eps)
        normed = (values - mean) * inverse
        grad = r.work[local, :]
        scaled = grad * r.smallf[0:1, :]
        first = jnp.sum(scaled, axis=1, keepdims=True)
        second = jnp.sum(scaled * normed, axis=1, keepdims=True)
        lane = lax.broadcasted_iota(jnp.int32, (48, 128), 1)
        r.stat[rows_now, :] = jnp.where(lane == 0, first, jnp.where(lane == 1, second, inverse))
        r.n1[rows_now, :] = own_columns(spot, normed)
        mine, other = core_columns(spot, grad)
        for y in range(2):
            r.mown[y, rows_now, :] = mine[y]
            r.msend[y, rows_now, :] = other[y].astype(BF16)
        return carry

    lax.fori_loop(0, PART // 48, block, 0)


def kernel_c(r, spot):
    peers = [(dp_partner(spot, bit), spot.mp) for bit in range(r.dp_bits)]
    greet([spot.sib, spot.yp] + peers)
    load = pltpu.make_async_copy(r.att.at[spot.mp], r.attown, r.load_sem)
    load.start()
    order = list(range(r.dp_bits))
    turned = order[1:] + order[:1]
    down = Reduce(spot, r.gdn, r.ardn, r.resdn, order, r.dn_send, r.dn_recv)
    up = Reduce(spot, r.gup, r.arup, r.resup, turned, r.up_send, r.up_recv)
    out = Reduce(spot, r.accwo, r.arwo, r.reswo, order, r.wo_send, r.wo_recv)
    qkv = Reduce(spot, r.accqkv, r.arqkv, r.resqkv, order, r.qk_send, r.qk_recv)
    down.start()
    up.start()
    load.wait()
    r.accwo[...] = (dot(r.attown[...], r.gatt[...], TN) * r.share[0:1, 0:1]).astype(BF16)
    out.start()
    r.sums[...] = jnp.zeros_like(r.sums)
    r.sums[8:16, :] = r.sumsb[...]
    r.dk[...] = jnp.zeros_like(r.dk)
    r.dv[...] = jnp.zeros_like(r.dv)

    def narrow(n, carry):
        turn = n + spot.y * (6 - 2 * n)
        tile, start = narrow_tile(turn)
        back_tile(r, spot, tile, start, NARROW)
        return carry

    lax.fori_loop(0, 3, narrow, 0)
    down.advance()
    up.advance()
    out.advance()
    lax.fori_loop(3, 5, narrow, 0)
    down.advance()
    out.advance()
    lax.fori_loop(5, 7, narrow, 0)
    up.advance()
    down.advance()
    out.advance()

    def wide(n, carry):
        tile, start = wide_tile(n)
        back_tile(r, spot, tile, start, WIDE)
        return carry

    lax.fori_loop(0, 2, wide, 0)
    down.advance()
    up.advance()
    out.advance()
    unrotate(r)
    r.accqkv[...] = (dot(r.h1[...], r.gproj[...], TN) * r.share[0:1, 0:1]).astype(BF16)
    qkv.start()
    down.advance()
    up.advance()
    out.advance()

    def core_copy(n):
        piece = part_rows(n)
        return remote(
            r.msend.at[:, piece], r.mrecv.at[:, piece], r.mc_send.at[n], r.mc_recv.at[n], spot.sib
        )

    def y_copy(n):
        piece = part_rows(n)
        return remote(
            r.ysend.at[piece], r.yrecv.at[piece], r.my_send.at[n], r.my_recv.at[n], spot.yp
        )

    def pass_on(n):
        core_copy(n).wait()

        def chip_sum(i, carry):
            rows_now = pl.ds(pl.multiple_of(n * PART + i * SUB, 16), SUB)
            r.ysend[rows_now, :] = (
                r.mown[1 - spot.y, rows_now, :] + r.mrecv[1 - spot.y, rows_now, :].astype(F32)
            ).astype(BF16)
            return carry

        lax.fori_loop(0, SUBS, chip_sum, 0)
        y_copy(n).start()

    def part(n, carry):
        first_norm_back(r, spot, n)
        core_copy(n).start()

        @pl.when(n >= 1)
        def _():
            pass_on(n - 1)

        return carry

    lax.fori_loop(0, 2, part, 0)
    up.advance()
    qkv.advance()
    lax.fori_loop(2, 4, part, 0)
    pass_on(3)
    for t in range(13):
        r.strow[:, 128 * t : 128 * t + 128] = jnp.transpose(r.stat[128 * t : 128 * t + 128, :])[0:8, :]
    r.strow[:, 1664:1792] = jnp.transpose(
        jnp.concatenate([r.stat[1664:1728, :], jnp.zeros((64, 128), F32)], axis=0)
    )[0:8, :]
    to_sib = remote(r.strow, r.starr.at[0], r.st_send.at[0], r.st_recv.at[0], spot.sib)
    to_sib.start()
    qkv.advance()
    to_sib.wait()
    r.stsum[...] = r.strow[...] + r.starr[0]
    to_y = remote(r.stsum, r.starr.at[1], r.st_send.at[1], r.st_recv.at[1], spot.yp)
    to_y.start()
    down.advance()
    qkv.advance()
    to_y.wait()
    r.sttot[0:8, :] = r.stsum[...] + r.starr[1]
    for t in range(13):
        r.back[128 * t : 128 * t + 128, :] = jnp.transpose(r.sttot[:, 128 * t : 128 * t + 128])
    r.back[1664:1728, :] = jnp.transpose(r.sttot[:, 1664:1792])[0:64, :]
    for n in range(4):
        y_copy(n).wait()

    def finish(i, carry):
        rows = pl.ds(pl.multiple_of(i * SUB, 16), SUB)
        grad = (
            r.mown[spot.y, rows, :]
            + r.mrecv[spot.y, rows, :].astype(F32)
            + r.yrecv[rows, :].astype(F32)
        )
        normed = r.n1[rows, :]
        r.sums[4:5, :192] += jnp.sum(grad * normed, axis=0, keepdims=True)
        r.sums[5:6, :192] += jnp.sum(grad, axis=0, keepdims=True)
        first = r.back[rows, 0:1] * (1.0 / 768.0)
        second = r.back[rows, 1:2] * (1.0 / 768.0)
        scaled = grad * r.small[0:1, :]
        step_back = r.stat[rows, 2:3] * (scaled - first - normed * second)
        r.igrad[rows, :] = own_columns(spot, r.gatt[rows, :].astype(F32)) + step_back
        return carry

    lax.fori_loop(0, ROWS // SUB, finish, 0)
    r.sums[...] = r.sums[...] * r.share[0:1, 0:1]
    for step, device in enumerate([spot.sib, spot.yp] + peers):
        span = pl.ds(8, 8) if step < 2 else pl.ds(0, 16)
        r.sumx[step] = r.sums[...]
        copy = remote(
            r.sumx.at[step, span], r.sumr.at[step, span], r.su_send.at[step], r.su_recv.at[step], device
        )
        copy.start()
        qkv.advance()
        copy.wait()
        if step < 2:
            r.sums[9:11, :] = r.sumx[step, 9:11, :] + r.sumr[step, 9:11, :]
        else:
            r.sums[...] = r.sumx[step] + r.sumr[step]
    for reduce in (down, up, out, qkv):
        while reduce.at < len(reduce.phases):
            reduce.advance()


def run_c(a, b, small, wout, wqkv, info, qseg, dp_bits):
    ins = dict(
        gatt=(b.gatt, VM),
        att=(a.att, pl.ANY),
        gdn=(b.gdn, VM),
        gup=(b.gup, VM),
        sumsb=(b.sums, VM),
        tokf=(a.tokf, VM),
        h1=(a.h1, VM),
        q3=(a.q3, VM),
        k3=(a.k3, VM),
        v3=(a.v3, VM),
        lse=(a.lse, VM),
        qk=(a.qk, VM),
        cos=(a.cos, VM),
        sin=(a.sin, VM),
        info=(info, VM),
        qseg=(qseg, VM),
        wout=(wout, VM),
        wqkv=(wqkv, VM),
        smallf=(a.smallf, VM),
        small=(small, VM),
        share=(a.share, VM),
    )
    outs = dict(
        igrad=((ROWS, 192), F32, VM),
        resdn=((768, 768), BF16, VM),
        resup=((768, 768), BF16, VM),
        reswo=((192, 768), BF16, VM),
        resqkv=((768, 576), BF16, VM),
        sums=((16, 768), F32, VM),
    )
    phases = 2 * dp_bits
    scratch = dict(
        attown=pltpu.VMEM((ROWS, 192), BF16),
        accwo=pltpu.VMEM((192, 768), BF16),
        accqkv=pltpu.VMEM((768, 576), BF16),
        ardn=pltpu.VMEM((arrive_rows(768, dp_bits), 768), BF16),
        arup=pltpu.VMEM((arrive_rows(768, dp_bits), 768), BF16),
        arwo=pltpu.VMEM((arrive_rows(192, dp_bits), 768), BF16),
        arqkv=pltpu.VMEM((arrive_rows(768, dp_bits), 576), BF16),
        dk=pltpu.VMEM((3, ROWS, 64), F32),
        dv=pltpu.VMEM((3, ROWS, 64), F32),
        dq=pltpu.VMEM((ROWS, 192), BF16),
        gproj=pltpu.VMEM((ROWS, 576), BF16),
        work=pltpu.VMEM((PART, 768), F32),
        stat=pltpu.VMEM((ROWS, 128), F32),
        back=pltpu.VMEM((ROWS, 128), F32),
        strow=pltpu.VMEM((8, 1792), F32),
        stsum=pltpu.VMEM((8, 1792), F32),
        starr=pltpu.VMEM((2, 8, 1792), F32),
        sttot=pltpu.VMEM((128, 1792), F32),
        n1=pltpu.VMEM((ROWS, 192), F32),
        mown=pltpu.VMEM((2, ROWS, 192), F32),
        msend=pltpu.VMEM((2, ROWS, 192), BF16),
        mrecv=pltpu.VMEM((2, ROWS, 192), BF16),
        ysend=pltpu.VMEM((ROWS, 192), BF16),
        yrecv=pltpu.VMEM((ROWS, 192), BF16),
        sumx=pltpu.VMEM((dp_bits + 2, 16, 768), F32),
        sumr=pltpu.VMEM((dp_bits + 2, 16, 768), F32),
        load_sem=dma(),
        dn_send=dma(phases),
        dn_recv=dma(phases),
        up_send=dma(phases),
        up_recv=dma(phases),
        wo_send=dma(phases),
        wo_recv=dma(phases),
        qk_send=dma(phases),
        qk_recv=dma(phases),
        mc_send=dma(4),
        mc_recv=dma(4),
        my_send=dma(4),
        my_recv=dma(4),
        st_send=dma(2),
        st_recv=dma(2),
        su_send=dma(dp_bits + 2),
        su_recv=dma(dp_bits + 2),
    )
    return call_kernel(kernel_c, ins, outs, scratch, 3, 63, dp_bits)


def key_windows(key_segment):
    starts = []
    for tile in range(TILES):
        if tile % 3 == 0 and tile:
            starts.append(384 + 576 * (tile // 3 - 1))
        else:
            starts.append(576 * (tile // 3) - 32 * (tile // 6))
    padded = jnp.pad(key_segment, (0, WIDE), constant_values=-3.0)
    return jnp.broadcast_to(
        jnp.stack([padded[s : s + WIDE] for s in starts])[:, None, :], (TILES, 8, WIDE)
    )


norm_eps = 1e-06
root_half = 0.7071067811865476
inv_root_two_pi = 0.3989422804014327


def local(
    tokens,
    w_qkv,
    b_qkv,
    freqs,
    w_out,
    b_out,
    norm1_gain,
    norm1_bias,
    norm2_gain,
    norm2_bias,
    w_up,
    b_up,
    w_down,
    b_down,
    cotangent,
    keep_mask,
    coords,
    block_group,
):
    row_count, width_loc = tokens.shape
    heads_loc = freqs.shape[1]
    column = lax.axis_index("mp") * width_loc
    keep_float = keep_mask.astype(jnp.float32)
    group_now = block_group[0]
    kept_total = jnp.sum(keep_float)
    row_index = jnp.arange(row_count, dtype=jnp.int32)
    segment_size = jnp.where(group_now == 0, GRID_LO * GRID_LO, SLOTS).astype(jnp.int32)
    segment_ids = row_index // segment_size
    key_keep = keep_mask > 0
    segment_float = segment_ids.astype(jnp.float32)
    key_segment = jnp.where(key_keep, segment_float, -1.0)
    info = jnp.stack(
        [coords[0].astype(F32), coords[1].astype(F32), keep_float, key_segment, segment_float]
        + [keep_float] * 3,
        axis=1,
    )
    small = jnp.stack(
        [
            part.astype(F32)
            for part in (norm1_gain, norm1_bias, norm2_gain, norm2_bias, b_out, b_down, b_out, b_out)
        ]
    )
    wqkv_flat = w_qkv.reshape(w_qkv.shape[0], 3 * width_loc)
    bqkv_flat = jnp.broadcast_to(b_qkv.reshape(1, 3 * width_loc).astype(F32), (8, 3 * width_loc))
    half_freqs = jnp.concatenate([freqs, freqs], axis=2).reshape(2, width_loc)
    freq = jnp.pad(jnp.concatenate([half_freqs, half_freqs], axis=1), ((0, 6), (0, 0)))
    low = (group_now == 0).astype(F32)
    cnt = jnp.pad(
        jnp.broadcast_to(jnp.stack([kept_total * low, kept_total * (1.0 - low), low]), (8, 3)),
        ((0, 0), (0, 125)),
    )
    dp_bits = lax.axis_size("dp").bit_length() - 1
    a = run_a(tokens, small, wqkv_flat, bqkv_flat, freq, info, key_windows(key_segment), cnt, dp_bits)
    a.smallb = jnp.broadcast_to(a.smallf[5:6], (8, 768))
    bup = jnp.broadcast_to(b_up.astype(F32)[None], (8, b_up.shape[0]))
    b = run_b(a, cotangent, w_out, w_up, bup, w_down, info, dp_bits)
    qseg = jnp.broadcast_to(segment_float.reshape(TILES, 1, TILE), (TILES, 8, TILE))
    c = run_c(a, b, small, w_out, wqkv_flat, info, qseg, dp_bits)
    sums = c.sums

    def own(row):
        return lax.dynamic_slice_in_dim(row, column, width_loc, 0)

    turns = sums[1:3, :384].reshape(2, 2, heads_loc, 2, HEAD_DIM // 2)
    return (
        b.out,
        c.igrad,
        c.resqkv.astype(F32).reshape(w_qkv.shape),
        sums[0, : 3 * width_loc].reshape(3, width_loc),
        jnp.sum(turns, axis=(1, 3)),
        c.reswo.astype(F32),
        own(sums[3]),
        sums[4, :width_loc],
        sums[5, :width_loc],
        own(sums[9]),
        own(sums[10]),
        c.resup.astype(F32),
        sums[8],
        c.resdn.astype(F32),
        sums[11, :width_loc],
    )


def solution(mesh):
    return jax.shard_map(
        local,
        mesh=mesh,
        in_specs=(
            P("dp", "mp"),
            P(None, None, "mp"),
            P(None, "mp"),
            P(None, "mp", None),
            P("mp", None),
            P("mp"),
            P("mp"),
            P("mp"),
            P("mp"),
            P("mp"),
            P(None, "mp"),
            P("mp"),
            P("mp", None),
            P("mp"),
            P("dp", "mp"),
            P("dp"),
            P(None, "dp"),
            P("dp"),
        ),
        out_specs=(
            P("dp", "mp"),
            P("dp", "mp"),
            P(None, None, "mp"),
            P(None, "mp"),
            P(None, "mp", None),
            P("mp", None),
            P("mp"),
            P("mp"),
            P("mp"),
            P("mp"),
            P("mp"),
            P(None, "mp"),
            P("mp"),
            P("mp", None),
            P("mp"),
        ),
        check_vma=False,
    )
```

time: 846 us -> 346 us (0.41)
  waiting for transfers between devices: 421 us -> 0 us
  Pallas kernels: 72.3 us -> 310 us
  matrix products: 115 us -> 0 us
  other arithmetic: 84.2 us -> 6.9 us
  blocking collectives: 60.8 us -> 0 us
  local copies, waits for them, and re-layouts: 64 us -> 25.2 us
  between operations: 19.5 us -> 2.88 us
    psum x4 -> x0, waiting for transfers between devices: 418 us -> none  [the longest x1 188 us: local(): lax.psum((own_weight * grad_w_qkv, own_weight * grad_b_qkv, own_weight *...]
    pallas_call x1 -> x3, Pallas kernels: 72.3 us -> 310 us  [call_kernel(): pl.pallas_call(body, out_shape=[jax.ShapeDtypeStruct(shape, dtype) for sh...]
    dot_general x25 -> x0, matrix products: 113 us -> none  [the longest x3 20.4 us: back_block(): jnp.einsum('qhd,khd->hqk', grad_blk, value_low, preferred_element_type=jn...]
    psum x2 -> x0, blocking collectives: 60.8 us -> none  [the longest x1 39.8 us: local(): lax.psum((own_weight * grad_w_qkv, own_weight * grad_b_qkv, own_weight *...]
    reduce_sum x7 -> x2, other arithmetic: 30.5 us -> 0.63 us  [the longest x1 0.6 us: local(): kept_total = jnp.sum(keep_float)]
    convert_element_type x11 -> x3, other arithmetic: 29.2 us -> 4.01 us  [the longest x1 1.58 us: local(): c.resup.astype(F32)]
    unnamed x95 -> x39, local copies, waits for them, and re-layouts: 32.6 us -> 9.83 us
    convert_element_type x3 -> x0, local copies, waits for them, and re-layouts: 9.72 us -> none  [the longest x2 6.62 us: local(): grad_query.reshape(head_shape).astype(jnp.float32)]
  transfers between devices with their start and end apart: 6 -> 0, of which waited for: 5 -> 0; matrix products, arithmetic and copies ran while one was open for 25% -> 0% of each run, Pallas kernels for 0% -> 0%
where the time goes in v2:
time: 346 us; the launch traced here: 345 us
  Pallas kernels  310 us (90%)
  local copies, waits for them, and re-layouts  25.2 us (7%)
  other arithmetic  6.9 us (2%)
    pallas_call x3, Pallas kernels, call_kernel(): pl.pallas_call(body, out_shape=[jax.ShapeDtypeStruct(shape, dtype) for sh...  310 us
    unnamed x39, local copies, waits for them, and re-layouts  9.83 us

profile of v2, /device:TPU:0, one launch (start us, length us, event | category | flops | bytes accessed | tf_op | source)
XLA Modules:
  0.0 345.2 jit_solution(1294373027915278115)
XLA Ops:
  0.6 0.0 copy-start.11
  0.7 0.0 copy-start.12
  0.7 0.0 copy-start.13
  0.7 0.0 copy-start.14
  0.7 0.0 copy-start.15
  0.7 0.0 copy-start.16
  0.7 0.0 copy-start.3
  0.7 0.0 copy-start.9
  0.7 0.0 copy-start.8
  0.7 2.4 copy.56.refs_0_
  3.1 0.0 copy-done.11
  3.2 0.0 copy-done.12
  3.2 0.0 copy-done.13
  3.2 0.0 copy-done.14
  3.2 0.0 copy-done.15
  3.2 0.0 copy-done.16
  3.3 0.6 stack.87.refs_1_.refs_19_
  3.9 0.0 copy-done.3
  3.9 1.3 copy.57.refs_2_.refs_17_
  5.2 0.0 copy-done.9
  5.2 0.1 reshape.145
  5.3 0.6 broadcast_in_dim.16.refs_3_
  5.9 0.0 copy-done.8
  5.9 0.1 pad_maximum_fusion
  6.0 0.1 reshape.141
  6.1 0.7 select_maximum_fusion.refs_4_
  7.4 0.6 convert_reduce_fusion
  8.1 0.6 fusion.5
  8.7 0.1 stack.90
  8.8 1.2 copy.58.refs_5_.refs_7_.refs_14_
  10.0 0.1 pad_slice_fusion
  10.1 0.1 stack.96
  10.2 0.7 broadcast_in_dim.18.refs_6_
  12.2 0.1 select_maximum_fusion.1
  12.2 0.6 pad.17.refs_7_
  12.8 73.8 %shard_map.289 = (bf16[1728,768]{1,0:T(8,128)(2,1)}, bf16[1728,768]{1,0:T(8,128)(2,1)}, bf16[1728,384]{1,0:T(8,128)(2,1)}, bf16[3,1728,64]{2,1,0:T(8,128)(2,1)},...) custom-call(bf16[1728,192]{1,0:T(8,128)(2,1)} %copy.56.refs_0_, ...), custom_call_target="tpu_custom_call" | custom-call | tf_op jit(solution)/shard_map/pallas_call | solution.py:288
  86.6 0.0 copy-start.10
  86.7 0.0 copy-done.4
  86.7 1.2 copy.59.refs_2_
  87.9 0.0 copy-done.10
  87.9 0.6 broadcast_in_dim.19.refs_5_
  88.5 0.8 slice_reduce_fusion.1
  89.2 0.6 broadcast_in_dim.39.refs_9_
  89.9 101.2 %shard_map.290 = (bf16[1728,768]{1,0:T(8,128)(2,1)}, bf16[1728,192]{1,0:T(8,128)(2,1)}, bf16[768,768]{1,0:T(8,128)(2,1)}, bf16[768,768]{1,0:T(8,128)(2,1)}, f32[8,768]{1,0:T(8,128)}) custom-call(bf16[4,1728,192]{2,1,0:T(8,128)(2,1)} %get-tuple-element.38.refs_0_.refs_1_, bf16[1728,768]{1,0:T(8,128)(2,1)} %get-tuple-element.39.refs_1_.refs_5_, ...), custom_call_target="tpu_custom_call" | custom-call | tf_op jit(solution)/shard_map/pallas_call | solution.py:288
  191.0 2.3 copy.64
  193.3 0.2 fusion
  193.6 0.6 broadcast_in_dim.40.refs_15_
  194.2 135.3 %shard_map.291 = (f32[1728,192]{1,0:T(8,128)}, bf16[768,768]{1,0:T(8,128)(2,1)}, bf16[768,768]{1,0:T(8,128)(2,1)}, bf16[192,768]{1,0:T(8,128)(2,1)}, bf16[768,576]{1,0:T(8,128)(2,1)}, /*index=5*/f32[16,768]{1,0:T(8,128)}) custom-call(bf16[1728,768]{1,0:T(8,128)(2,1)} %get-tuple-element.43.refs_0_, bf16[4,1728,192]{2,1,0:T(8,128)(2,1)} %get-tuple-element.38.refs_0_.refs_1_, ...), custom_call_target="tpu_custom_call" | custom-call | tf_op jit(solution)/shard_map/pallas_call | solution.py:288
  329.5 3.2 copy.65
  332.7 0.0 copy-done.2
  332.7 1.5 copy.63
  334.2 0.7 slice_reduce_fusion.2
  334.9 0.7 reshape_squeeze.3
  335.6 0.7 slice.68
  336.3 0.1 reshape.144
  336.4 0.6 copy.66
  337.0 0.9 convert_element_type.98
  337.8 1.5 slice_reduce_fusion
  339.3 0.6 constant_dynamic-slice_fusion.2
  340.0 1.3 fusion.6
  341.3 0.6 constant_dynamic-slice_fusion
  341.9 1.6 convert_element_type.99
  343.5 0.1 copy-done
  343.6 1.6 convert_element_type.100
  (29 shorter events, 0.2 us)
Async XLA Ops:
  0.6 2.5 copy-start.11
  0.7 2.5 copy-start.12
  0.7 2.5 copy-start.13
  0.7 2.5 copy-start.14
  0.7 2.5 copy-start.15
  0.7 2.5 copy-start.16
  0.7 3.2 copy-start.3
  0.7 4.5 %copy-start.9 = (bf16[3,192]{1,0:T(4,128)(2,1)S(1)}, bf16[3,192]{1,0:T(4,128)(2,1)}, u32[]{:S(2)}) copy-start(bf16[3,192]{1,0:T(4,128)(2,1)} %param.20) | copy-start | bytes 3460
  0.7 5.2 %copy-start.8 = (f32[2,3,32]{2,0,1:T(2,128)S(1)}, f32[2,3,32]{2,0,1:T(2,128)}, u32[]{:S(2)}) copy-start(f32[2,3,32]{2,0,1:T(2,128)} %param.21) | copy-start | bytes 2308
  3.1 3.6 %copy-start.7 = (s32[2,1728]{1,0:T(2,128)S(1)}, s32[2,1728]{1,0:T(2,128)}, u32[]{:S(2)}) copy-start(s32[2,1728]{1,0:T(2,128)} %param.34) | copy-start | bytes 41476
  3.1 3.6 %copy-start.6 = (s32[1728]{0:T(1024)S(1)}, s32[1728]{0:T(1024)}, u32[]{:S(2)}) copy-start(s32[1728]{0:T(1024)} %param.33) | copy-start | bytes 20740
  12.8 73.8 %copy-start.4 = (bf16[1728,192]{0,1:T(8,128)(2,1)S(1)}, bf16[1728,192]{0,1:T(8,128)(2,1)}, u32[]{:S(2)}) copy-start(bf16[1728,192]{0,1:T(8,128)(2,1)} %param.32) | copy-start | bytes 1990660
  86.6 1.2 copy-start.10
  329.5 3.2 copy-start.2
  332.7 4.3 %copy-start.5 = (bf16[192,768]{1,0:T(8,128)(2,1)S(1)}, bf16[192,768]{1,0:T(8,128)(2,1)}, u32[]{:S(2)}) copy-start(bf16[192,768]{1,0:T(8,128)(2,1)} %get-tuple-element.58) | copy-start | bytes 884740
  332.7 9.3 %copy-start.1 = (bf16[768,768]{1,0:T(8,128)(2,1)S(1)}, bf16[768,768]{1,0:T(8,128)(2,1)}, u32[]{:S(2)}) copy-start(bf16[768,768]{1,0:T(8,128)(2,1)} %get-tuple-element.59) | copy-start | bytes 3538948
  341.9 1.7 copy-start

commit v3 on v0

v3 whole, which is shorter than its diff:
```python
import jax
import jax.numpy as jnp
from jax import lax
from jax.experimental import pallas as pl
from jax.experimental.pallas import tpu as pltpu
from jax.sharding import PartitionSpec as P

HEAD_DIM = 64
GRID_LO = 14
SLOTS = 576

MESH = pl.DeviceIdType.MESH
MIB = 1024 * 1024
VM = pltpu.VMEM
F32 = jnp.float32
BF16 = jnp.bfloat16
NT = (((1,), (1,)), ((), ()))
NN = (((1,), (0,)), ((), ()))

D = 768
OWN = 192
ROWS = 1728
LANES = 1792
CHUNK = 256
CHUNKS = LANES // CHUNK
TILE = 128
TILES = LANES // TILE
NARROW = 608

norm_eps = 1e-06
root_half = 0.7071067811865476
inv_root_two_pi = 0.3989422804014327


class Refs:
    pass


def dot(left, right, dims=NN):
    return lax.dot_general(left, right, dims, preferred_element_type=F32)


def remote(src, dst, send, recv, device):
    return pltpu.make_async_remote_copy(
        src_ref=src, dst_ref=dst, send_sem=send, recv_sem=recv, device_id=device, device_id_type=MESH
    )


def place():
    spot = Refs()
    spot.dp = lax.axis_index("dp")
    spot.mp = lax.axis_index("mp")
    spot.y = spot.mp // 2
    spot.c = spot.mp % 2
    spot.sib_mp = 2 * spot.y + 1 - spot.c
    spot.yp_mp = 2 * (1 - spot.y) + spot.c
    spot.sib = (spot.dp, spot.sib_mp)
    spot.yp = (spot.dp, spot.yp_mp)
    return spot


def greet(devices):
    barrier = pltpu.get_barrier_semaphore()
    for device in devices:
        pl.semaphore_signal(barrier, inc=1, device_id=device, device_id_type=MESH)
    pl.semaphore_wait(barrier, len(devices))


def dp_partner(spot, bit):
    mine = (spot.dp // (1 << bit)) % 2
    return (spot.dp + (1 - 2 * mine) * (1 << bit), spot.mp)


def feat(j):
    return pl.ds(pl.multiple_of(OWN * j, 16), OWN)


def lanes(c):
    return pl.ds(pl.multiple_of(c * CHUNK, CHUNK), CHUNK)


def tile_lanes(t):
    return pl.ds(pl.multiple_of(t * TILE, TILE), TILE)


class Reduce:
    def __init__(self, spot, acc, arrive, res, order, send, recv):
        self.spot, self.res, self.send, self.recv = spot, res, send, recv
        self.at = 0
        self.phases = []
        gathers = []
        rows, cols = acc.shape
        row, col = 0, 0
        source, own_row, own_col = acc, 0, 0
        for level, bit in enumerate(order):
            mine = (spot.dp // (1 << bit)) % 2
            keep, away, halved = (0, 0), (0, 0), True
            if (rows // 2) % 16 == 0:
                rows = rows // 2
                keep, away = (mine * rows, 0), ((1 - mine) * rows, 0)
            elif (cols // 2) % 128 == 0:
                cols = cols // 2
                keep, away = (0, mine * cols), (0, (1 - mine) * cols)
            else:
                halved = False
            own_row, own_col = own_row + keep[0], own_col + keep[1]
            shape = (rows, cols)
            self.phases.append((bit, source, away, keep, shape, arrive[level]))
            if halved:
                gathers.append((bit, res, (own_row, own_col), None, shape, res))
            source = arrive[level]
        self.own = (own_row, own_col)
        self.sums = len(self.phases)
        self.phases += gathers[::-1]

    def piece(self, ref, corner, shape):
        def span(start, size, unit, whole):
            if size == whole:
                return pl.ds(0, size)
            return pl.ds(pl.multiple_of(start, unit), size)

        return ref.at[
            span(corner[0], shape[0], 16, ref.shape[0]), span(corner[1], shape[1], 128, ref.shape[1])
        ]

    def copy(self):
        bit, source, away, keep, shape, target = self.phases[self.at]
        piece = self.piece(source, away, shape)
        goal = piece if keep is None else target
        return remote(
            piece, goal, self.send.at[self.at], self.recv.at[self.at], dp_partner(self.spot, bit)
        )

    def start(self):
        self.copy().start()

    def add(self):
        _, source, _, keep, shape, target = self.phases[self.at]
        held = self.piece(source, keep, shape)
        last = self.at == self.sums - 1
        goal = self.piece(self.res, self.own, shape) if last else target
        step = 48 if shape[0] % 48 == 0 else 16

        def block(i, carry):
            rows = pl.ds(pl.multiple_of(i * step, 16), step)
            goal[rows, :] = (held[rows, :].astype(F32) + target[rows, :].astype(F32)).astype(BF16)
            return carry

        lax.fori_loop(0, shape[0] // step, block, 0)

    def advance(self):
        if self.at >= len(self.phases):
            return
        self.copy().wait()
        if self.at < self.sums:
            self.add()
        self.at += 1
        if self.at < len(self.phases):
            self.start()


def arrive_shapes(rows, cols, dp_bits):
    shapes = []
    for _ in range(dp_bits):
        if (rows // 2) % 16 == 0:
            rows = rows // 2
        elif (cols // 2) % 128 == 0:
            cols = cols // 2
        shapes.append((rows, cols))
    return shapes


class Exchange:
    def __init__(self, r, spot, part, arrive, out, come, sems, stats=None):
        self.r, self.spot = r, spot
        self.part, self.arrive, self.out, self.come = part, arrive, out, come
        self.sems, self.stats = sems, stats

    def core(self, c):
        at = lanes(c)
        copies = [
            remote(
                self.part.at[:, 1 - self.spot.c, :, at],
                self.arrive.at[:, :, at],
                self.sems.at[0, c],
                self.sems.at[1, c],
                self.spot.sib,
            )
        ]
        if self.stats is not None:
            copies.append(
                remote(
                    self.stats.at[0, :, at],
                    self.stats.at[1, :, at],
                    self.sems.at[2, c],
                    self.sems.at[3, c],
                    self.spot.sib,
                )
            )
        return copies

    def over(self, c):
        at = lanes(c)
        copies = [
            remote(
                self.out.at[:, at],
                self.come.at[:, at],
                self.sems.at[4, c],
                self.sems.at[5, c],
                self.spot.yp,
            )
        ]
        if self.stats is not None:
            copies.append(
                remote(
                    self.stats.at[2, :, at],
                    self.stats.at[3, :, at],
                    self.sems.at[6, c],
                    self.sems.at[7, c],
                    self.spot.yp,
                )
            )
        return copies

    def give(self, c, values):
        at = lanes(c)
        for j in range(4):
            self.part[j // 2, j % 2, :, at] = values[OWN * j : OWN * j + OWN].astype(BF16)
        for copy in self.core(c):
            copy.start()

    def pass_on(self, c):
        at = lanes(c)
        for copy in self.core(c):
            copy.wait()
        away = 1 - self.spot.y
        self.out[:, at] = (
            self.part[away, self.spot.c, :, at].astype(F32) + self.arrive[away, :, at].astype(F32)
        ).astype(BF16)
        if self.stats is not None:
            self.stats[2, :, at] = self.stats[0, :, at] + self.stats[1, :, at]
        for copy in self.over(c):
            copy.start()

    def take(self, c):
        at = lanes(c)
        for copy in self.over(c):
            copy.wait()
        home = self.spot.y
        return (
            self.part[home, self.spot.c, :, at].astype(F32)
            + self.arrive[home, :, at].astype(F32)
            + self.come[:, at].astype(F32)
        )

    def take_stats(self, c):
        at = lanes(c)
        return (self.stats[2, :, at] + self.stats[3, :, at]) * (1.0 / D)


class Spread:
    def __init__(self, spot, full, sems):
        self.spot, self.full, self.sems = spot, full, sems

    def piece(self, j, c, kind, device):
        part = self.full.at[feat(j), lanes(c)]
        return remote(part, part, self.sems.at[2 * kind, c], self.sems.at[2 * kind + 1, c], device)

    def to_y(self, c):
        return self.piece(self.spot.mp, c, 0, self.spot.yp)

    def to_sib(self, c):
        return self.piece(self.spot.mp, c, 1, self.spot.sib)

    def onward(self, c):
        return self.piece(self.spot.yp_mp, c, 2, self.spot.sib)

    def send(self, c):
        self.to_y(c).start()
        self.to_sib(c).start()

    def relay(self, c):
        self.to_y(c).wait()
        self.onward(c).start()

    def arrived(self, c):
        self.to_sib(c).wait()
        self.onward(c).wait()


def sin_cos(angle):
    turns = jnp.floor(angle * 0.6366197723675814 + 0.5)
    rest = angle - turns * 1.5703125
    rest = rest - turns * 4.837512969970703e-4
    rest = rest - turns * 7.549789948768648e-8
    square = rest * rest
    sine = rest + rest * square * (
        -1.6666654611e-1 + square * (8.3321608736e-3 + square * -1.9515295891e-4)
    )
    cosine = (
        1.0
        - 0.5 * square
        + square
        * square
        * (4.166664568298827e-2 + square * (-1.388731625493765e-3 + square * 2.443315711809948e-5))
    )
    quarter = turns - 4.0 * jnp.floor(turns * 0.25)
    odd = (quarter == 1.0) | (quarter == 3.0)
    sine_sign = jnp.where(quarter >= 2.0, -1.0, 1.0)
    cosine_sign = jnp.where((quarter == 1.0) | (quarter == 2.0), -1.0, 1.0)
    return (
        jnp.where(odd, cosine, sine) * sine_sign,
        jnp.where(odd, sine, cosine) * cosine_sign,
    )


def phi_parts(value):
    scaled = jnp.clip(value * root_half, -3.832506856900711, 3.832506856900711)
    square = scaled * scaled
    top = 0.00022905065861350646
    for factor in (
        0.0034082910107109506,
        0.050955695062380861,
        0.18520832239976145,
        1.128379143519084,
    ):
        top = top * square + factor
    low = -1.1791602954361697e-7
    for factor in (
        0.000023547966471313185,
        0.0010179625278914885,
        0.014070470171167667,
        0.11098505178285362,
        0.49746925110067538,
        1.0,
    ):
        low = low * square + factor
    error = scaled * top / low
    return (0.5 + 0.5 * error, inv_root_two_pi * jnp.exp(-0.5 * value * value))


def normalize(values):
    mean = jnp.mean(values, axis=0, keepdims=True)
    square = jnp.mean(values * values, axis=0, keepdims=True)
    inverse = lax.rsqrt(square - mean * mean + norm_eps)
    return ((values - mean) * inverse, mean, inverse)


def turn_by(values, cosine, sine):
    out = []
    for h in range(3):
        front, rear = values[64 * h : 64 * h + 32], values[64 * h + 32 : 64 * h + 64]
        co, si = cosine[32 * h : 32 * h + 32], sine[32 * h : 32 * h + 32]
        out += [front * co - rear * si, front * si + rear * co]
    return jnp.concatenate(out, axis=0)


def block_diagonal(tile):
    zero = jnp.zeros((64, TILE), tile.dtype)
    parts = []
    for h in range(3):
        column = [zero, zero, zero]
        column[h] = tile[64 * h : 64 * h + 64]
        parts.append(jnp.concatenate(column, axis=0))
    return jnp.concatenate(parts, axis=1)


def from_diagonal(values, heads):
    return jnp.concatenate(
        [values[64 * h : 64 * h + 64, TILE * n : TILE * n + TILE] for n, h in enumerate(heads)], axis=0
    )


def fold(values):
    return values[:, :128] + values[:, 128:]


def angle_tables(r):
    def block(c, carry):
        at = lanes(c)
        angle = r.cols[0:96, 2:3] * r.info[0:1, at] + r.cols[0:96, 3:4] * r.info[1:2, at]
        sine, cosine = sin_cos(angle)
        r.cos[:, at] = cosine
        r.sin[:, at] = sine
        return carry

    lax.fori_loop(0, CHUNKS, block, 0)

    def column(t, carry):
        row = r.info[3:4, tile_lanes(t)]
        r.kcol[pl.ds(pl.multiple_of(t * TILE, TILE), TILE), :] = jnp.transpose(
            jnp.broadcast_to(row, (TILE, TILE))
        )
        return carry

    lax.fori_loop(0, TILES, column, 0)


def flip(source, goal):
    for i in range(source.shape[1] // 128):
        part = source[:, 128 * i : 128 * i + 128].astype(F32)
        goal[128 * i : 128 * i + 128, 0 : source.shape[0]] = jnp.transpose(part).astype(BF16)


def project(r, c):
    at = lanes(c)
    normed, _, _ = normalize(r.x[:, at].astype(F32))
    h1 = (normed * r.small[:, 4:5] + r.small[:, 5:6]).astype(BF16)
    r.h1[:, at] = h1
    projected = dot(r.wqkv[...], h1) + r.cols[0:576, 1:2]
    cosine, sine = r.cos[:, at], r.sin[:, at]
    query = turn_by(projected[0:192], cosine, sine)
    key = turn_by(projected[192:384], cosine, sine)
    value = projected[384:576]
    r.qk[0:192, at] = query.astype(BF16)
    r.qk[192:384, at] = key.astype(BF16)
    r.v[:, at] = value.astype(BF16)
    r.kn[at, :] = jnp.transpose(key).astype(BF16)
    r.vn[at, :] = jnp.transpose(value).astype(BF16)


def tile_mask(r, tile, start, width):
    window = pl.ds(pl.multiple_of(start, 16), width)
    allowed = r.kcol[window, :] == r.info[4:5, tile_lanes(tile)]
    return jnp.where(allowed, 0.0, -1e30)


def repeat(mask, values):
    return jnp.concatenate([mask] * (values.shape[1] // TILE), axis=1)


def head_groups(width):
    return [(0, 1, 2)] if width <= NARROW else [(0,), (1,), (2,)]


def attend_tile(r, spot, tile, start, width, values):
    window = pl.ds(pl.multiple_of(start, 16), width)
    at = tile_lanes(tile)
    queries = block_diagonal(r.qk[0:192, at] * BF16(0.125))
    mask = tile_mask(r, tile, start, width)
    for heads in head_groups(width):
        span = slice(TILE * heads[0], TILE * heads[-1] + TILE)
        scores = dot(r.kn[window, :], queries[:, span])
        scores = scores + repeat(mask, scores)
        top = jnp.max(scores, axis=0, keepdims=True)
        exponent = jnp.exp(scores - top)
        total = jnp.sum(exponent, axis=0, keepdims=True)
        probs = (exponent * (1.0 / total)).astype(BF16)
        out = from_diagonal(dot(values, probs), heads).astype(BF16)
        r.att[head_rows(spot, heads), at] = out
        r.lse[tile, :, span] = jnp.broadcast_to(top + jnp.log(total), (8, span.stop - span.start))


def head_rows(spot, heads):
    return pl.ds(pl.multiple_of(OWN * spot.mp + 64 * heads[0], 16), 64 * len(heads))


def back_tile(r, spot, tile, start, width, keys):
    window = pl.ds(pl.multiple_of(start, 16), width)
    at = tile_lanes(tile)
    queries = block_diagonal(r.qk[0:192, at] * BF16(0.125))
    grads = block_diagonal(dot(r.wout[...], r.gatt[:, at]).astype(BF16))
    mask = tile_mask(r, tile, start, width)
    for heads in head_groups(width):
        span = slice(TILE * heads[0], TILE * heads[-1] + TILE)
        query, grad = queries[:, span], grads[:, span]
        scores = dot(r.kn[window, :], query)
        probs = jnp.exp(scores + repeat(mask, scores) - r.lse[tile, 0:1, span])
        g_probs = dot(r.vn[window, :], grad)
        center = jnp.sum(probs * g_probs, axis=0, keepdims=True)
        g_scores = (probs * (g_probs - center)).astype(BF16)
        r.dv[window, :] += dot(probs.astype(BF16), grad, NT)
        r.dk[window, :] += dot(g_scores, query, NT)
        rows = slice(64 * heads[0], 64 * heads[-1] + 64)
        r.dq[rows, at] = (from_diagonal(dot(keys, g_scores), heads) * 0.125).astype(BF16)


def mlp_part(r, spot, c, outward, sums):
    at = lanes(c)
    mid = r.x[:, at].astype(F32) + (dot(r.wot[...], r.att[:, at]) + r.small[:, 8:9])
    normed, mean, inverse = normalize(mid)
    r.work[...] = mid
    r.mido[:, at] = r.work[feat(spot.mp), :]
    r.rows2[0:1, at] = mean
    r.rows2[1:2, at] = inverse
    h2 = (normed * r.small[:, 6:7] + r.small[:, 7:8]).astype(BF16)
    r.h2[:, at] = h2
    hidden = dot(r.wupt[...], h2) + r.cols[:, 0:1]
    lower, density = phi_parts(hidden)
    active = (hidden * lower).astype(BF16)
    r.act[:, at] = active
    slope = lower + hidden * density
    outward.give(c, dot(r.wdnt[...], active))
    g_pre = (dot(r.wdn[...], r.gout[:, at]) * slope).astype(BF16)
    r.gpre[:, at] = g_pre
    r.sbup[...] += fold(g_pre.astype(F32))
    g_h2 = dot(r.wup[...], g_pre)
    scaled = g_h2 * r.small[:, 6:7]
    r.stats[0, 0:1, at] = jnp.sum(scaled, axis=0, keepdims=True)
    r.stats[0, 1:2, at] = jnp.sum(scaled * normed, axis=0, keepdims=True)
    sums.give(c, g_h2)


def second_norm_back(r, spot, c, sums):
    at = lanes(c)
    grad = sums.take(c)
    means = sums.take_stats(c)
    normed = (r.mido[:, at] - r.rows2[0:1, at]) * r.rows2[1:2, at]
    r.sg2[...] += fold(grad * normed)
    r.sb2[...] += fold(grad)
    back = r.rows2[1:2, at] * (
        grad * r.cols[0:192, 6:7] - means[0:1, :] - normed * means[1:2, :]
    )
    g_att = (r.gout[feat(spot.mp), at].astype(F32) + back).astype(BF16)
    r.gatt[feat(spot.mp), at] = g_att
    r.sbo[...] += fold(g_att.astype(F32))


def unrotate(r, c):
    at = lanes(c)
    cosine, sine = r.cos[:, at], r.sin[:, at]
    g_query = r.dq[0:192, at].astype(F32)
    g_key = jnp.transpose(r.dk[at, :]).astype(BF16).astype(F32)
    g_value = jnp.transpose(r.dv[at, :]).astype(BF16)
    plain = [turn_by(g, cosine, -sine).astype(BF16) for g in (g_query, g_key)]
    r.gproj[0:576, at] = jnp.concatenate(plain + [g_value], axis=0)
    angle = []
    for h in range(3):
        total = 0.0
        for part, g in enumerate((g_query, g_key)):
            rotated = r.qk[192 * part : 192 * part + 192, at].astype(F32)
            a, b = slice(64 * h, 64 * h + 32), slice(64 * h + 32, 64 * h + 64)
            total = total + (g[b] * rotated[a] - g[a] * rotated[b])
        angle.append(total)
    angle = jnp.concatenate(angle, axis=0)
    r.sf0[...] += fold(angle * r.info[0:1, at])
    r.sf1[...] += fold(angle * r.info[1:2, at])


def first_part(r, spot, c, sums):
    at = lanes(c)
    g_h1 = dot(r.wqkvn[:, 0:576], r.gproj[0:576, at])
    normed, mean, inverse = normalize(r.x[:, at].astype(F32))
    r.rows2[0:1, at] = mean
    r.rows2[1:2, at] = inverse
    scaled = g_h1 * r.small[:, 4:5]
    r.stats[0, 0:1, at] = jnp.sum(scaled, axis=0, keepdims=True)
    r.stats[0, 1:2, at] = jnp.sum(scaled * normed, axis=0, keepdims=True)
    sums.give(c, g_h1)


def first_norm_back(r, spot, c, sums):
    at = lanes(c)
    grad = sums.take(c)
    means = sums.take_stats(c)
    own = feat(spot.mp)
    normed = (r.x[own, at].astype(F32) - r.rows2[0:1, at]) * r.rows2[1:2, at]
    r.sg1[...] += fold(grad * normed)
    r.sb1[...] += fold(grad)
    back = r.rows2[1:2, at] * (
        grad * r.cols[0:192, 4:5] - means[0:1, :] - normed * means[1:2, :]
    )
    r.mido[:, at] = r.gatt[own, at].astype(F32) + back


def kernel(r, spot):
    peers = [dp_partner(spot, bit) for bit in range(r.dp_bits)]
    token_load = pltpu.make_async_copy(r.tok, r.out, r.load_sem.at[4])
    token_load.start()
    loads = Refs()
    for n, (name, source) in enumerate(
        dict(wqkv=r.in_wqkv, wup=r.in_wup, wdn=r.in_wdn, wout=r.in_wout).items()
    ):
        setattr(loads, name, pltpu.make_async_copy(source, getattr(r, name), r.load_sem.at[n]))
        getattr(loads, name).start()
    greet([spot.sib, spot.yp] + peers)
    own = feat(spot.mp)
    r.x[own, ROWS - 64 : LANES] = jnp.zeros((OWN, 128), BF16)
    token_load.wait()
    r.x[own, 0:ROWS] = r.out[...]
    pltpu.make_async_copy(r.cot, r.out, r.load_sem.at[5]).start()
    tokens = Spread(spot, r.x, r.tk_sem)
    for c in range(CHUNKS):
        tokens.send(c)
    r.small[own, :] = r.cols[0:192, :]
    small_y = remote(r.cols.at[0:192], r.small.at[own], r.sm_sem.at[0], r.sm_sem.at[1], spot.yp)
    small_c = remote(r.cols.at[0:192], r.small.at[own], r.sm_sem.at[2], r.sm_sem.at[3], spot.sib)
    there = r.small.at[feat(spot.yp_mp)]
    small_f = remote(there, there, r.sm_sem.at[4], r.sm_sem.at[5], spot.sib)
    small_y.start()
    small_c.start()

    def count_copy(bit):
        return remote(r.cnts.at[bit], r.cntr.at[bit], r.cn_sem.at[0, bit], r.cn_sem.at[1, bit], peers[bit])

    r.cnts[0] = r.cnt[...]
    count_copy(0).start()
    angle_tables(r)
    small_y.wait()
    small_f.start()
    for ref in (r.sbup, r.sg1, r.sb1, r.sg2, r.sb2, r.sbo, r.sf0, r.sf1, r.dk, r.dv):
        ref[...] = jnp.zeros_like(ref)
    loads.wup.wait()
    flip(r.wup, r.wupt)
    small_c.wait()
    small_f.wait()
    loads.wdn.wait()
    flip(r.wdn, r.wdnt)
    for bit in range(r.dp_bits):
        count_copy(bit).wait()
        total = r.cnts[bit] + r.cntr[bit]
        if bit + 1 < r.dp_bits:
            r.cnts[bit + 1] = total
            count_copy(bit + 1).start()
    low, high = total[:, 0:1], total[:, 1:2]
    share = jnp.where(r.cnt[:, 2:3] > 0.5, low, high) / (low + high)
    r.share[...] = jnp.broadcast_to(share, (8, 128))
    loads.wqkv.wait()
    loads.wout.wait()

    tokens.relay(0)

    def project_chunk(c, carry):
        @pl.when(c + 1 < CHUNKS)
        def _():
            tokens.relay(c + 1)

        tokens.arrived(c)
        project(r, c)
        return carry

    lax.fori_loop(0, CHUNKS, project_chunk, 0)

    wo_here = r.wof.at[own]
    wo_there = r.wof.at[feat(spot.yp_mp)]
    wo_y = remote(r.wout, wo_here, r.wo_sem.at[0], r.wo_sem.at[1], spot.yp)
    wo_c = remote(r.wout, wo_here, r.wo_sem.at[2], r.wo_sem.at[3], spot.sib)
    wo_f = remote(wo_there, wo_there, r.wo_sem.at[4], r.wo_sem.at[5], spot.sib)
    wo_y.start()
    wo_c.start()
    r.wof[own, :] = r.wout[...]
    r.gout[own, ROWS - 64 : LANES] = jnp.zeros((OWN, 128), BF16)
    keep = r.info[2:3, 0:ROWS]
    pltpu.make_async_copy(r.cot, r.out, r.load_sem.at[5]).wait()
    r.gout[own, 0:ROWS] = (r.out[...].astype(F32) * keep).astype(BF16)
    attended = Spread(spot, r.att, r.at_sem)
    cotangents = Spread(spot, r.gout, r.ct_sem)

    def after_tile(t):
        @pl.when(t % 2 == 1)
        def _():
            attended.send(t // 2)
            cotangents.send(t // 2)

            @pl.when(t >= 5)
            def _():
                attended.relay(t // 2 - 2)
                cotangents.relay(t // 2 - 2)

    for j in range(3):
        start = 576 * j - 32 * (j // 2)
        r.win[:, 0:NARROW] = r.v[:, start : start + NARROW]

        def attend(i, carry):
            attend_tile(r, spot, 5 * j + i, start, NARROW, r.win[:, 0:NARROW])
            after_tile(5 * j + i)
            return carry

        lax.fori_loop(0, 4, attend, 0)
        if j == 0:
            attend_tile(r, spot, 4, 0, 1152, r.v[:, 0:1152])
            after_tile(4)
        if j == 1:
            attend_tile(r, spot, 9, 976, 752, r.v[:, 976:1728])
            after_tile(9)
    wo_y.wait()
    wo_f.start()
    wo_c.wait()
    wo_f.wait()
    flip(r.wof, r.wot)
    r.atto[...] = r.att[own, :]

    outward = Exchange(r, spot, r.mp, r.mr, r.ms, r.mc, r.mo_sem)
    second = Exchange(r, spot, r.gp, r.gr, r.gs, r.gc, r.g2_sem, r.stats)
    g_att = Spread(spot, r.gatt, r.ga_sem)
    order = list(range(r.dp_bits))
    turned = order[1:] + order[:1]
    down = Reduce(spot, r.accdn, r.ardn, r.resdn, order, r.dn_sem.at[0], r.dn_sem.at[1])
    up = Reduce(spot, r.accup, r.arup, r.resup, turned, r.up_sem.at[0], r.up_sem.at[1])
    out = Reduce(spot, r.accwo, r.arwo, r.reswo, order, r.wr_sem.at[0], r.wr_sem.at[1])
    share = r.share[0:1, 0:1]

    def mlp_step(n, carry):
        @pl.when(n < CHUNKS)
        def _():
            @pl.when(n >= CHUNKS - 2)
            def _():
                attended.relay(n)
                cotangents.relay(n)

            attended.arrived(n)
            cotangents.arrived(n)
            mlp_part(r, spot, n, outward, second)

        @pl.when(n == CHUNKS)
        def _():
            r.accdn[...] = (dot(r.act[...], r.gout[...], NT) * r.share[0:1, 0:1]).astype(BF16)
            down.start()

        @pl.when(n == CHUNKS + 1)
        def _():
            r.accup[...] = (dot(r.h2[...], r.gpre[...], NT) * r.share[0:1, 0:1]).astype(BF16)
            up.start()

        @pl.when((n >= 1) & (n <= CHUNKS))
        def _():
            second.pass_on(n - 1)

        @pl.when((n >= 3) & (n <= CHUNKS + 2))
        def _():
            second_norm_back(r, spot, n - 3, second)
            g_att.send(n - 3)

        @pl.when(n >= 4)
        def _():
            g_att.relay(n - 4)

        return carry

    lax.fori_loop(0, CHUNKS + 4, mlp_step, 0)

    for c in range(CHUNKS):
        outward.pass_on(c)

    def before_tile(t):
        @pl.when(t % 2 == 0)
        def _():
            g_att.arrived(t // 2)

    for j in range(3):
        start = 576 * j - 32 * (j // 2)
        r.win[:, 0:NARROW] = r.qk[192:384, start : start + NARROW]

        def back(i, carry):
            before_tile(5 * j + i)
            back_tile(r, spot, 5 * j + i, start, NARROW, r.win[:, 0:NARROW])
            return carry

        lax.fori_loop(0, 4, back, 0)
        if j == 0:
            before_tile(4)
            back_tile(r, spot, 4, 0, 1152, r.qk[192:384, 0:1152])
        if j == 1:
            back_tile(r, spot, 9, 976, 752, r.qk[192:384, 976:1728])
        down.advance()
        up.advance()
        if j == 1:
            finish_out(r, spot, outward)
            down.advance()
    r.accwo[...] = (dot(r.atto[...], r.gatt[...], NT) * r.share[0:1, 0:1]).astype(BF16)
    out.start()
    lax.fori_loop(0, CHUNKS, lambda c, carry: (unrotate(r, c), carry)[1], 0)
    down.advance()
    up.advance()
    r.accqk[...] = (dot(r.gproj[0:384, :], r.h1[...], NT) * r.share[0:1, 0:1]).astype(BF16)
    r.accv[...] = (dot(r.gproj[384:576, :], r.h1[...], NT) * r.share[0:1, 0:1]).astype(BF16)
    pair = Reduce(spot, r.accqk, r.arqk, r.resqk, order, r.qr_sem.at[0], r.qr_sem.at[1])
    value = Reduce(spot, r.accv, r.arv, r.resv, turned, r.vr_sem.at[0], r.vr_sem.at[1])
    pair.start()
    value.start()
    out.advance()
    flip(r.wqkv, r.wqkvn)
    first = Exchange(r, spot, r.gp, r.gr, r.gs, r.gc, r.g1_sem, r.stats)

    def last_step(n, carry):
        @pl.when(n < CHUNKS)
        def _():
            first_part(r, spot, n, first)

        @pl.when((n >= 1) & (n <= CHUNKS))
        def _():
            first.pass_on(n - 1)

        @pl.when(n >= 3)
        def _():
            first_norm_back(r, spot, n - 3, first)

        @pl.when(n == 3)
        def _():
            pair.advance()
            value.advance()
            out.advance()

        @pl.when(n == 5)
        def _():
            down.advance()
            up.advance()

        @pl.when(n == 7)
        def _():
            pair.advance()
            value.advance()
            out.advance()

        return carry

    lax.fori_loop(0, CHUNKS + 3, last_step, 0)

    def total(ref):
        return jnp.sum(ref[...], axis=1, keepdims=True)

    b_down = jnp.sum(r.gout[own, :].astype(F32), axis=1, keepdims=True)
    b_qkv = jnp.sum(r.gproj[0:576, :].astype(F32), axis=1, keepdims=True)
    columns = [
        total(r.sbup),
        jnp.concatenate([b_qkv, total(r.sf0), total(r.sf1)], axis=0),
        jnp.concatenate([total(r.sbo), total(r.sg1), total(r.sb1), total(r.sg2)], axis=0),
        jnp.concatenate([total(r.sb2), b_down, jnp.zeros((384, 1), F32)], axis=0),
    ]
    lane = lax.broadcasted_iota(jnp.int32, (D, 128), 1)
    table = jnp.zeros((D, 128), F32)
    for n, column in enumerate(columns):
        table = jnp.where(lane == n, column, table)
    table = jnp.transpose(table * r.share[0:1, 0:1])[0:8, :]
    for bit in range(r.dp_bits):
        r.sumx[bit] = table
        copy = remote(
            r.sumx.at[bit], r.sumr.at[bit], r.su_sem.at[0, bit], r.su_sem.at[1, bit], peers[bit]
        )
        copy.start()
        pair.advance()
        value.advance()
        out.advance()
        copy.wait()
        table = table + r.sumr[bit]
    r.sums[...] = table
    reduces = (pair, value, out, down, up)
    while any(reduce.at < len(reduce.phases) for reduce in reduces):
        for reduce in reduces:
            reduce.advance()


def finish_out(r, spot, outward):
    for c in range(CHUNKS):
        at = lanes(c)
        total = outward.take(c)
        whole = r.mido[:, at] + (total + r.cols[0:192, 9:10])
        r.gs[:, at] = (r.info[2:3, at] * whole).astype(BF16)
    r.out[...] = r.gs[:, 0:ROWS]


def dma(*shape):
    return pltpu.SemaphoreType.DMA(shape)


def run(dp_bits, **arrays):
    on_demand = ("tok", "cot", "in_wqkv", "in_wup", "in_wdn", "in_wout")
    outs = dict(
        out=((OWN, ROWS), BF16),
        igrad=((OWN, LANES), F32),
        resdn=((D, D), BF16),
        resup=((D, D), BF16),
        reswo=((OWN, D), BF16),
        resqk=((384, D), BF16),
        resv=((OWN, D), BF16),
        sums=((8, D), F32),
    )

    def levels(rows):
        return [VM(shape, BF16) for shape in arrive_shapes(rows, D, dp_bits)]

    full = VM((D, LANES), BF16)
    own = VM((OWN, LANES), BF16)
    square = VM((D, D), BF16)
    spread = dma(6, CHUNKS)
    reduce = dma(2, 2 * dp_bits)
    scratch = dict(
        x=full,
        h1=full,
        qk=VM((384, LANES), BF16),
        v=own,
        kn=VM((LANES, OWN), BF16),
        vn=VM((LANES, OWN), BF16),
        cos=VM((96, LANES), F32),
        sin=VM((96, LANES), F32),
        kcol=VM((LANES, TILE), F32),
        win=VM((OWN, 640), BF16),
        lse=VM((TILES, 8, 384), F32),
        small=VM((D, 128), F32),
        share=VM((8, 128), F32),
        att=full,
        gout=full,
        wqkv=VM((576, D), BF16),
        wup=square,
        wupt=square,
        wdn=square,
        wdnt=square,
        wout=VM((OWN, D), BF16),
        wof=square,
        wot=square,
        h2=full,
        act=full,
        gpre=full,
        work=VM((D, CHUNK), F32),
        rows2=VM((8, LANES), F32),
        stats=VM((4, 8, LANES), F32),
        mp=VM((2, 2, OWN, LANES), BF16),
        mr=VM((2, OWN, LANES), BF16),
        gp=VM((2, 2, OWN, LANES), BF16),
        gr=VM((2, OWN, LANES), BF16),
        gs=own,
        gc=own,
        dk=VM((LANES, OWN), F32),
        dv=VM((LANES, OWN), F32),
        ardn=levels(D),
        arup=levels(D),
        arwo=levels(OWN),
        arqk=levels(384),
        arv=levels(OWN),
        sbup=VM((D, 128), F32),
        sg1=VM((OWN, 128), F32),
        sb1=VM((OWN, 128), F32),
        sg2=VM((OWN, 128), F32),
        sb2=VM((OWN, 128), F32),
        sbo=VM((OWN, 128), F32),
        sf0=VM((96, 128), F32),
        sf1=VM((96, 128), F32),
        cnts=VM((dp_bits, 8, 128), F32),
        cntr=VM((dp_bits, 8, 128), F32),
        sumx=VM((dp_bits, 8, D), F32),
        sumr=VM((dp_bits, 8, D), F32),
        load_sem=dma(6),
        tk_sem=spread,
        at_sem=spread,
        ct_sem=spread,
        ga_sem=spread,
        sm_sem=dma(6),
        wo_sem=dma(6),
        cn_sem=dma(2, dp_bits),
        su_sem=dma(2, dp_bits),
        mo_sem=dma(8, CHUNKS),
        g2_sem=dma(8, CHUNKS),
        g1_sem=dma(8, CHUNKS),
        dn_sem=reduce,
        up_sem=reduce,
        wr_sem=reduce,
        qr_sem=reduce,
        vr_sem=reduce,
    )
    shapes, structure = jax.tree.flatten(scratch, is_leaf=lambda leaf: not isinstance(leaf, (dict, list)))

    def body(*refs):
        r = Refs()
        for name, ref in zip(list(arrays) + list(outs), refs):
            setattr(r, name, ref)
        named = jax.tree.unflatten(structure, refs[len(arrays) + len(outs) :])
        for name, ref in named.items():
            setattr(r, name, ref)
        r.mido, r.gatt, r.atto = r.igrad, r.att, r.v
        r.dq, r.gproj, r.ms = r.act, r.h2, r.act.at[OWN : 2 * OWN]
        r.mc = r.act.at[2 * OWN : 3 * OWN]
        r.accdn, r.accup, r.accwo = r.wof, r.wupt, r.wdn.at[0:OWN]
        r.wqkvn = r.wot
        r.accqk, r.accv = r.wdnt.at[0:384], r.wdnt.at[384:576]
        r.dp_bits = dp_bits
        kernel(r, place())

    results = pl.pallas_call(
        body,
        out_shape=[jax.ShapeDtypeStruct(shape, dtype) for shape, dtype in outs.values()],
        in_specs=[
            pl.BlockSpec(memory_space=pl.ANY if name in on_demand else VM) for name in arrays
        ],
        out_specs=[pl.BlockSpec(memory_space=VM) for _ in outs],
        scratch_shapes=shapes,
        compiler_params=pltpu.CompilerParams(
            collective_id=1, has_side_effects=True, vmem_limit_bytes=64 * MIB - 65536
        ),
    )(*arrays.values())
    named = Refs()
    for name, result in zip(outs, results, strict=True):
        setattr(named, name, result)
    return named


def local(
    tokens,
    w_qkv,
    b_qkv,
    freqs,
    w_out,
    b_out,
    norm1_gain,
    norm1_bias,
    norm2_gain,
    norm2_bias,
    w_up,
    b_up,
    w_down,
    b_down,
    cotangent,
    keep_mask,
    coords,
    block_group,
):
    row_count, width_loc = tokens.shape
    heads_loc = freqs.shape[1]
    keep = keep_mask.astype(F32)
    group_now = block_group[0]
    low = (group_now == 0).astype(F32)
    kept_total = jnp.sum(keep)
    segment_size = jnp.where(group_now == 0, GRID_LO * GRID_LO, SLOTS).astype(jnp.int32)
    segment = (jnp.arange(row_count, dtype=jnp.int32) // segment_size).astype(F32)
    key_segment = jnp.where(keep_mask > 0, segment, -1.0)
    info = jnp.stack(
        [coords[0].astype(F32), coords[1].astype(F32), keep, key_segment, segment] + [keep] * 3
    )
    info = jnp.pad(info, ((0, 0), (0, LANES - row_count)))
    small = jnp.stack(
        [part.astype(F32) for part in (norm1_gain, norm1_bias, norm2_gain, norm2_bias, b_out, b_down)],
        axis=1,
    )
    cols = jnp.concatenate(
        [
            b_up.astype(F32)[:, None],
            jnp.pad(b_qkv.reshape(-1, 1).astype(F32), ((0, D - 3 * width_loc), (0, 0))),
            jnp.pad(freqs.reshape(2, 96).T, ((0, D - 96), (0, 0))),
            jnp.pad(small, ((0, D - width_loc), (0, 0))),
        ],
        axis=1,
    )
    counts = jnp.stack([kept_total * low, kept_total * (1.0 - low), low])

    def wide(array):
        return jnp.pad(array, ((0, 0), (0, 128 - array.shape[1])))

    a = run(
        lax.axis_size("dp").bit_length() - 1,
        tok=tokens.T,
        cot=cotangent.T,
        cols=wide(cols),
        info=info,
        cnt=wide(jnp.broadcast_to(counts, (8, 3))),
        in_wqkv=w_qkv.transpose(1, 2, 0).reshape(3 * width_loc, D),
        in_wup=w_up,
        in_wdn=w_down,
        in_wout=w_out,
    )
    sums = a.sums
    grad_qkv = jnp.concatenate([a.resqk, a.resv], axis=0).astype(F32)
    half = (2, heads_loc, HEAD_DIM // 2)
    return (
        a.out.T,
        a.igrad[:, :row_count].T,
        grad_qkv.reshape(3, width_loc, D).transpose(2, 0, 1),
        sums[1, : 3 * width_loc].reshape(3, width_loc),
        sums[1, 3 * width_loc :].reshape(half),
        a.reswo.astype(F32),
        sums[2, 0:192],
        sums[2, 192:384],
        sums[2, 384:576],
        sums[2, 576:768],
        sums[3, 0:192],
        a.resup.astype(F32),
        sums[0],
        a.resdn.astype(F32),
        sums[3, 192:384],
    )


def solution(mesh):
    return jax.shard_map(
        local,
        mesh=mesh,
        in_specs=(
            P("dp", "mp"),
            P(None, None, "mp"),
            P(None, "mp"),
            P(None, "mp", None),
            P("mp", None),
            P("mp"),
            P("mp"),
            P("mp"),
            P("mp"),
            P("mp"),
            P(None, "mp"),
            P("mp"),
            P("mp", None),
            P("mp"),
            P("dp", "mp"),
            P("dp"),
            P(None, "dp"),
            P("dp"),
        ),
        out_specs=(
            P("dp", "mp"),
            P("dp", "mp"),
            P(None, None, "mp"),
            P(None, "mp"),
            P(None, "mp", None),
            P("mp", None),
            P("mp"),
            P("mp"),
            P("mp"),
            P("mp"),
            P("mp"),
            P(None, "mp"),
            P("mp"),
            P("mp", None),
            P("mp"),
        ),
        check_vma=False,
    )
```

time: 878 us -> 254 us (0.29)
  waiting for transfers between devices: 440 us -> 0 us
  Pallas kernels: 0 us -> 227 us
  matrix products: 168 us -> 0 us
  other arithmetic: 105 us -> 10.3 us
  blocking collectives: 75.6 us -> 0 us
  local copies, waits for them, and re-layouts: 60.4 us -> 13.6 us
  between operations: 20.6 us -> 2.65 us
    psum x4 -> x0, waiting for transfers between devices: 433 us -> none  [the longest x1 188 us: local(): lax.psum((own_weight * grad_w_qkv, own_weight * grad_b_qkv, own_weight *...]
    pallas_call x0 -> x1, Pallas kernels: none -> 227 us  [run(): pl.pallas_call(body, out_shape=[jax.ShapeDtypeStruct(shape, dtype) for sh...]
    dot_general x31 -> x0, matrix products: 161 us -> none  [the longest x6 33.8 us: masked_scores(): jnp.einsum('qhd,khd->hqk', query_blk, key_all, preferred_element_type=jnp...]
    psum x2 -> x0, blocking collectives: 61.7 us -> none  [the longest x1 39.9 us: local(): lax.psum((own_weight * grad_w_qkv, own_weight * grad_b_qkv, own_weight *...]
    reduce_sum x12 -> x1, other arithmetic: 52.7 us -> 1.5 us  [local(): kept_total = jnp.sum(keep)]
    unnamed x135 -> x15, local copies, waits for them, and re-layouts: 28.1 us -> 2.56 us
    convert_element_type x16 -> x5, other arithmetic: 24.8 us -> 6.09 us  [the longest x1 1.58 us: local(): a.resup.astype(F32)]
    unnamed x1 -> x0, blocking collectives: 13.9 us -> none
  transfers between devices with their start and end apart: 7 -> 0, of which waited for: 5 -> 0; matrix products, arithmetic and copies ran while one was open for 33% -> 0% of each run, Pallas kernels for 0% -> 0%
where the time goes in v3:
time: 254 us
  Pallas kernels  227 us (89%)
  local copies, waits for them, and re-layouts  13.6 us (5%)
  other arithmetic  10.3 us (4%)
  between operations  2.65 us (1%)
    pallas_call x1, Pallas kernels, run(): pl.pallas_call(body, out_shape=[jax.ShapeDtypeStruct(shape, dtype) for sh...  227 us

profile of v3, /device:TPU:0, one launch (start us, length us, event | category | flops | bytes accessed | tf_op | source)
XLA Modules:
  0.0 253.6 jit_solution(7614170470683465731)
XLA Ops:
  1.3 1.4 slice_convert_fusion
  2.7 1.5 convert_reduce_fusion
  4.2 0.7 convert_element_type.74
  4.9 0.1 stack.64
  5.0 0.6 pad.38.refs_3_
  6.9 0.1 select_maximum_fusion.1
  7.0 0.6 pad.40.refs_4_
  7.6 0.7 stack.55
  8.3 0.7 stack.56
  8.9 0.7 stack.57
  9.6 0.7 stack.58
  10.2 0.7 stack.59
  10.9 0.7 stack.60
  11.6 0.8 convert_element_type.71
  12.4 0.7 copy.48
  13.0 0.1 reshape.94
  13.1 0.7 reshape.96
  13.8 0.2 copy.49
  14.0 0.8 pad.37.refs_2_
  14.8 227.1 %shard_map.289 = (bf16[192,1728]{1,0:T(8,128)(2,1)}, f32[192,1792]{1,0:T(8,128)}, bf16[768,768]{1,0:T(8,128)(2,1)}, bf16[768,768]{1,0:T(8,128)(2,1)}, bf16[192,7...) custom-call(bf16[192,1728]{1,0:T(8,128)(2,1)} %bitcast.25, ...), custom_call_target="tpu_custom_call" | custom-call | tf_op jit(solution)/shard_map/pallas_call | solution.py:968
  241.9 1.2 pad_maximum_fusion
  243.2 0.0 copy-start.5
  243.2 0.0 copy-start.2
  243.2 1.4 convert_bitcast_fusion
  244.5 0.0 copy-done.5
  244.5 0.7 fusion.6
  245.2 0.1 reshape_squeeze.7
  245.3 0.6 copy.50
  245.9 0.7 reshape_squeeze.6
  246.5 0.6 slice_reduce_fusion
  247.1 0.0 copy-done.2
  247.1 0.0 copy-start.1
  247.1 1.6 convert_element_type.80
  248.7 0.1 copy-done.1
  248.8 0.0 copy-start
  248.8 1.6 convert_element_type.81
  250.4 0.3 copy-done
  250.7 0.0 copy-start.4
  250.7 0.0 copy-start.3
  250.7 1.2 slice_bitcast_fusion
  251.9 0.0 copy-done.4
  251.9 0.9 convert_element_type.79
  252.8 0.0 copy-done.3
  252.8 0.8 copy.53
  (7 shorter events, 0.1 us)
Async XLA Ops:
  243.2 1.4 copy-start.5
  243.2 4.0 %copy-start.2 = (bf16[768,768]{1,0:T(8,128)(2,1)S(1)}, bf16[768,768]{1,0:T(8,128)(2,1)}, u32[]{:S(2)}) copy-start(bf16[768,768]{1,0:T(8,128)(2,1)} %get-tuple-element.29) | copy-start | bytes 3538948
  247.1 1.7 copy-start.1
  248.8 1.9 copy-start
  250.7 1.2 copy-start.4
  250.7 2.0 copy-start.3

commit v4 on v3

--- a/solution.py
+++ b/solution.py
@@ -84,8 +84,8 @@
 
 
 class Reduce:
-    def __init__(self, spot, acc, arrive, res, order, send, recv):
-        self.spot, self.res, self.send, self.recv = spot, res, send, recv
+    def __init__(self, spot, acc, arrive, res, order, sems):
+        self.spot, self.res, self.send, self.recv = spot, res, sems.at[0], sems.at[1]
         self.at = 0
         self.phases = []
         gathers = []
@@ -375,6 +375,32 @@
     return values[:, :128] + values[:, 128:]
 
 
+def row_tables(r):
+    pad = jnp.zeros((1, D - 3 * OWN), F32)
+    qkv = jnp.concatenate([r.bqkv[n : n + 1, :].astype(F32) for n in range(3)] + [pad], axis=1)
+    pad = jnp.zeros((2, D - 96), F32)
+    freqs = jnp.concatenate([r.freqs[h] for h in range(3)] + [pad], axis=1)
+    table = jnp.concatenate(
+        [r.pack[0:1, :], qkv, freqs, r.pack[1:8, :], jnp.zeros((117, D), F32)], axis=0
+    )
+    for i in range(D // 128):
+        r.cols[128 * i : 128 * i + 128, :] = jnp.transpose(table[:, 128 * i : 128 * i + 128])
+    low = 1.0 - r.group[0].astype(F32)
+    keep = r.keep[...].astype(F32)
+    middle = lax.broadcasted_iota(jnp.int32, (1, ROWS), 1).astype(F32) + 0.5
+    segment = low * jnp.floor(middle * (1.0 / (GRID_LO * GRID_LO))) + (1.0 - low) * jnp.floor(
+        middle * (1.0 / SLOTS)
+    )
+    r.info[...] = jnp.zeros_like(r.info)
+    r.info[0:2, 0:ROWS] = r.coords[...].astype(F32)
+    r.info[2:3, 0:ROWS] = keep
+    r.info[3:4, 0:ROWS] = keep * (segment + 1.0) - 1.0
+    r.info[4:5, 0:ROWS] = segment
+    kept = jnp.sum(keep, axis=1, keepdims=True)
+    lane = lax.broadcasted_iota(jnp.int32, (8, 128), 1)
+    r.cnt[...] = kept * jnp.where(lane == 0, low, jnp.where(lane == 1, 1.0 - low, 0.0))
+
+
 def angle_tables(r):
     def block(c, carry):
         at = lanes(c)
@@ -404,7 +430,9 @@
 
 def project(r, c):
     at = lanes(c)
-    normed, _, _ = normalize(r.x[:, at].astype(F32))
+    normed, mean, inverse = normalize(r.x[:, at].astype(F32))
+    r.rows1[0:1, at] = mean
+    r.rows1[1:2, at] = inverse
     h1 = (normed * r.small[:, 4:5] + r.small[:, 5:6]).astype(BF16)
     r.h1[:, at] = h1
     projected = dot(r.wqkv[...], h1) + r.cols[0:576, 1:2]
@@ -475,7 +503,7 @@
         r.dq[rows, at] = (from_diagonal(dot(keys, g_scores), heads) * 0.125).astype(BF16)
 
 
-def mlp_part(r, spot, c, outward, sums):
+def mlp_forward(r, spot, c, outward):
     at = lanes(c)
     mid = r.x[:, at].astype(F32) + (dot(r.wot[...], r.att[:, at]) + r.small[:, 8:9])
     normed, mean, inverse = normalize(mid)
@@ -489,16 +517,24 @@
     lower, density = phi_parts(hidden)
     active = (hidden * lower).astype(BF16)
     r.act[:, at] = active
-    slope = lower + hidden * density
+    r.gpre[:, at] = (lower + hidden * density).astype(BF16)
     outward.give(c, dot(r.wdnt[...], active))
-    g_pre = (dot(r.wdn[...], r.gout[:, at]) * slope).astype(BF16)
+
+
+def give_gradient(r, c, sums, grad, gain, bias, low):
+    at = lanes(c)
+    r.stats[0, 0:1, at] = jnp.sum(grad * gain, axis=0, keepdims=True)
+    r.stats[0, 1:2, at] = jnp.sum(grad * (low[:, at].astype(F32) - bias), axis=0, keepdims=True)
+    sums.give(c, grad)
+
+
+def mlp_backward(r, c, sums):
+    at = lanes(c)
+    g_act = dot(r.wdn[...], r.gout[:, at])
+    g_pre = (g_act * r.gpre[:, at].astype(F32)).astype(BF16)
     r.gpre[:, at] = g_pre
     r.sbup[...] += fold(g_pre.astype(F32))
-    g_h2 = dot(r.wup[...], g_pre)
-    scaled = g_h2 * r.small[:, 6:7]
-    r.stats[0, 0:1, at] = jnp.sum(scaled, axis=0, keepdims=True)
-    r.stats[0, 1:2, at] = jnp.sum(scaled * normed, axis=0, keepdims=True)
-    sums.give(c, g_h2)
+    give_gradient(r, c, sums, dot(r.wup[...], g_pre), r.small[:, 6:7], r.small[:, 7:8], r.h2)
 
 
 def second_norm_back(r, spot, c, sums):
@@ -537,16 +573,9 @@
     r.sf1[...] += fold(angle * r.info[1:2, at])
 
 
-def first_part(r, spot, c, sums):
-    at = lanes(c)
-    g_h1 = dot(r.wqkvn[:, 0:576], r.gproj[0:576, at])
-    normed, mean, inverse = normalize(r.x[:, at].astype(F32))
-    r.rows2[0:1, at] = mean
-    r.rows2[1:2, at] = inverse
-    scaled = g_h1 * r.small[:, 4:5]
-    r.stats[0, 0:1, at] = jnp.sum(scaled, axis=0, keepdims=True)
-    r.stats[0, 1:2, at] = jnp.sum(scaled * normed, axis=0, keepdims=True)
-    sums.give(c, g_h1)
+def first_part(r, c, sums):
+    grad = dot(r.wqkvn[:, 0:576], r.gproj[0:576, lanes(c)])
+    give_gradient(r, c, sums, grad, r.small[:, 4:5], r.small[:, 5:6], r.h1)
 
 
 def first_norm_back(r, spot, c, sums):
@@ -554,19 +583,20 @@
     grad = sums.take(c)
     means = sums.take_stats(c)
     own = feat(spot.mp)
-    normed = (r.x[own, at].astype(F32) - r.rows2[0:1, at]) * r.rows2[1:2, at]
+    normed = (r.x[own, at].astype(F32) - r.rows1[0:1, at]) * r.rows1[1:2, at]
     r.sg1[...] += fold(grad * normed)
     r.sb1[...] += fold(grad)
-    back = r.rows2[1:2, at] * (
+    back = r.rows1[1:2, at] * (
         grad * r.cols[0:192, 4:5] - means[0:1, :] - normed * means[1:2, :]
     )
-    r.mido[:, at] = r.gatt[own, at].astype(F32) + back
+    r.igrad[:, at] = r.gatt[own, at].astype(F32) + back
 
 
 def kernel(r, spot):
     peers = [dp_partner(spot, bit) for bit in range(r.dp_bits)]
     token_load = pltpu.make_async_copy(r.tok, r.out, r.load_sem.at[4])
     token_load.start()
+    cot_load = pltpu.make_async_copy(r.cot, r.out, r.load_sem.at[5])
     loads = Refs()
     for n, (name, source) in enumerate(
         dict(wqkv=r.in_wqkv, wup=r.in_wup, wdn=r.in_wdn, wout=r.in_wout).items()
@@ -578,24 +608,30 @@
     r.x[own, ROWS - 64 : LANES] = jnp.zeros((OWN, 128), BF16)
     token_load.wait()
     r.x[own, 0:ROWS] = r.out[...]
-    pltpu.make_async_copy(r.cot, r.out, r.load_sem.at[5]).start()
+    cot_load.start()
     tokens = Spread(spot, r.x, r.tk_sem)
     for c in range(CHUNKS):
         tokens.send(c)
+    row_tables(r)
     r.small[own, :] = r.cols[0:192, :]
-    small_y = remote(r.cols.at[0:192], r.small.at[own], r.sm_sem.at[0], r.sm_sem.at[1], spot.yp)
-    small_c = remote(r.cols.at[0:192], r.small.at[own], r.sm_sem.at[2], r.sm_sem.at[3], spot.sib)
-    there = r.small.at[feat(spot.yp_mp)]
+    here, there = r.small.at[own], r.small.at[feat(spot.yp_mp)]
+    small_y = remote(r.cols.at[0:192], here, r.sm_sem.at[0], r.sm_sem.at[1], spot.yp)
+    small_c = remote(r.cols.at[0:192], here, r.sm_sem.at[2], r.sm_sem.at[3], spot.sib)
     small_f = remote(there, there, r.sm_sem.at[4], r.sm_sem.at[5], spot.sib)
     small_y.start()
     small_c.start()
 
     def count_copy(bit):
-        return remote(r.cnts.at[bit], r.cntr.at[bit], r.cn_sem.at[0, bit], r.cn_sem.at[1, bit], peers[bit])
+        return remote(
+            r.cnts.at[bit], r.cntr.at[bit], r.cn_sem.at[0, bit], r.cn_sem.at[1, bit], peers[bit]
+        )
 
     r.cnts[0] = r.cnt[...]
     count_copy(0).start()
     angle_tables(r)
+    cot_load.wait()
+    r.gout[own, ROWS - 64 : LANES] = jnp.zeros((OWN, 128), BF16)
+    r.gout[own, 0:ROWS] = (r.out[...].astype(F32) * r.info[2:3, 0:ROWS]).astype(BF16)
     small_y.wait()
     small_f.start()
     for ref in (r.sbup, r.sg1, r.sb1, r.sg2, r.sb2, r.sbo, r.sf0, r.sf1, r.dk, r.dv):
@@ -606,6 +642,7 @@
     small_f.wait()
     loads.wdn.wait()
     flip(r.wdn, r.wdnt)
+    total = r.cnt[...]
     for bit in range(r.dp_bits):
         count_copy(bit).wait()
         total = r.cnts[bit] + r.cntr[bit]
@@ -613,231 +650,298 @@
             r.cnts[bit + 1] = total
             count_copy(bit + 1).start()
     low, high = total[:, 0:1], total[:, 1:2]
-    share = jnp.where(r.cnt[:, 2:3] > 0.5, low, high) / (low + high)
+    own_low = 1.0 - r.group[0].astype(F32)
+    share = (own_low * low + (1.0 - own_low) * high) / (low + high)
     r.share[...] = jnp.broadcast_to(share, (8, 128))
     loads.wqkv.wait()
     loads.wout.wait()
-
-    tokens.relay(0)
-
-    def project_chunk(c, carry):
-        @pl.when(c + 1 < CHUNKS)
-        def _():
-            tokens.relay(c + 1)
-
-        tokens.arrived(c)
-        project(r, c)
-        return carry
-
-    lax.fori_loop(0, CHUNKS, project_chunk, 0)
-
     wo_here = r.wof.at[own]
     wo_there = r.wof.at[feat(spot.yp_mp)]
     wo_y = remote(r.wout, wo_here, r.wo_sem.at[0], r.wo_sem.at[1], spot.yp)
     wo_c = remote(r.wout, wo_here, r.wo_sem.at[2], r.wo_sem.at[3], spot.sib)
     wo_f = remote(wo_there, wo_there, r.wo_sem.at[4], r.wo_sem.at[5], spot.sib)
-    wo_y.start()
     wo_c.start()
     r.wof[own, :] = r.wout[...]
-    r.gout[own, ROWS - 64 : LANES] = jnp.zeros((OWN, 128), BF16)
-    keep = r.info[2:3, 0:ROWS]
-    pltpu.make_async_copy(r.cot, r.out, r.load_sem.at[5]).wait()
-    r.gout[own, 0:ROWS] = (r.out[...].astype(F32) * keep).astype(BF16)
     attended = Spread(spot, r.att, r.at_sem)
     cotangents = Spread(spot, r.gout, r.ct_sem)
 
-    def after_tile(t):
-        @pl.when(t % 2 == 1)
-        def _():
-            attended.send(t // 2)
-            cotangents.send(t // 2)
-
-            @pl.when(t >= 5)
+    tokens.relay(0)
+
+    def project_chunk(c, carry):
+        @pl.when(c + 1 < CHUNKS)
+        def _():
+            tokens.relay(c + 1)
+
+        tokens.arrived(c)
+
+        @pl.when(c == 2)
+        def _():
+            wo_y.start()
+
+        @pl.when(c >= 4)
+        def _():
+            cotangents.send(c - 4)
+
+        project(r, c)
+        return carry
+
+    lax.fori_loop(0, CHUNKS, project_chunk, 0)
+
+    def windows(source):
+        for j in range(3):
+            start = 576 * j - 32 * (j // 2)
+            r.win[j, :, 0:NARROW] = source[:, start : start + NARROW]
+
+    def both_tiles(c, tile, source):
+        for half in range(2):
+            t = 2 * c + half
+            j = t // 5
+
+            @pl.when((t != 4) & (t != 9))
             def _():
-                attended.relay(t // 2 - 2)
-                cotangents.relay(t // 2 - 2)
-
-    for j in range(3):
-        start = 576 * j - 32 * (j // 2)
-        r.win[:, 0:NARROW] = r.v[:, start : start + NARROW]
-
-        def attend(i, carry):
-            attend_tile(r, spot, 5 * j + i, start, NARROW, r.win[:, 0:NARROW])
-            after_tile(5 * j + i)
-            return carry
-
-        lax.fori_loop(0, 4, attend, 0)
-        if j == 0:
-            attend_tile(r, spot, 4, 0, 1152, r.v[:, 0:1152])
-            after_tile(4)
-        if j == 1:
-            attend_tile(r, spot, 9, 976, 752, r.v[:, 976:1728])
-            after_tile(9)
+                tile(r, spot, t, 576 * j - 32 * (j // 2), NARROW, r.win[j, :, 0:NARROW])
+
+            if half == 0:
+
+                @pl.when(t == 4)
+                def _():
+                    tile(r, spot, 4, 0, 1152, source[:, 0:1152])
+
+            else:
+
+                @pl.when(t == 9)
+                def _():
+                    tile(r, spot, 9, 976, 752, source[:, 976:1728])
+
+    windows(r.v)
+
+    def attend(c, carry):
+        both_tiles(c, attend_tile, r.v)
+        attended.send(c)
+
+        @pl.when(c + 3 < CHUNKS)
+        def _():
+            cotangents.send(c + 3)
+
+        @pl.when((c >= 3) & (c <= 5))
+        def _():
+            cotangents.relay(c - 3)
+
+        return carry
+
+    lax.fori_loop(0, CHUNKS, attend, 0)
     wo_y.wait()
     wo_f.start()
+    r.atto[...] = r.att[own, :]
+    attended.relay(0)
     wo_c.wait()
     wo_f.wait()
     flip(r.wof, r.wot)
-    r.atto[...] = r.att[own, :]
 
     outward = Exchange(r, spot, r.mp, r.mr, r.ms, r.mc, r.mo_sem)
     second = Exchange(r, spot, r.gp, r.gr, r.gs, r.gc, r.g2_sem, r.stats)
     g_att = Spread(spot, r.gatt, r.ga_sem)
     order = list(range(r.dp_bits))
     turned = order[1:] + order[:1]
-    down = Reduce(spot, r.accdn, r.ardn, r.resdn, order, r.dn_sem.at[0], r.dn_sem.at[1])
-    up = Reduce(spot, r.accup, r.arup, r.resup, turned, r.up_sem.at[0], r.up_sem.at[1])
-    out = Reduce(spot, r.accwo, r.arwo, r.reswo, order, r.wr_sem.at[0], r.wr_sem.at[1])
-    share = r.share[0:1, 0:1]
-
-    def mlp_step(n, carry):
-        @pl.when(n < CHUNKS)
-        def _():
-            @pl.when(n >= CHUNKS - 2)
+
+    def halves(acc, arrive, res, sems):
+        rows = acc.shape[0] // 2
+        return [
+            Reduce(
+                spot,
+                acc.at[rows * n : rows * n + rows],
+                arrive[n],
+                res.at[rows * n : rows * n + rows],
+                order,
+                sems.at[n],
+            )
+            for n in range(2)
+        ]
+
+    down = halves(r.accdn, r.ardn, r.resdn, r.dn_sem)
+    up = halves(r.accup, r.arup, r.resup, r.up_sem)
+
+    def advance(*reduces):
+        for reduce in reduces:
+            reduce.advance()
+
+    def forward(n, carry):
+        @pl.when(n + 1 < CHUNKS)
+        def _():
+            attended.relay(n + 1)
+
+            @pl.when(n + 1 >= 3)
             def _():
-                attended.relay(n)
-                cotangents.relay(n)
-
-            attended.arrived(n)
-            cotangents.arrived(n)
-            mlp_part(r, spot, n, outward, second)
-
-        @pl.when(n == CHUNKS)
-        def _():
-            r.accdn[...] = (dot(r.act[...], r.gout[...], NT) * r.share[0:1, 0:1]).astype(BF16)
-            down.start()
-
-        @pl.when(n == CHUNKS + 1)
-        def _():
-            r.accup[...] = (dot(r.h2[...], r.gpre[...], NT) * r.share[0:1, 0:1]).astype(BF16)
-            up.start()
-
-        @pl.when((n >= 1) & (n <= CHUNKS))
+                cotangents.relay(n + 1)
+
+        attended.arrived(n)
+        mlp_forward(r, spot, n, outward)
+        return carry
+
+    lax.fori_loop(0, CHUNKS, forward, 0)
+    for c in range(CHUNKS):
+        cotangents.arrived(c)
+    r.accdn[...] = (dot(r.act[...], r.gout[...], NT) * r.share[0:1, 0:1]).astype(BF16)
+    down[0].start()
+    down[1].start()
+
+    def norm_step(c):
+        second_norm_back(r, spot, c, second)
+        g_att.send(c)
+
+    def backward(n, carry):
+        mlp_backward(r, n, second)
+
+        @pl.when(n >= 1)
         def _():
             second.pass_on(n - 1)
 
-        @pl.when((n >= 3) & (n <= CHUNKS + 2))
-        def _():
-            second_norm_back(r, spot, n - 3, second)
-            g_att.send(n - 3)
-
-        @pl.when(n >= 4)
-        def _():
-            g_att.relay(n - 4)
+        @pl.when(n >= 3)
+        def _():
+            norm_step(n - 3)
+
+        @pl.when(n == 3)
+        def _():
+            advance(down[0])
+
+        @pl.when(n == 6)
+        def _():
+            advance(down[1], down[0])
 
         return carry
 
-    lax.fori_loop(0, CHUNKS + 4, mlp_step, 0)
-
-    for c in range(CHUNKS):
+    lax.fori_loop(0, CHUNKS, backward, 0)
+    second.pass_on(CHUNKS - 1)
+    r.accup[...] = (dot(r.h2[...], r.gpre[...], NT) * r.share[0:1, 0:1]).astype(BF16)
+    up[0].start()
+    up[1].start()
+    flip(r.wqkv, r.wqkvn)
+    windows(r.qk.at[192:384])
+    first = Exchange(r, spot, r.gp, r.gr, r.gs, r.gc, r.g1_sem, r.stats)
+    g_att.relay(0)
+
+    def first_chunks(chunks):
+        def one(c, carry):
+            unrotate(r, c)
+            first_part(r, c, first)
+            return carry
+
+        lax.fori_loop(chunks[0], chunks[-1] + 1, one, 0)
+
+    def back(c, carry):
+        @pl.when(c + 4 < CHUNKS)
+        def _():
+            norm_step(c + 4)
+
+        @pl.when(c + 1 < CHUNKS)
+        def _():
+            g_att.relay(c + 1)
+
+        g_att.arrived(c)
+        both_tiles(c, back_tile, r.qk.at[192:384])
+
+        @pl.when(c == 0)
+        def _():
+            advance(down[1], down[0])
+
+        @pl.when(c == 2)
+        def _():
+            first_chunks((0, 1))
+            advance(up[0], down[1], down[0], up[1])
+
+        @pl.when(c == 3)
+        def _():
+            first.pass_on(0)
+            first.pass_on(1)
+            outward.pass_on(0)
+            outward.pass_on(1)
+
+        @pl.when(c == 4)
+        def _():
+            first_chunks((2, 3))
+            advance(up[0], down[1], down[0])
+
+        @pl.when(c == 5)
+        def _():
+            first.pass_on(2)
+            first.pass_on(3)
+            outward.pass_on(2)
+            outward.pass_on(3)
+            advance(up[1])
+
+        return carry
+
+    lax.fori_loop(0, CHUNKS, back, 0)
+    first_chunks((4, 5, 6))
+    advance(down[1], up[0], down[0], up[1])
+    r.accqkv[...] = (dot(r.gproj[0:576, :], r.h1[...], NT) * r.share[0:1, 0:1]).astype(BF16)
+    qkv = [
+        Reduce(
+            spot,
+            r.accqkv.at[OWN * n : OWN * n + OWN],
+            r.arqkv[n],
+            r.resqkv.at[OWN * n : OWN * n + OWN],
+            order if n < 2 else turned,
+            r.qr_sem.at[n],
+        )
+        for n in range(3)
+    ]
+    for reduce in qkv:
+        reduce.start()
+    for c in range(4, CHUNKS):
+        first.pass_on(c)
+    r.accwo[...] = (dot(r.atto[...], r.gatt[...], NT) * r.share[0:1, 0:1]).astype(BF16)
+    out = Reduce(spot, r.accwo, r.arwo, r.reswo, turned, r.wr_sem)
+    out.start()
+    for c in range(4, CHUNKS):
         outward.pass_on(c)
-
-    def before_tile(t):
-        @pl.when(t % 2 == 0)
-        def _():
-            g_att.arrived(t // 2)
-
-    for j in range(3):
-        start = 576 * j - 32 * (j // 2)
-        r.win[:, 0:NARROW] = r.qk[192:384, start : start + NARROW]
-
-        def back(i, carry):
-            before_tile(5 * j + i)
-            back_tile(r, spot, 5 * j + i, start, NARROW, r.win[:, 0:NARROW])
-            return carry
-
-        lax.fori_loop(0, 4, back, 0)
-        if j == 0:
-            before_tile(4)
-            back_tile(r, spot, 4, 0, 1152, r.qk[192:384, 0:1152])
-        if j == 1:
-            back_tile(r, spot, 9, 976, 752, r.qk[192:384, 976:1728])
-        down.advance()
-        up.advance()
-        if j == 1:
-            finish_out(r, spot, outward)
-            down.advance()
-    r.accwo[...] = (dot(r.atto[...], r.gatt[...], NT) * r.share[0:1, 0:1]).astype(BF16)
-    out.start()
-    lax.fori_loop(0, CHUNKS, lambda c, carry: (unrotate(r, c), carry)[1], 0)
-    down.advance()
-    up.advance()
-    r.accqk[...] = (dot(r.gproj[0:384, :], r.h1[...], NT) * r.share[0:1, 0:1]).astype(BF16)
-    r.accv[...] = (dot(r.gproj[384:576, :], r.h1[...], NT) * r.share[0:1, 0:1]).astype(BF16)
-    pair = Reduce(spot, r.accqk, r.arqk, r.resqk, order, r.qr_sem.at[0], r.qr_sem.at[1])
-    value = Reduce(spot, r.accv, r.arv, r.resv, turned, r.vr_sem.at[0], r.vr_sem.at[1])
-    pair.start()
-    value.start()
-    out.advance()
-    flip(r.wqkv, r.wqkvn)
-    first = Exchange(r, spot, r.gp, r.gr, r.gs, r.gc, r.g1_sem, r.stats)
-
-    def last_step(n, carry):
-        @pl.when(n < CHUNKS)
-        def _():
-            first_part(r, spot, n, first)
-
-        @pl.when((n >= 1) & (n <= CHUNKS))
-        def _():
-            first.pass_on(n - 1)
-
-        @pl.when(n >= 3)
-        def _():
-            first_norm_back(r, spot, n - 3, first)
-
-        @pl.when(n == 3)
-        def _():
-            pair.advance()
-            value.advance()
-            out.advance()
-
-        @pl.when(n == 5)
-        def _():
-            down.advance()
-            up.advance()
-
-        @pl.when(n == 7)
-        def _():
-            pair.advance()
-            value.advance()
-            out.advance()
-
+    advance(up[0])
+
+    def norm_one(c, carry):
+        first_norm_back(r, spot, c, first)
         return carry
 
-    lax.fori_loop(0, CHUNKS + 3, last_step, 0)
-
-    def total(ref):
+    lax.fori_loop(0, 5, norm_one, 0)
+    advance(down[1], qkv[2], up[1])
+    lax.fori_loop(5, CHUNKS, norm_one, 0)
+    advance(qkv[0], out)
+
+    def lane_sum(ref):
         return jnp.sum(ref[...], axis=1, keepdims=True)
 
     b_down = jnp.sum(r.gout[own, :].astype(F32), axis=1, keepdims=True)
     b_qkv = jnp.sum(r.gproj[0:576, :].astype(F32), axis=1, keepdims=True)
     columns = [
-        total(r.sbup),
-        jnp.concatenate([b_qkv, total(r.sf0), total(r.sf1)], axis=0),
-        jnp.concatenate([total(r.sbo), total(r.sg1), total(r.sb1), total(r.sg2)], axis=0),
-        jnp.concatenate([total(r.sb2), b_down, jnp.zeros((384, 1), F32)], axis=0),
+        lane_sum(r.sbup),
+        jnp.concatenate([b_qkv, lane_sum(r.sf0), lane_sum(r.sf1)], axis=0),
+        jnp.concatenate([lane_sum(r.sbo), lane_sum(r.sg1), lane_sum(r.sb1), lane_sum(r.sg2)], axis=0),
+        jnp.concatenate([lane_sum(r.sb2), b_down, jnp.zeros((384, 1), F32)], axis=0),
     ]
     lane = lax.broadcasted_iota(jnp.int32, (D, 128), 1)
     table = jnp.zeros((D, 128), F32)
     for n, column in enumerate(columns):
         table = jnp.where(lane == n, column, table)
     table = jnp.transpose(table * r.share[0:1, 0:1])[0:8, :]
+    between = [
+        (qkv[1], up[0], qkv[2], up[1], out, qkv[0], qkv[1]),
+        (up[0], qkv[0], qkv[2], qkv[1]),
+        (qkv[0], qkv[1], up[1], out, qkv[2], qkv[0], qkv[1], out),
+    ]
     for bit in range(r.dp_bits):
         r.sumx[bit] = table
         copy = remote(
             r.sumx.at[bit], r.sumr.at[bit], r.su_sem.at[0, bit], r.su_sem.at[1, bit], peers[bit]
         )
         copy.start()
-        pair.advance()
-        value.advance()
-        out.advance()
+        if bit < len(between):
+            advance(*between[bit])
         copy.wait()
         table = table + r.sumr[bit]
     r.sums[...] = table
-    reduces = (pair, value, out, down, up)
+    finish_out(r, spot, outward)
+    reduces = [qkv[2], qkv[0], out, qkv[1]] + up + down
     while any(reduce.at < len(reduce.phases) for reduce in reduces):
-        for reduce in reduces:
-            reduce.advance()
+        advance(*reduces)
 
 
 def finish_out(r, spot, outward):
@@ -854,6 +958,7 @@
 
 
 def run(dp_bits, **arrays):
+    scalars = ("group",)
     on_demand = ("tok", "cot", "in_wqkv", "in_wup", "in_wdn", "in_wout")
     outs = dict(
         out=((OWN, ROWS), BF16),
@@ -861,8 +966,7 @@
         resdn=((D, D), BF16),
         resup=((D, D), BF16),
         reswo=((OWN, D), BF16),
-        resqk=((384, D), BF16),
-        resv=((OWN, D), BF16),
+        resqkv=((576, D), BF16),
         sums=((8, D), F32),
     )
 
@@ -873,7 +977,6 @@
     own = VM((OWN, LANES), BF16)
     square = VM((D, D), BF16)
     spread = dma(6, CHUNKS)
-    reduce = dma(2, 2 * dp_bits)
     scratch = dict(
         x=full,
         h1=full,
@@ -884,7 +987,7 @@
         cos=VM((96, LANES), F32),
         sin=VM((96, LANES), F32),
         kcol=VM((LANES, TILE), F32),
-        win=VM((OWN, 640), BF16),
+        win=VM((3, OWN, 640), BF16),
         lse=VM((TILES, 8, 384), F32),
         small=VM((D, 128), F32),
         share=VM((8, 128), F32),
@@ -902,7 +1005,12 @@
         act=full,
         gpre=full,
         work=VM((D, CHUNK), F32),
+        mido=VM((OWN, LANES), F32),
+        rows1=VM((8, LANES), F32),
         rows2=VM((8, LANES), F32),
+        info=VM((8, LANES), F32),
+        cols=VM((D, 128), F32),
+        cnt=VM((8, 128), F32),
         stats=VM((4, 8, LANES), F32),
         mp=VM((2, 2, OWN, LANES), BF16),
         mr=VM((2, OWN, LANES), BF16),
@@ -912,11 +1020,10 @@
         gc=own,
         dk=VM((LANES, OWN), F32),
         dv=VM((LANES, OWN), F32),
-        ardn=levels(D),
-        arup=levels(D),
+        ardn=[levels(384), levels(384)],
+        arup=[levels(384), levels(384)],
         arwo=levels(OWN),
-        arqk=levels(384),
-        arv=levels(OWN),
+        arqkv=[levels(OWN), levels(OWN), levels(OWN)],
         sbup=VM((D, 128), F32),
         sg1=VM((OWN, 128), F32),
         sb1=VM((OWN, 128), F32),
@@ -941,11 +1048,10 @@
         mo_sem=dma(8, CHUNKS),
         g2_sem=dma(8, CHUNKS),
         g1_sem=dma(8, CHUNKS),
-        dn_sem=reduce,
-        up_sem=reduce,
-        wr_sem=reduce,
-        qr_sem=reduce,
-        vr_sem=reduce,
+        dn_sem=dma(2, 2, 2 * dp_bits),
+        up_sem=dma(2, 2, 2 * dp_bits),
+        wr_sem=dma(2, 2 * dp_bits),
+        qr_sem=dma(3, 2, 2 * dp_bits),
     )
     shapes, structure = jax.tree.flatten(scratch, is_leaf=lambda leaf: not isinstance(leaf, (dict, list)))
 
@@ -956,12 +1062,12 @@
         named = jax.tree.unflatten(structure, refs[len(arrays) + len(outs) :])
         for name, ref in named.items():
             setattr(r, name, ref)
-        r.mido, r.gatt, r.atto = r.igrad, r.att, r.v
+        r.gatt, r.atto = r.att, r.v
         r.dq, r.gproj, r.ms = r.act, r.h2, r.act.at[OWN : 2 * OWN]
         r.mc = r.act.at[2 * OWN : 3 * OWN]
         r.accdn, r.accup, r.accwo = r.wof, r.wupt, r.wdn.at[0:OWN]
         r.wqkvn = r.wot
-        r.accqk, r.accv = r.wdnt.at[0:384], r.wdnt.at[384:576]
+        r.accqkv = r.wdnt.at[0:576]
         r.dp_bits = dp_bits
         kernel(r, place())
 
@@ -969,7 +1075,10 @@
         body,
         out_shape=[jax.ShapeDtypeStruct(shape, dtype) for shape, dtype in outs.values()],
         in_specs=[
-            pl.BlockSpec(memory_space=pl.ANY if name in on_demand else VM) for name in arrays
+            pl.BlockSpec(
+                memory_space=pl.ANY if name in on_demand else pltpu.SMEM if name in scalars else VM
+            )
+            for name in arrays
         ],
         out_specs=[pl.BlockSpec(memory_space=VM) for _ in outs],
         scratch_shapes=shapes,
@@ -1005,49 +1114,30 @@
 ):
     row_count, width_loc = tokens.shape
     heads_loc = freqs.shape[1]
-    keep = keep_mask.astype(F32)
-    group_now = block_group[0]
-    low = (group_now == 0).astype(F32)
-    kept_total = jnp.sum(keep)
-    segment_size = jnp.where(group_now == 0, GRID_LO * GRID_LO, SLOTS).astype(jnp.int32)
-    segment = (jnp.arange(row_count, dtype=jnp.int32) // segment_size).astype(F32)
-    key_segment = jnp.where(keep_mask > 0, segment, -1.0)
-    info = jnp.stack(
-        [coords[0].astype(F32), coords[1].astype(F32), keep, key_segment, segment] + [keep] * 3
-    )
-    info = jnp.pad(info, ((0, 0), (0, LANES - row_count)))
-    small = jnp.stack(
-        [part.astype(F32) for part in (norm1_gain, norm1_bias, norm2_gain, norm2_bias, b_out, b_down)],
-        axis=1,
-    )
-    cols = jnp.concatenate(
-        [
-            b_up.astype(F32)[:, None],
-            jnp.pad(b_qkv.reshape(-1, 1).astype(F32), ((0, D - 3 * width_loc), (0, 0))),
-            jnp.pad(freqs.reshape(2, 96).T, ((0, D - 96), (0, 0))),
-            jnp.pad(small, ((0, D - width_loc), (0, 0))),
-        ],
-        axis=1,
-    )
-    counts = jnp.stack([kept_total * low, kept_total * (1.0 - low), low])
-
-    def wide(array):
-        return jnp.pad(array, ((0, 0), (0, 128 - array.shape[1])))
+    row = lax.broadcasted_iota(jnp.int32, (8, D), 0)
+    pack = jnp.zeros((8, D), F32)
+    vectors = (b_up, norm1_gain, norm1_bias, norm2_gain, norm2_bias, b_out, b_down)
+    for n, vector in enumerate(vectors):
+        wide = jnp.pad(vector.astype(F32), (0, D - vector.shape[0]))
+        pack = jnp.where(row == n, wide[None, :], pack)
 
     a = run(
         lax.axis_size("dp").bit_length() - 1,
         tok=tokens.T,
         cot=cotangent.T,
-        cols=wide(cols),
-        info=info,
-        cnt=wide(jnp.broadcast_to(counts, (8, 3))),
+        pack=pack,
+        bqkv=b_qkv,
+        freqs=freqs.transpose(1, 0, 2),
+        keep=keep_mask.reshape(1, row_count),
+        coords=coords,
+        group=block_group,
         in_wqkv=w_qkv.transpose(1, 2, 0).reshape(3 * width_loc, D),
         in_wup=w_up,
         in_wdn=w_down,
         in_wout=w_out,
     )
     sums = a.sums
-    grad_qkv = jnp.concatenate([a.resqk, a.resv], axis=0).astype(F32)
+    grad_qkv = a.resqkv.astype(F32)
     half = (2, heads_loc, HEAD_DIM // 2)
     return (
         a.out.T,

time: 254 us -> 211 us (0.83)
  Pallas kernels: 227 us -> 190 us
  local copies, waits for them, and re-layouts: 13.6 us -> 8.85 us
    pallas_call x1, Pallas kernels: 227 us -> 190 us  [run(): pl.pallas_call(body, out_shape=[jax.ShapeDtypeStruct(shape, dtype) for sh...]
    another operation x10 -> x0, local copies, waits for them, and re-layouts: 4.09 us -> none  [the longest x7 3.98 us: local(): jnp.stack([part.astype(F32) for part in (norm1_gain, norm1_bias, norm2_ga...]
where the time goes in v4:
time: 211 us; the launch traced here: 210 us
  Pallas kernels  190 us (90%)
  other arithmetic  10.1 us (5%)
  local copies, waits for them, and re-layouts  8.85 us (4%)
    pallas_call x1, Pallas kernels, run(): pl.pallas_call(body, out_shape=[jax.ShapeDtypeStruct(shape, dtype) for sh...  190 us

profile of v4, /device:TPU:0, one launch (start us, length us, event | category | flops | bytes accessed | tf_op | source)
XLA Modules:
  0.0 210.1 jit_solution(10016928861900465596)
XLA Ops:
  0.6 0.7 pad_convert_fusion
  1.3 0.7 pad_convert_fusion.2
  2.0 0.7 pad_convert_fusion.4
  2.7 0.7 convert_element_type.26
  3.4 0.7 select_select_fusion.refs_2_
  4.1 1.3 reshape.47.refs_5_
  6.0 189.7 %shard_map.289 = (bf16[192,1728]{1,0:T(8,128)(2,1)}, f32[192,1792]{1,0:T(8,128)}, bf16[768,768]{1,0:T(8,128)(2,1)}, bf16[768,768]{1,0:T(8,128)(2,1)}, bf16[192,7...) custom-call(bf16[192,1728]{1,0:T(8,128)(2,1)} %bitcast.21, bf16[192,1728]{1,0:T(8,128)(2,1)} %bitcast.22, ...), custom_call_target="tpu_custom_call" | custom-call | tf_op jit(solution)/shard_map/pallas_call | solution.py:1074
  195.8 1.5 fusion
  197.3 0.1 reshape_squeeze.7
  197.4 0.6 copy.34
  197.9 0.7 slice_reduce_fusion.1
  198.7 0.7 reshape_squeeze.6
  199.4 1.3 slice_reduce_fusion
  200.7 0.0 copy-start.1
  200.7 2.9 %convert_element_type.28 = f32[768,768]{1,0:T(8,128)} convert(bf16[768,768]{1,0:T(8,128)(2,1)} %get-tuple-element.27) | non-fusion elementwise | flops 589824 | bytes 3538944 | tf_op jit(solution)/shard_map/convert_element_type | solution.py:1154
  203.6 0.0 copy-done.1
  203.7 0.0 copy-start.2
  203.7 1.6 convert_element_type.29
  205.2 0.0 copy-start
  205.2 0.0 copy-done.2
  205.2 1.4 convert_bitcast_fusion
  206.6 0.6 copy-done
  207.2 0.0 copy-start.4
  207.2 0.0 copy-start.3
  207.2 1.2 slice_bitcast_fusion
  208.4 0.0 copy-done.4
  208.4 0.9 convert_element_type.27
  209.2 0.0 copy-done.3
  209.2 0.8 copy.37
  (4 shorter events, 0.0 us)
Async XLA Ops:
  200.7 2.9 %copy-start.1 = (bf16[768,768]{1,0:T(8,128)(2,1)S(1)}, bf16[768,768]{1,0:T(8,128)(2,1)}, u32[]{:S(2)}) copy-start(bf16[768,768]{1,0:T(8,128)(2,1)} %get-tuple-element.28) | copy-start | bytes 3538948
  203.7 1.6 copy-start.2
  205.2 2.0 copy-start
  207.2 1.2 copy-start.4
  207.2 2.0 copy-start.3

commit v5 on v4

--- a/solution.py
+++ b/solution.py
@@ -30,6 +30,14 @@
 norm_eps = 1e-06
 root_half = 0.7071067811865476
 inv_root_two_pi = 0.3989422804014327
+
+
+EARLY = 2
+IN_BACKWARD = {6: (0,)}
+BEFORE_TILES = {0: (0,), 1: (1,)}
+AFTER_TILES = {1: (2, 0), 2: (3, 1, 2, 0), 3: (3,), 4: (1, 2, 0, 3), 5: (1,), 6: (2, 0, 3)}
+AT_END = {1: (1, 2), 2: (3,), 4: (4, 6, 5, 7), 5: (1,)}
+IN_SUMS = ((), (4, 2, 6, 5, 7, 3), (6, 7, 4, 5))
 
 
 class Refs:
@@ -63,7 +71,10 @@
     barrier = pltpu.get_barrier_semaphore()
     for device in devices:
         pl.semaphore_signal(barrier, inc=1, device_id=device, device_id_type=MESH)
-    pl.semaphore_wait(barrier, len(devices))
+
+
+def meet(devices):
+    pl.semaphore_wait(pltpu.get_barrier_semaphore(), len(devices))
 
 
 def dp_partner(spot, bit):
@@ -83,33 +94,70 @@
     return pl.ds(pl.multiple_of(t * TILE, TILE), TILE)
 
 
+def flipped(spot, bits, number):
+    dp = spot.dp
+    for n, bit in enumerate(bits):
+        if (number >> n) & 1:
+            dp = dp + (1 - 2 * ((spot.dp // (1 << bit)) % 2)) * (1 << bit)
+    return (dp, spot.mp)
+
+
+def cut(shape):
+    rows, cols = shape
+    if (rows // 2) % 16 == 0:
+        return (rows // 2, cols)
+    if (cols // 2) % 128 == 0:
+        return (rows, cols // 2)
+    return shape
+
+
+def plan(shape, groups):
+    steps = []
+    for bits in groups:
+        after = shape
+        for _ in bits:
+            after = cut(after)
+        whole = cut(cut(shape)) if len(bits) == 2 else cut(shape)
+        if len(bits) == 2 and cut(shape) == cut(cut(shape)):
+            for bit in bits:
+                now = cut(shape)
+                steps.append(((bit,), now, now != shape))
+                shape = now
+            continue
+        steps.append((bits, whole, whole != shape))
+        shape = after
+    return steps
+
+
 class Reduce:
-    def __init__(self, spot, acc, arrive, res, order, sems):
-        self.spot, self.res, self.send, self.recv = spot, res, sems.at[0], sems.at[1]
+    def __init__(self, spot, acc, arrive, res, groups, sems):
+        self.spot, self.res, self.sems = spot, res, sems
         self.at = 0
         self.phases = []
         gathers = []
-        rows, cols = acc.shape
-        row, col = 0, 0
-        source, own_row, own_col = acc, 0, 0
-        for level, bit in enumerate(order):
-            mine = (spot.dp // (1 << bit)) % 2
-            keep, away, halved = (0, 0), (0, 0), True
-            if (rows // 2) % 16 == 0:
-                rows = rows // 2
-                keep, away = (mine * rows, 0), ((1 - mine) * rows, 0)
-            elif (cols // 2) % 128 == 0:
-                cols = cols // 2
-                keep, away = (0, mine * cols), (0, (1 - mine) * cols)
-            else:
-                halved = False
-            own_row, own_col = own_row + keep[0], own_col + keep[1]
-            shape = (rows, cols)
-            self.phases.append((bit, source, away, keep, shape, arrive[level]))
-            if halved:
-                gathers.append((bit, res, (own_row, own_col), None, shape, res))
-            source = arrive[level]
-        self.own = (own_row, own_col)
+        source, row, col = acc, 0, 0
+        steps = plan(acc.shape, groups)
+        shape = acc.shape
+        for (bits, after, differ), target in zip(steps, arrive, strict=True):
+            corners = []
+            for number in range(1 << len(bits)):
+                at, part = (0, 0), shape
+                for n, bit in enumerate(bits):
+                    smaller = cut(part)
+                    mine = (spot.dp // (1 << bit)) % 2
+                    side = 1 - mine if (number >> n) & 1 else mine
+                    if smaller[0] < part[0]:
+                        at = (at[0] + side * smaller[0], at[1])
+                    elif smaller[1] < part[1]:
+                        at = (at[0], at[1] + side * smaller[1])
+                    part = smaller
+                corners.append(at)
+            row, col = row + corners[0][0], col + corners[0][1]
+            self.phases.append((bits, source, corners, after, target))
+            if differ:
+                gathers.append((bits, res, (row, col), after, None))
+            source, shape = target.at[0], after
+        self.own = (row, col)
         self.sums = len(self.phases)
         self.phases += gathers[::-1]
 
@@ -123,27 +171,37 @@
             span(corner[0], shape[0], 16, ref.shape[0]), span(corner[1], shape[1], 128, ref.shape[1])
         ]
 
-    def copy(self):
-        bit, source, away, keep, shape, target = self.phases[self.at]
-        piece = self.piece(source, away, shape)
-        goal = piece if keep is None else target
-        return remote(
-            piece, goal, self.send.at[self.at], self.recv.at[self.at], dp_partner(self.spot, bit)
-        )
+    def copies(self):
+        bits, source, corners, shape, target = self.phases[self.at]
+        out = []
+        for number in range(1, 1 << len(bits)):
+            if target is None:
+                piece = self.piece(source, corners, shape)
+                goal = piece
+            else:
+                piece = self.piece(source, corners[number], shape)
+                goal = target.at[number - 1]
+            sems = (self.sems.at[0, self.at, number - 1], self.sems.at[1, self.at, number - 1])
+            out.append(remote(piece, goal, *sems, flipped(self.spot, bits, number)))
+        return out
 
     def start(self):
-        self.copy().start()
+        for copy in self.copies():
+            copy.start()
 
     def add(self):
-        _, source, _, keep, shape, target = self.phases[self.at]
-        held = self.piece(source, keep, shape)
+        bits, source, corners, shape, target = self.phases[self.at]
+        held = self.piece(source, corners[0], shape)
         last = self.at == self.sums - 1
-        goal = self.piece(self.res, self.own, shape) if last else target
+        goal = self.piece(self.res, self.own, shape) if last else target.at[0]
         step = 48 if shape[0] % 48 == 0 else 16
 
         def block(i, carry):
             rows = pl.ds(pl.multiple_of(i * step, 16), step)
-            goal[rows, :] = (held[rows, :].astype(F32) + target[rows, :].astype(F32)).astype(BF16)
+            total = held[rows, :].astype(F32)
+            for n in range((1 << len(bits)) - 1):
+                total = total + target[n, rows, :].astype(F32)
+            goal[rows, :] = total.astype(BF16)
             return carry
 
         lax.fori_loop(0, shape[0] // step, block, 0)
@@ -151,23 +209,13 @@
     def advance(self):
         if self.at >= len(self.phases):
             return
-        self.copy().wait()
+        for copy in self.copies():
+            copy.wait()
         if self.at < self.sums:
             self.add()
         self.at += 1
         if self.at < len(self.phases):
             self.start()
-
-
-def arrive_shapes(rows, cols, dp_bits):
-    shapes = []
-    for _ in range(dp_bits):
-        if (rows // 2) % 16 == 0:
-            rows = rows // 2
-        elif (cols // 2) % 128 == 0:
-            cols = cols // 2
-        shapes.append((rows, cols))
-    return shapes
 
 
 class Exchange:
@@ -315,28 +363,13 @@
 
 
 def phi_parts(value):
-    scaled = jnp.clip(value * root_half, -3.832506856900711, 3.832506856900711)
-    square = scaled * scaled
-    top = 0.00022905065861350646
-    for factor in (
-        0.0034082910107109506,
-        0.050955695062380861,
-        0.18520832239976145,
-        1.128379143519084,
-    ):
-        top = top * square + factor
-    low = -1.1791602954361697e-7
-    for factor in (
-        0.000023547966471313185,
-        0.0010179625278914885,
-        0.014070470171167667,
-        0.11098505178285362,
-        0.49746925110067538,
-        1.0,
-    ):
-        low = low * square + factor
-    error = scaled * top / low
-    return (0.5 + 0.5 * error, inv_root_two_pi * jnp.exp(-0.5 * value * value))
+    bell = jnp.exp(-0.5 * value * value)
+    inner = 1.0 / (1.0 + (0.3275911 * root_half) * jnp.abs(value))
+    series = 0.5 * 1.061405429
+    for factor in (-1.453152027, 1.421413741, -0.284496736, 0.254829592):
+        series = series * inner + 0.5 * factor
+    beyond = series * inner * bell
+    return (jnp.where(value >= 0.0, 1.0 - beyond, beyond), inv_root_two_pi * bell)
 
 
 def normalize(values):
@@ -483,22 +516,36 @@
     return pl.ds(pl.multiple_of(OWN * spot.mp + 64 * heads[0], 16), 64 * len(heads))
 
 
+def key_blocks(width):
+    count = -(-width // 384)
+    size = -(-width // (16 * count)) * 16
+    return [(at, min(size, width - at)) for at in range(0, width, size)]
+
+
 def back_tile(r, spot, tile, start, width, keys):
-    window = pl.ds(pl.multiple_of(start, 16), width)
     at = tile_lanes(tile)
     queries = block_diagonal(r.qk[0:192, at] * BF16(0.125))
-    grads = block_diagonal(dot(r.wout[...], r.gatt[:, at]).astype(BF16))
-    mask = tile_mask(r, tile, start, width)
+    grad_rows = dot(r.wout[...], r.gatt[:, at]).astype(BF16)
+    grads = block_diagonal(grad_rows)
+    product = grad_rows.astype(F32) * r.atto[:, at].astype(F32)
+    centers = [jnp.sum(product[64 * h : 64 * h + 64], axis=0, keepdims=True) for h in range(3)]
     for heads in head_groups(width):
         span = slice(TILE * heads[0], TILE * heads[-1] + TILE)
         query, grad = queries[:, span], grads[:, span]
-        scores = dot(r.kn[window, :], query)
-        probs = jnp.exp(scores + repeat(mask, scores) - r.lse[tile, 0:1, span])
-        g_probs = dot(r.vn[window, :], grad)
-        center = jnp.sum(probs * g_probs, axis=0, keepdims=True)
-        g_scores = (probs * (g_probs - center)).astype(BF16)
-        r.dv[window, :] += dot(probs.astype(BF16), grad, NT)
-        r.dk[window, :] += dot(g_scores, query, NT)
+        center = jnp.concatenate([centers[h] for h in heads], axis=1)
+        log = r.lse[tile, 0:1, span]
+        parts = []
+        for offset, size in key_blocks(width):
+            window = pl.ds(pl.multiple_of(start + offset, 16), size)
+            mask = tile_mask(r, tile, start + offset, size)
+            scores = dot(r.kn[window, :], query)
+            probs = jnp.exp(scores + repeat(mask, scores) - log)
+            g_probs = dot(r.vn[window, :], grad)
+            g_scores = (probs * (g_probs - center)).astype(BF16)
+            r.dv[window, :] += dot(probs.astype(BF16), grad, NT)
+            r.dk[window, :] += dot(g_scores, query, NT)
+            parts.append(g_scores)
+        g_scores = jnp.concatenate(parts, axis=0)
         rows = slice(64 * heads[0], 64 * heads[-1] + 64)
         r.dq[rows, at] = (from_diagonal(dot(keys, g_scores), heads) * 0.125).astype(BF16)
 
@@ -533,7 +580,6 @@
     g_act = dot(r.wdn[...], r.gout[:, at])
     g_pre = (g_act * r.gpre[:, at].astype(F32)).astype(BF16)
     r.gpre[:, at] = g_pre
-    r.sbup[...] += fold(g_pre.astype(F32))
     give_gradient(r, c, sums, dot(r.wup[...], g_pre), r.small[:, 6:7], r.small[:, 7:8], r.h2)
 
 
@@ -594,6 +640,9 @@
 
 def kernel(r, spot):
     peers = [dp_partner(spot, bit) for bit in range(r.dp_bits)]
+    both = [flipped(spot, bits, 3) for bits in r.groups if len(bits) == 2]
+    greeted = [spot.sib, spot.yp] + peers + both
+    greet(greeted)
     token_load = pltpu.make_async_copy(r.tok, r.out, r.load_sem.at[4])
     token_load.start()
     cot_load = pltpu.make_async_copy(r.cot, r.out, r.load_sem.at[5])
@@ -603,135 +652,136 @@
     ):
         setattr(loads, name, pltpu.make_async_copy(source, getattr(r, name), r.load_sem.at[n]))
         getattr(loads, name).start()
-    greet([spot.sib, spot.yp] + peers)
     own = feat(spot.mp)
-    r.x[own, ROWS - 64 : LANES] = jnp.zeros((OWN, 128), BF16)
-    token_load.wait()
-    r.x[own, 0:ROWS] = r.out[...]
-    cot_load.start()
-    tokens = Spread(spot, r.x, r.tk_sem)
-    for c in range(CHUNKS):
-        tokens.send(c)
-    row_tables(r)
-    r.small[own, :] = r.cols[0:192, :]
     here, there = r.small.at[own], r.small.at[feat(spot.yp_mp)]
     small_y = remote(r.cols.at[0:192], here, r.sm_sem.at[0], r.sm_sem.at[1], spot.yp)
     small_c = remote(r.cols.at[0:192], here, r.sm_sem.at[2], r.sm_sem.at[3], spot.sib)
     small_f = remote(there, there, r.sm_sem.at[4], r.sm_sem.at[5], spot.sib)
-    small_y.start()
-    small_c.start()
 
     def count_copy(bit):
         return remote(
             r.cnts.at[bit], r.cntr.at[bit], r.cn_sem.at[0, bit], r.cn_sem.at[1, bit], peers[bit]
         )
 
+    def count_step(bit):
+        count_copy(bit).wait()
+        if bit + 1 < r.dp_bits:
+            r.cnts[bit + 1] = r.cnts[bit] + r.cntr[bit]
+            count_copy(bit + 1).start()
+
+    tokens = Spread(spot, r.x, r.tk_sem)
+    attended = Spread(spot, r.att, r.at_sem)
+    cotangents = Spread(spot, r.gout, r.ct_sem)
+    r.x[own, ROWS - 64 : LANES] = jnp.zeros((OWN, 128), BF16)
+    r.gout[own, ROWS - 64 : LANES] = jnp.zeros((OWN, 128), BF16)
+    token_load.wait()
+    r.x[own, 0:ROWS] = r.out[...]
+    cot_load.start()
+    meet(greeted)
+    tokens.to_y(0).start()
+    row_tables(r)
+    r.small[own, :] = r.cols[0:192, :]
     r.cnts[0] = r.cnt[...]
+    small_y.start()
     count_copy(0).start()
-    angle_tables(r)
-    cot_load.wait()
-    r.gout[own, ROWS - 64 : LANES] = jnp.zeros((OWN, 128), BF16)
-    r.gout[own, 0:ROWS] = (r.out[...].astype(F32) * r.info[2:3, 0:ROWS]).astype(BF16)
-    small_y.wait()
-    small_f.start()
-    for ref in (r.sbup, r.sg1, r.sb1, r.sg2, r.sb2, r.sbo, r.sf0, r.sf1, r.dk, r.dv):
-        ref[...] = jnp.zeros_like(ref)
-    loads.wup.wait()
-    flip(r.wup, r.wupt)
-    small_c.wait()
-    small_f.wait()
-    loads.wdn.wait()
-    flip(r.wdn, r.wdnt)
-    total = r.cnt[...]
-    for bit in range(r.dp_bits):
-        count_copy(bit).wait()
-        total = r.cnts[bit] + r.cntr[bit]
-        if bit + 1 < r.dp_bits:
-            r.cnts[bit + 1] = total
-            count_copy(bit + 1).start()
-    low, high = total[:, 0:1], total[:, 1:2]
-    own_low = 1.0 - r.group[0].astype(F32)
-    share = (own_low * low + (1.0 - own_low) * high) / (low + high)
-    r.share[...] = jnp.broadcast_to(share, (8, 128))
-    loads.wqkv.wait()
+    for c in range(1, CHUNKS):
+        tokens.to_y(c).start()
+    small_c.start()
+    for c in range(CHUNKS):
+        tokens.to_sib(c).start()
     loads.wout.wait()
     wo_here = r.wof.at[own]
     wo_there = r.wof.at[feat(spot.yp_mp)]
     wo_y = remote(r.wout, wo_here, r.wo_sem.at[0], r.wo_sem.at[1], spot.yp)
     wo_c = remote(r.wout, wo_here, r.wo_sem.at[2], r.wo_sem.at[3], spot.sib)
     wo_f = remote(wo_there, wo_there, r.wo_sem.at[4], r.wo_sem.at[5], spot.sib)
+    wo_y.start()
     wo_c.start()
     r.wof[own, :] = r.wout[...]
-    attended = Spread(spot, r.att, r.at_sem)
-    cotangents = Spread(spot, r.gout, r.ct_sem)
-
+    angle_tables(r)
+    small_y.wait()
+    small_f.start()
+    cot_load.wait()
+    r.gout[own, 0:ROWS] = (r.out[...].astype(F32) * r.info[2:3, 0:ROWS]).astype(BF16)
+    for c in range(2):
+        cotangents.send(c)
+    count_step(0)
+    loads.wup.wait()
+    flip(r.wup, r.wupt)
+    count_step(1)
+    for ref in (r.sg1, r.sb1, r.sg2, r.sb2, r.sbo, r.sf0, r.sf1, r.dk, r.dv):
+        ref[...] = jnp.zeros_like(ref)
+    loads.wdn.wait()
+    flip(r.wdn, r.wdnt)
+    loads.wqkv.wait()
+    small_c.wait()
+    small_f.wait()
     tokens.relay(0)
 
-    def project_chunk(c, carry):
-        @pl.when(c + 1 < CHUNKS)
-        def _():
-            tokens.relay(c + 1)
-
-        tokens.arrived(c)
+    def window(source, j):
+        start = 576 * j - 32 * (j // 2)
+        r.win[j, :, 0:NARROW] = source[:, start : start + NARROW]
+
+    def both_tiles(c, tile, source):
+        def narrow(t):
+            j = t // 5
+            tile(r, spot, t, 576 * j - 32 * (j // 2), NARROW, r.win[j, :, 0:NARROW])
+
+        @pl.when((c != 2) & (c != 4))
+        def _():
+            narrow(2 * c)
+            narrow(2 * c + 1)
 
         @pl.when(c == 2)
         def _():
-            wo_y.start()
-
-        @pl.when(c >= 4)
-        def _():
-            cotangents.send(c - 4)
-
-        project(r, c)
+            tile(r, spot, 4, 0, 1152, source[:, 0:1152])
+            narrow(5)
+
+        @pl.when(c == 4)
+        def _():
+            narrow(8)
+            tile(r, spot, 9, 976, 752, source[:, 976:1728])
+
+    def attention(n, carry):
+        @pl.when(n < CHUNKS)
+        def _():
+            @pl.when(n + 1 < CHUNKS)
+            def _():
+                tokens.relay(n + 1)
+
+            tokens.arrived(n)
+            project(r, n)
+
+        for j in range(3):
+
+            @pl.when(n == 2 * j + 2)
+            def _():
+                window(r.v, j)
+
+        @pl.when(n >= 2)
+        def _():
+            both_tiles(n - 2, attend_tile, r.v)
+            attended.send(n - 2)
+
+        @pl.when(n == CHUNKS)
+        def _():
+            wo_y.wait()
+            wo_f.start()
+
         return carry
 
-    lax.fori_loop(0, CHUNKS, project_chunk, 0)
-
-    def windows(source):
-        for j in range(3):
-            start = 576 * j - 32 * (j // 2)
-            r.win[j, :, 0:NARROW] = source[:, start : start + NARROW]
-
-    def both_tiles(c, tile, source):
-        for half in range(2):
-            t = 2 * c + half
-            j = t // 5
-
-            @pl.when((t != 4) & (t != 9))
-            def _():
-                tile(r, spot, t, 576 * j - 32 * (j // 2), NARROW, r.win[j, :, 0:NARROW])
-
-            if half == 0:
-
-                @pl.when(t == 4)
-                def _():
-                    tile(r, spot, 4, 0, 1152, source[:, 0:1152])
-
-            else:
-
-                @pl.when(t == 9)
-                def _():
-                    tile(r, spot, 9, 976, 752, source[:, 976:1728])
-
-    windows(r.v)
-
-    def attend(c, carry):
-        both_tiles(c, attend_tile, r.v)
-        attended.send(c)
-
-        @pl.when(c + 3 < CHUNKS)
-        def _():
-            cotangents.send(c + 3)
-
-        @pl.when((c >= 3) & (c <= 5))
-        def _():
-            cotangents.relay(c - 3)
-
-        return carry
-
-    lax.fori_loop(0, CHUNKS, attend, 0)
-    wo_y.wait()
-    wo_f.start()
+    lax.fori_loop(0, CHUNKS + 2, attention, 0)
+    for c in range(2, CHUNKS):
+        cotangents.send(c)
+    for bit in range(2, r.dp_bits):
+        count_step(bit)
+    last = r.dp_bits - 1
+    total = r.cnts[last] + r.cntr[last]
+    low, high = total[:, 0:1], total[:, 1:2]
+    own_low = 1.0 - r.group[0].astype(F32)
+    share = (own_low * low + (1.0 - own_low) * high) / (low + high)
+    r.share[...] = jnp.broadcast_to(share, (8, 128))
+
     r.atto[...] = r.att[own, :]
     attended.relay(0)
     wo_c.wait()
@@ -741,8 +791,6 @@
     outward = Exchange(r, spot, r.mp, r.mr, r.ms, r.mc, r.mo_sem)
     second = Exchange(r, spot, r.gp, r.gr, r.gs, r.gc, r.g2_sem, r.stats)
     g_att = Spread(spot, r.gatt, r.ga_sem)
-    order = list(range(r.dp_bits))
-    turned = order[1:] + order[:1]
 
     def halves(acc, arrive, res, sems):
         rows = acc.shape[0] // 2
@@ -752,7 +800,7 @@
                 acc.at[rows * n : rows * n + rows],
                 arrive[n],
                 res.at[rows * n : rows * n + rows],
-                order,
+                r.groups,
                 sems.at[n],
             )
             for n in range(2)
@@ -761,62 +809,77 @@
     down = halves(r.accdn, r.ardn, r.resdn, r.dn_sem)
     up = halves(r.accup, r.arup, r.resup, r.up_sem)
 
-    def advance(*reduces):
-        for reduce in reduces:
-            reduce.advance()
+    pieces = down + up
+
+    def advance(numbers):
+        for number in numbers:
+            if number < len(pieces):
+                pieces[number].advance()
+
+    def slots(table, n):
+        for at in sorted(table):
+
+            @pl.when(n == at)
+            def _():
+                advance(table[at])
+
+    def norm_step(c):
+        second_norm_back(r, spot, c, second)
+        g_att.send(c)
 
     def forward(n, carry):
         @pl.when(n + 1 < CHUNKS)
         def _():
             attended.relay(n + 1)
-
-            @pl.when(n + 1 >= 3)
-            def _():
-                cotangents.relay(n + 1)
 
         attended.arrived(n)
         mlp_forward(r, spot, n, outward)
         return carry
 
     lax.fori_loop(0, CHUNKS, forward, 0)
-    for c in range(CHUNKS):
+    cotangents.relay(0)
+
+    def backward(n, carry):
+        @pl.when(n < EARLY)
+        def _():
+            cotangents.relay(n + 1)
+            cotangents.arrived(n)
+
+        mlp_backward(r, n, second)
+
+        @pl.when(n >= 1)
+        def _():
+            second.pass_on(n - 1)
+
+        @pl.when(n >= 4)
+        def _():
+            norm_step(n - 4)
+
+        return carry
+
+    def late_backward(n, carry):
+        backward(n, carry)
+        slots(IN_BACKWARD, n)
+        return carry
+
+    lax.fori_loop(0, EARLY, backward, 0)
+    for c in range(EARLY + 1, CHUNKS):
+        cotangents.relay(c)
+    for c in range(EARLY, CHUNKS):
         cotangents.arrived(c)
     r.accdn[...] = (dot(r.act[...], r.gout[...], NT) * r.share[0:1, 0:1]).astype(BF16)
     down[0].start()
     down[1].start()
-
-    def norm_step(c):
-        second_norm_back(r, spot, c, second)
-        g_att.send(c)
-
-    def backward(n, carry):
-        mlp_backward(r, n, second)
-
-        @pl.when(n >= 1)
-        def _():
-            second.pass_on(n - 1)
-
-        @pl.when(n >= 3)
-        def _():
-            norm_step(n - 3)
-
-        @pl.when(n == 3)
-        def _():
-            advance(down[0])
-
-        @pl.when(n == 6)
-        def _():
-            advance(down[1], down[0])
-
-        return carry
-
-    lax.fori_loop(0, CHUNKS, backward, 0)
+    lax.fori_loop(EARLY, CHUNKS, late_backward, 0)
     second.pass_on(CHUNKS - 1)
     r.accup[...] = (dot(r.h2[...], r.gpre[...], NT) * r.share[0:1, 0:1]).astype(BF16)
     up[0].start()
     up[1].start()
+    norm_step(3)
+    advance(AT_END.get(5, ()))
     flip(r.wqkv, r.wqkvn)
-    windows(r.qk.at[192:384])
+    for j in range(3):
+        window(r.qk.at[192:384], j)
     first = Exchange(r, spot, r.gp, r.gr, r.gs, r.gc, r.g1_sem, r.stats)
     g_att.relay(0)
 
@@ -838,42 +901,37 @@
             g_att.relay(c + 1)
 
         g_att.arrived(c)
+
+        slots(BEFORE_TILES, c)
         both_tiles(c, back_tile, r.qk.at[192:384])
-
-        @pl.when(c == 0)
-        def _():
-            advance(down[1], down[0])
+        slots(AFTER_TILES, c)
+
+        @pl.when((c >= 1) & (c <= 5))
+        def _():
+            outward.pass_on(c - 1)
 
         @pl.when(c == 2)
         def _():
             first_chunks((0, 1))
-            advance(up[0], down[1], down[0], up[1])
 
         @pl.when(c == 3)
         def _():
             first.pass_on(0)
             first.pass_on(1)
-            outward.pass_on(0)
-            outward.pass_on(1)
 
         @pl.when(c == 4)
         def _():
             first_chunks((2, 3))
-            advance(up[0], down[1], down[0])
 
         @pl.when(c == 5)
         def _():
             first.pass_on(2)
             first.pass_on(3)
-            outward.pass_on(2)
-            outward.pass_on(3)
-            advance(up[1])
 
         return carry
 
     lax.fori_loop(0, CHUNKS, back, 0)
     first_chunks((4, 5, 6))
-    advance(down[1], up[0], down[0], up[1])
     r.accqkv[...] = (dot(r.gproj[0:576, :], r.h1[...], NT) * r.share[0:1, 0:1]).astype(BF16)
     qkv = [
         Reduce(
@@ -881,30 +939,35 @@
             r.accqkv.at[OWN * n : OWN * n + OWN],
             r.arqkv[n],
             r.resqkv.at[OWN * n : OWN * n + OWN],
-            order if n < 2 else turned,
+            r.groups if n < 2 else r.turned,
             r.qr_sem.at[n],
         )
         for n in range(3)
     ]
     for reduce in qkv:
         reduce.start()
+    pieces += qkv
+    advance(AT_END.get(0, ()))
     for c in range(4, CHUNKS):
         first.pass_on(c)
     r.accwo[...] = (dot(r.atto[...], r.gatt[...], NT) * r.share[0:1, 0:1]).astype(BF16)
-    out = Reduce(spot, r.accwo, r.arwo, r.reswo, turned, r.wr_sem)
+    out = Reduce(spot, r.accwo, r.arwo, r.reswo, r.turned, r.wr_sem)
     out.start()
-    for c in range(4, CHUNKS):
-        outward.pass_on(c)
-    advance(up[0])
+    pieces.append(out)
+    outward.pass_on(5)
+    outward.pass_on(6)
+    advance(AT_END.get(1, ()))
 
     def norm_one(c, carry):
         first_norm_back(r, spot, c, first)
         return carry
 
-    lax.fori_loop(0, 5, norm_one, 0)
-    advance(down[1], qkv[2], up[1])
+    lax.fori_loop(0, 2, norm_one, 0)
+    advance(AT_END.get(2, ()))
+    lax.fori_loop(2, 5, norm_one, 0)
+    advance(AT_END.get(3, ()))
     lax.fori_loop(5, CHUNKS, norm_one, 0)
-    advance(qkv[0], out)
+    advance(AT_END.get(4, ()))
 
     def lane_sum(ref):
         return jnp.sum(ref[...], axis=1, keepdims=True)
@@ -912,7 +975,7 @@
     b_down = jnp.sum(r.gout[own, :].astype(F32), axis=1, keepdims=True)
     b_qkv = jnp.sum(r.gproj[0:576, :].astype(F32), axis=1, keepdims=True)
     columns = [
-        lane_sum(r.sbup),
+        jnp.sum(r.gpre[...].astype(F32), axis=1, keepdims=True),
         jnp.concatenate([b_qkv, lane_sum(r.sf0), lane_sum(r.sf1)], axis=0),
         jnp.concatenate([lane_sum(r.sbo), lane_sum(r.sg1), lane_sum(r.sb1), lane_sum(r.sg2)], axis=0),
         jnp.concatenate([lane_sum(r.sb2), b_down, jnp.zeros((384, 1), F32)], axis=0),
@@ -922,26 +985,29 @@
     for n, column in enumerate(columns):
         table = jnp.where(lane == n, column, table)
     table = jnp.transpose(table * r.share[0:1, 0:1])[0:8, :]
-    between = [
-        (qkv[1], up[0], qkv[2], up[1], out, qkv[0], qkv[1]),
-        (up[0], qkv[0], qkv[2], qkv[1]),
-        (qkv[0], qkv[1], up[1], out, qkv[2], qkv[0], qkv[1], out),
-    ]
-    for bit in range(r.dp_bits):
-        r.sumx[bit] = table
-        copy = remote(
-            r.sumx.at[bit], r.sumr.at[bit], r.su_sem.at[0, bit], r.su_sem.at[1, bit], peers[bit]
-        )
-        copy.start()
-        if bit < len(between):
-            advance(*between[bit])
-        copy.wait()
-        table = table + r.sumr[bit]
+    for step, bits in enumerate(r.groups):
+        r.sumx[step] = table
+        copies = [
+            remote(
+                r.sumx.at[step],
+                r.sumr.at[step, number - 1],
+                r.su_sem.at[0, step, number - 1],
+                r.su_sem.at[1, step, number - 1],
+                flipped(spot, bits, number),
+            )
+            for number in range(1, 1 << len(bits))
+        ]
+        for copy in copies:
+            copy.start()
+        if step < len(IN_SUMS):
+            advance(IN_SUMS[step])
+        for number, copy in enumerate(copies):
+            copy.wait()
+            table = table + r.sumr[step, number]
     r.sums[...] = table
     finish_out(r, spot, outward)
-    reduces = [qkv[2], qkv[0], out, qkv[1]] + up + down
-    while any(reduce.at < len(reduce.phases) for reduce in reduces):
-        advance(*reduces)
+    while any(piece.at < len(piece.phases) for piece in pieces):
+        advance(range(len(pieces)))
 
 
 def finish_out(r, spot, outward):
@@ -970,8 +1036,12 @@
         sums=((8, D), F32),
     )
 
+    groups = [(bit,) for bit in range(dp_bits)]
+    turned = groups[1:] + groups[:1]
+
     def levels(rows):
-        return [VM(shape, BF16) for shape in arrive_shapes(rows, D, dp_bits)]
+        steps = plan((rows, D), groups)
+        return [VM(((1 << len(bits)) - 1, *shape), BF16) for bits, shape, _ in steps]
 
     full = VM((D, LANES), BF16)
     own = VM((OWN, LANES), BF16)
@@ -1014,6 +1084,8 @@
         stats=VM((4, 8, LANES), F32),
         mp=VM((2, 2, OWN, LANES), BF16),
         mr=VM((2, OWN, LANES), BF16),
+        ms=own,
+        mc=own,
         gp=VM((2, 2, OWN, LANES), BF16),
         gr=VM((2, OWN, LANES), BF16),
         gs=own,
@@ -1024,7 +1096,6 @@
         arup=[levels(384), levels(384)],
         arwo=levels(OWN),
         arqkv=[levels(OWN), levels(OWN), levels(OWN)],
-        sbup=VM((D, 128), F32),
         sg1=VM((OWN, 128), F32),
         sb1=VM((OWN, 128), F32),
         sg2=VM((OWN, 128), F32),
@@ -1034,8 +1105,8 @@
         sf1=VM((96, 128), F32),
         cnts=VM((dp_bits, 8, 128), F32),
         cntr=VM((dp_bits, 8, 128), F32),
-        sumx=VM((dp_bits, 8, D), F32),
-        sumr=VM((dp_bits, 8, D), F32),
+        sumx=VM((len(groups), 8, D), F32),
+        sumr=VM((len(groups), 3, 8, D), F32),
         load_sem=dma(6),
         tk_sem=spread,
         at_sem=spread,
@@ -1044,14 +1115,14 @@
         sm_sem=dma(6),
         wo_sem=dma(6),
         cn_sem=dma(2, dp_bits),
-        su_sem=dma(2, dp_bits),
+        su_sem=dma(2, len(groups), 3),
         mo_sem=dma(8, CHUNKS),
         g2_sem=dma(8, CHUNKS),
         g1_sem=dma(8, CHUNKS),
-        dn_sem=dma(2, 2, 2 * dp_bits),
-        up_sem=dma(2, 2, 2 * dp_bits),
-        wr_sem=dma(2, 2 * dp_bits),
-        qr_sem=dma(3, 2, 2 * dp_bits),
+        dn_sem=dma(2, 2, 2 * dp_bits, 3),
+        up_sem=dma(2, 2, 2 * dp_bits, 3),
+        wr_sem=dma(2, 2 * dp_bits, 3),
+        qr_sem=dma(3, 2, 2 * dp_bits, 3),
     )
     shapes, structure = jax.tree.flatten(scratch, is_leaf=lambda leaf: not isinstance(leaf, (dict, list)))
 
@@ -1063,12 +1134,11 @@
         for name, ref in named.items():
             setattr(r, name, ref)
         r.gatt, r.atto = r.att, r.v
-        r.dq, r.gproj, r.ms = r.act, r.h2, r.act.at[OWN : 2 * OWN]
-        r.mc = r.act.at[2 * OWN : 3 * OWN]
+        r.dq, r.gproj = r.act, r.h2
         r.accdn, r.accup, r.accwo = r.wof, r.wupt, r.wdn.at[0:OWN]
         r.wqkvn = r.wot
         r.accqkv = r.wdnt.at[0:576]
-        r.dp_bits = dp_bits
+        r.dp_bits, r.groups, r.turned = dp_bits, groups, turned
         kernel(r, place())
 
     results = pl.pallas_call(

time: 211 us -> 194 us (0.919)
  Pallas kernels: 190 us -> 173 us
    pallas_call x1, Pallas kernels: 190 us -> 173 us  [run(): pl.pallas_call(body, out_shape=[jax.ShapeDtypeStruct(shape, dtype) for sh...]
where the time goes in v5:
time: 194 us
  Pallas kernels  173 us (89%)
  other arithmetic  10.1 us (5%)
  local copies, waits for them, and re-layouts  8.85 us (5%)
    pallas_call x1, Pallas kernels, run(): pl.pallas_call(body, out_shape=[jax.ShapeDtypeStruct(shape, dtype) for sh...  173 us

profile of v5, /device:TPU:0, one launch (start us, length us, event | category | flops | bytes accessed | tf_op | source)
XLA Modules:
  0.0 193.6 jit_solution(4845396502448262403)
XLA Ops:
  0.6 0.7 pad_convert_fusion
  1.3 0.7 pad_convert_fusion.2
  2.0 0.7 pad_convert_fusion.4
  2.7 0.7 convert_element_type.26
  3.4 0.7 select_select_fusion.refs_2_
  4.1 1.3 reshape.47.refs_5_
  6.0 173.3 %shard_map.289 = (bf16[192,1728]{1,0:T(8,128)(2,1)}, f32[192,1792]{1,0:T(8,128)}, bf16[768,768]{1,0:T(8,128)(2,1)}, bf16[768,768]{1,0:T(8,128)(2,1)}, bf16[192,7...) custom-call(bf16[192,1728]{1,0:T(8,128)(2,1)} %bitcast.21, bf16[192,1728]{1,0:T(8,128)(2,1)} %bitcast.22, ...), custom_call_target="tpu_custom_call" | custom-call | tf_op jit(solution)/shard_map/pallas_call | solution.py:1144
  179.4 1.5 fusion
  180.9 0.1 reshape_squeeze.7
  180.9 0.6 copy.34
  181.5 0.7 slice_reduce_fusion.1
  182.3 0.7 reshape_squeeze.6
  182.9 1.3 slice_reduce_fusion
  184.3 0.0 copy-start.1
  184.3 2.9 %convert_element_type.28 = f32[768,768]{1,0:T(8,128)} convert(bf16[768,768]{1,0:T(8,128)(2,1)} %get-tuple-element.27) | non-fusion elementwise | flops 589824 | bytes 3538944 | tf_op jit(solution)/shard_map/convert_element_type | solution.py:1224
  187.2 0.0 copy-done.1
  187.2 0.0 copy-start.2
  187.2 1.6 convert_element_type.29
  188.8 0.0 copy-start
  188.8 0.0 copy-done.2
  188.8 1.4 convert_bitcast_fusion
  190.2 0.6 copy-done
  190.8 0.0 copy-start.4
  190.8 0.0 copy-start.3
  190.8 1.2 slice_bitcast_fusion
  191.9 0.0 copy-done.4
  191.9 0.9 convert_element_type.27
  192.8 0.0 copy-done.3
  192.8 0.8 copy.37
  (4 shorter events, 0.0 us)
Async XLA Ops:
  184.3 2.9 %copy-start.1 = (bf16[768,768]{1,0:T(8,128)(2,1)S(1)}, bf16[768,768]{1,0:T(8,128)(2,1)}, u32[]{:S(2)}) copy-start(bf16[768,768]{1,0:T(8,128)(2,1)} %get-tuple-element.28) | copy-start | bytes 3538948
  187.2 1.6 copy-start.2
  188.8 2.0 %copy-start = (f32[192,1792]{1,0:T(8,128)S(1)}, f32[192,1792]{1,0:T(8,128)}, u32[]{:S(2)}) copy-start(f32[192,1792]{1,0:T(8,128)} %get-tuple-element.23) | copy-start | bytes 4128772
  190.8 1.2 copy-start.4
  190.8 2.0 %copy-start.3 = (bf16[192,1728]{1,0:T(8,128)(2,1)S(1)}, bf16[192,1728]{1,0:T(8,128)(2,1)}, u32[]{:S(2)}) copy-start(bf16[192,1728]{1,0:T(8,128)(2,1)} %get-tuple-element.22) | copy-start | bytes 1990660

commit v6 on v5

--- a/solution.py
+++ b/solution.py
@@ -33,11 +33,35 @@
 
 
 EARLY = 2
-IN_BACKWARD = {6: (0,)}
-BEFORE_TILES = {0: (0,), 1: (1,)}
-AFTER_TILES = {1: (2, 0), 2: (3, 1, 2, 0), 3: (3,), 4: (1, 2, 0, 3), 5: (1,), 6: (2, 0, 3)}
-AT_END = {1: (1, 2), 2: (3,), 4: (4, 6, 5, 7), 5: (1,)}
-IN_SUMS = ((), (4, 2, 6, 5, 7, 3), (6, 7, 4, 5))
+IN_BACKWARD, BEFORE_TILES, AFTER_TILES, IN_LAST, TAIL = range(5)
+MOVES = (
+    {6: (0,)},
+    {0: (1, 0), 2: (1,), 3: (3, 2), 5: (2,)},
+    {1: (2,), 2: (0,), 3: (1,), 4: (0, 3), 5: (1,), 6: (0,)},
+    {0: (3, 2, 1), 1: (0,), 4: (6, 4), 5: (7, 5), 6: (3,)},
+)
+IN_TAIL = (9, 2, 9, 9, 9, 9, 9, 9, 6, 1, 4, 8, 7, 5, 3, 2, 6, 8, 4, 7, 5, 8, 4, 3, 5, 6, 7, 4, 5, 6, 4, 7, 5, 6, 7)
+
+
+def numbered_moves():
+    points = [(IN_BACKWARD, n) for n in range(CHUNKS)]
+    for c in range(CHUNKS):
+        points += [(BEFORE_TILES, c), (AFTER_TILES, c)]
+    points += [(IN_LAST, n) for n in range(CHUNKS)]
+    taken = [0] * 9
+    moves = {}
+    for kind, n in points:
+        for piece in MOVES[kind].get(n, ()):
+            moves.setdefault((kind, n), []).append((piece, taken[piece]))
+            taken[piece] += 1
+    tail = []
+    for piece in IN_TAIL:
+        if piece < 9:
+            tail.append((piece, taken[piece]))
+            taken[piece] += 1
+        else:
+            tail.append((piece, 0))
+    return moves, tail, taken
 
 
 class Refs:
@@ -132,7 +156,6 @@
 class Reduce:
     def __init__(self, spot, acc, arrive, res, groups, sems):
         self.spot, self.res, self.sems = spot, res, sems
-        self.at = 0
         self.phases = []
         gathers = []
         source, row, col = acc, 0, 0
@@ -171,8 +194,8 @@
             span(corner[0], shape[0], 16, ref.shape[0]), span(corner[1], shape[1], 128, ref.shape[1])
         ]
 
-    def copies(self):
-        bits, source, corners, shape, target = self.phases[self.at]
+    def copies(self, at):
+        bits, source, corners, shape, target = self.phases[at]
         out = []
         for number in range(1, 1 << len(bits)):
             if target is None:
@@ -181,18 +204,18 @@
             else:
                 piece = self.piece(source, corners[number], shape)
                 goal = target.at[number - 1]
-            sems = (self.sems.at[0, self.at, number - 1], self.sems.at[1, self.at, number - 1])
+            sems = (self.sems.at[0, at, number - 1], self.sems.at[1, at, number - 1])
             out.append(remote(piece, goal, *sems, flipped(self.spot, bits, number)))
         return out
 
-    def start(self):
-        for copy in self.copies():
+    def start(self, at=0):
+        for copy in self.copies(at):
             copy.start()
 
-    def add(self):
-        bits, source, corners, shape, target = self.phases[self.at]
+    def add(self, at):
+        bits, source, corners, shape, target = self.phases[at]
         held = self.piece(source, corners[0], shape)
-        last = self.at == self.sums - 1
+        last = at == self.sums - 1
         goal = self.piece(self.res, self.own, shape) if last else target.at[0]
         step = 48 if shape[0] % 48 == 0 else 16
 
@@ -206,16 +229,15 @@
 
         lax.fori_loop(0, shape[0] // step, block, 0)
 
-    def advance(self):
-        if self.at >= len(self.phases):
+    def advance(self, at):
+        if at >= len(self.phases):
             return
-        for copy in self.copies():
+        for copy in self.copies(at):
             copy.wait()
-        if self.at < self.sums:
-            self.add()
-        self.at += 1
-        if self.at < len(self.phases):
-            self.start()
+        if at < self.sums:
+            self.add(at)
+        if at + 1 < len(self.phases):
+            self.start(at + 1)
 
 
 class Exchange:
@@ -811,17 +833,19 @@
 
     pieces = down + up
 
-    def advance(numbers):
-        for number in numbers:
-            if number < len(pieces):
-                pieces[number].advance()
-
-    def slots(table, n):
-        for at in sorted(table):
-
-            @pl.when(n == at)
-            def _():
-                advance(table[at])
+    moves, tail, taken = numbered_moves()
+
+    def move(kind, n):
+        for piece, step in moves.get((kind, n), ()):
+            pieces[piece].advance(step)
+
+    def slots(kind, n):
+        for point, at in sorted(moves):
+            if point == kind:
+
+                @pl.when(n == at)
+                def _():
+                    move(kind, at)
 
     def norm_step(c):
         second_norm_back(r, spot, c, second)
@@ -876,21 +900,12 @@
     up[0].start()
     up[1].start()
     norm_step(3)
-    advance(AT_END.get(5, ()))
     flip(r.wqkv, r.wqkvn)
     for j in range(3):
         window(r.qk.at[192:384], j)
     first = Exchange(r, spot, r.gp, r.gr, r.gs, r.gc, r.g1_sem, r.stats)
     g_att.relay(0)
 
-    def first_chunks(chunks):
-        def one(c, carry):
-            unrotate(r, c)
-            first_part(r, c, first)
-            return carry
-
-        lax.fori_loop(chunks[0], chunks[-1] + 1, one, 0)
-
     def back(c, carry):
         @pl.when(c + 4 < CHUNKS)
         def _():
@@ -906,13 +921,18 @@
         both_tiles(c, back_tile, r.qk.at[192:384])
         slots(AFTER_TILES, c)
 
-        @pl.when((c >= 1) & (c <= 5))
-        def _():
-            outward.pass_on(c - 1)
+        def ready(chunks, give):
+            def one(n, carry):
+                unrotate(r, n)
+                if give:
+                    first_part(r, n, first)
+                return carry
+
+            lax.fori_loop(chunks[0], chunks[-1] + 1, one, 0)
 
         @pl.when(c == 2)
         def _():
-            first_chunks((0, 1))
+            ready((0, 1), True)
 
         @pl.when(c == 3)
         def _():
@@ -921,17 +941,22 @@
 
         @pl.when(c == 4)
         def _():
-            first_chunks((2, 3))
+            ready((2, 3), True)
 
         @pl.when(c == 5)
         def _():
             first.pass_on(2)
             first.pass_on(3)
 
+        @pl.when(c == 6)
+        def _():
+            outward.pass_on(0)
+            outward.pass_on(1)
+            ready((4, 5, 6), False)
+
         return carry
 
     lax.fori_loop(0, CHUNKS, back, 0)
-    first_chunks((4, 5, 6))
     r.accqkv[...] = (dot(r.gproj[0:576, :], r.h1[...], NT) * r.share[0:1, 0:1]).astype(BF16)
     qkv = [
         Reduce(
@@ -947,27 +972,26 @@
     for reduce in qkv:
         reduce.start()
     pieces += qkv
-    advance(AT_END.get(0, ()))
-    for c in range(4, CHUNKS):
-        first.pass_on(c)
+    lax.fori_loop(4, CHUNKS, lambda n, carry: (first_part(r, n, first), carry)[1], 0)
     r.accwo[...] = (dot(r.atto[...], r.gatt[...], NT) * r.share[0:1, 0:1]).astype(BF16)
     out = Reduce(spot, r.accwo, r.arwo, r.reswo, r.turned, r.wr_sem)
     out.start()
     pieces.append(out)
-    outward.pass_on(5)
-    outward.pass_on(6)
-    advance(AT_END.get(1, ()))
-
-    def norm_one(c, carry):
-        first_norm_back(r, spot, c, first)
+
+    def last(n, carry):
+        @pl.when(n < 3)
+        def _():
+            first.pass_on(n + 4)
+
+        @pl.when(n >= 2)
+        def _():
+            outward.pass_on(n)
+
+        first_norm_back(r, spot, n, first)
+        slots(IN_LAST, n)
         return carry
 
-    lax.fori_loop(0, 2, norm_one, 0)
-    advance(AT_END.get(2, ()))
-    lax.fori_loop(2, 5, norm_one, 0)
-    advance(AT_END.get(3, ()))
-    lax.fori_loop(5, CHUNKS, norm_one, 0)
-    advance(AT_END.get(4, ()))
+    lax.fori_loop(0, CHUNKS, last, 0)
 
     def lane_sum(ref):
         return jnp.sum(ref[...], axis=1, keepdims=True)
@@ -985,38 +1009,50 @@
     for n, column in enumerate(columns):
         table = jnp.where(lane == n, column, table)
     table = jnp.transpose(table * r.share[0:1, 0:1])[0:8, :]
-    for step, bits in enumerate(r.groups):
-        r.sumx[step] = table
-        copies = [
-            remote(
-                r.sumx.at[step],
-                r.sumr.at[step, number - 1],
-                r.su_sem.at[0, step, number - 1],
-                r.su_sem.at[1, step, number - 1],
-                flipped(spot, bits, number),
-            )
-            for number in range(1, 1 << len(bits))
-        ]
-        for copy in copies:
-            copy.start()
-        if step < len(IN_SUMS):
-            advance(IN_SUMS[step])
-        for number, copy in enumerate(copies):
-            copy.wait()
-            table = table + r.sumr[step, number]
-    r.sums[...] = table
-    finish_out(r, spot, outward)
-    while any(piece.at < len(piece.phases) for piece in pieces):
-        advance(range(len(pieces)))
-
-
-def finish_out(r, spot, outward):
-    for c in range(CHUNKS):
-        at = lanes(c)
-        total = outward.take(c)
-        whole = r.mido[:, at] + (total + r.cols[0:192, 9:10])
-        r.gs[:, at] = (r.info[2:3, at] * whole).astype(BF16)
+    vectors = Vectors(r, spot, table)
+    vectors.start()
+    pieces.append(vectors)
+    finished = 0
+    for piece, step in tail:
+        if piece < 9:
+            pieces[piece].advance(step)
+        else:
+            finish_out(r, outward, finished)
+            finished += 1
     r.out[...] = r.gs[:, 0:ROWS]
+    for step in range(2 * r.dp_bits):
+        for piece, first_step in zip(pieces, taken, strict=True):
+            piece.advance(first_step + step)
+    r.sums[...] = vectors.table
+
+
+class Vectors:
+    def __init__(self, r, spot, table):
+        self.r, self.spot, self.table = r, spot, table
+
+    def copy(self, at):
+        r = self.r
+        return remote(
+            r.sumx.at[at], r.sumr.at[at], r.su_sem.at[0, at], r.su_sem.at[1, at], dp_partner(self.spot, at)
+        )
+
+    def start(self, at=0):
+        self.r.sumx[at] = self.table
+        self.copy(at).start()
+
+    def advance(self, at):
+        if at >= self.r.dp_bits:
+            return
+        self.copy(at).wait()
+        self.table = self.table + self.r.sumr[at]
+        if at + 1 < self.r.dp_bits:
+            self.start(at + 1)
+
+
+def finish_out(r, outward, c):
+    at = lanes(c)
+    whole = r.mido[:, at] + (outward.take(c) + r.cols[0:192, 9:10])
+    r.gs[:, at] = (r.info[2:3, at] * whole).astype(BF16)
 
 
 def dma(*shape):
@@ -1105,8 +1141,8 @@
         sf1=VM((96, 128), F32),
         cnts=VM((dp_bits, 8, 128), F32),
         cntr=VM((dp_bits, 8, 128), F32),
-        sumx=VM((len(groups), 8, D), F32),
-        sumr=VM((len(groups), 3, 8, D), F32),
+        sumx=VM((dp_bits, 8, D), F32),
+        sumr=VM((dp_bits, 8, D), F32),
         load_sem=dma(6),
         tk_sem=spread,
         at_sem=spread,
@@ -1115,7 +1151,7 @@
         sm_sem=dma(6),
         wo_sem=dma(6),
         cn_sem=dma(2, dp_bits),
-        su_sem=dma(2, len(groups), 3),
+        su_sem=dma(2, dp_bits),
         mo_sem=dma(8, CHUNKS),
         g2_sem=dma(8, CHUNKS),
         g1_sem=dma(8, CHUNKS),

time: 194 us -> 188 us (0.969)
  Pallas kernels: 173 us -> 167 us
    pallas_call x1, Pallas kernels: 173 us -> 167 us  [run(): pl.pallas_call(body, out_shape=[jax.ShapeDtypeStruct(shape, dtype) for sh...]
where the time goes in v6:
time: 188 us
  Pallas kernels  167 us (89%)
  other arithmetic  10.1 us (5%)
  local copies, waits for them, and re-layouts  8.85 us (5%)
    pallas_call x1, Pallas kernels, run(): pl.pallas_call(body, out_shape=[jax.ShapeDtypeStruct(shape, dtype) for sh...  167 us

profile of v6, /device:TPU:0, one launch (start us, length us, event | category | flops | bytes accessed | tf_op | source)
XLA Modules:
  0.0 187.7 jit_solution(14194501527743681515)
XLA Ops:
  0.6 0.7 pad_convert_fusion
  1.3 0.7 pad_convert_fusion.2
  2.0 0.7 pad_convert_fusion.4
  2.7 0.7 convert_element_type.26
  3.4 0.7 select_select_fusion.refs_2_
  4.1 1.3 reshape.47.refs_5_
  6.0 167.4 %shard_map.289 = (bf16[192,1728]{1,0:T(8,128)(2,1)}, f32[192,1792]{1,0:T(8,128)}, bf16[768,768]{1,0:T(8,128)(2,1)}, bf16[768,768]{1,0:T(8,128)(2,1)}, bf16[192,7...) custom-call(bf16[192,1728]{1,0:T(8,128)(2,1)} %bitcast.21, bf16[192,1728]{1,0:T(8,128)(2,1)} %bitcast.22, ...), custom_call_target="tpu_custom_call" | custom-call | tf_op jit(solution)/shard_map/pallas_call | solution.py:1180
  173.4 1.5 fusion
  175.0 0.1 reshape_squeeze.7
  175.0 0.6 copy.34
  175.6 0.7 slice_reduce_fusion.1
  176.4 0.7 reshape_squeeze.6
  177.0 1.3 slice_reduce_fusion
  178.4 0.0 copy-start.1
  178.4 2.9 %convert_element_type.28 = f32[768,768]{1,0:T(8,128)} convert(bf16[768,768]{1,0:T(8,128)(2,1)} %get-tuple-element.27) | non-fusion elementwise | flops 589824 | bytes 3538944 | tf_op jit(solution)/shard_map/convert_element_type | solution.py:1260
  181.3 0.0 copy-done.1
  181.3 0.0 copy-start.2
  181.3 1.6 convert_element_type.29
  182.9 0.0 copy-start
  182.9 0.0 copy-done.2
  182.9 1.4 convert_bitcast_fusion
  184.3 0.6 copy-done
  184.9 0.0 copy-start.4
  184.9 0.0 copy-start.3
  184.9 1.2 slice_bitcast_fusion
  186.0 0.0 copy-done.4
  186.0 0.9 convert_element_type.27
  186.9 0.0 copy-done.3
  186.9 0.8 copy.37
  (4 shorter events, 0.0 us)
Async XLA Ops:
  178.4 2.9 %copy-start.1 = (bf16[768,768]{1,0:T(8,128)(2,1)S(1)}, bf16[768,768]{1,0:T(8,128)(2,1)}, u32[]{:S(2)}) copy-start(bf16[768,768]{1,0:T(8,128)(2,1)} %get-tuple-element.28) | copy-start | bytes 3538948
  181.3 1.6 copy-start.2
  182.9 2.0 %copy-start = (f32[192,1792]{1,0:T(8,128)S(1)}, f32[192,1792]{1,0:T(8,128)}, u32[]{:S(2)}) copy-start(f32[192,1792]{1,0:T(8,128)} %get-tuple-element.23) | copy-start | bytes 4128772
  184.9 1.2 copy-start.4
  184.9 2.0 %copy-start.3 = (bf16[192,1728]{1,0:T(8,128)(2,1)S(1)}, bf16[192,1728]{1,0:T(8,128)(2,1)}, u32[]{:S(2)}) copy-start(bf16[192,1728]{1,0:T(8,128)(2,1)} %get-tuple-element.22) | copy-start | bytes 1990660

commit v7 on v6

--- a/solution.py
+++ b/solution.py
@@ -35,12 +35,12 @@
 EARLY = 2
 IN_BACKWARD, BEFORE_TILES, AFTER_TILES, IN_LAST, TAIL = range(5)
 MOVES = (
-    {6: (0,)},
-    {0: (1, 0), 2: (1,), 3: (3, 2), 5: (2,)},
-    {1: (2,), 2: (0,), 3: (1,), 4: (0, 3), 5: (1,), 6: (0,)},
-    {0: (3, 2, 1), 1: (0,), 4: (6, 4), 5: (7, 5), 6: (3,)},
+    {6: (0, 1,)},
+    {0: (0, 1,), 2: (0,), 3: (2,), 5: (2, 0,), 6: (1,)},
+    {1: (2,), 2: (1, 3,), 3: (0,), 4: (1, 3,)},
+    {0: (3, 2, 0, 1,), 3: (4, 6,), 5: (5, 3,), 6: (2, 7, 4,)},
 )
-IN_TAIL = (9, 2, 9, 9, 9, 9, 9, 9, 6, 1, 4, 8, 7, 5, 3, 2, 6, 8, 4, 7, 5, 8, 4, 3, 5, 6, 7, 4, 5, 6, 4, 7, 5, 6, 7)
+IN_TAIL = (6, 9, 5, 9, 9, 9, 9, 9, 9, 3, 7, 4, 2, 6, 8, 5, 7, 8, 4, 6, 3, 5, 7, 4, 8, 6, 5, 7, 4, 6, 5, 7)
 
 
 def numbered_moves():
@@ -432,16 +432,23 @@
 
 def row_tables(r):
     pad = jnp.zeros((1, D - 3 * OWN), F32)
+    rest = jnp.zeros((1, D - OWN), F32)
     qkv = jnp.concatenate([r.bqkv[n : n + 1, :].astype(F32) for n in range(3)] + [pad], axis=1)
     pad = jnp.zeros((2, D - 96), F32)
     freqs = jnp.concatenate([r.freqs[h] for h in range(3)] + [pad], axis=1)
     table = jnp.concatenate(
-        [r.pack[0:1, :], qkv, freqs, r.pack[1:8, :], jnp.zeros((117, D), F32)], axis=0
+        [r.b_up[...].astype(F32).reshape(1, D), qkv, freqs]
+        + [
+            jnp.concatenate([ref[...].astype(F32).reshape(1, OWN), rest], axis=1)
+            for ref in (r.gain1, r.bias1, r.gain2, r.bias2, r.b_out, r.b_down)
+        ]
+        + [jnp.zeros((118, D), F32)],
+        axis=0,
     )
     for i in range(D // 128):
         r.cols[128 * i : 128 * i + 128, :] = jnp.transpose(table[:, 128 * i : 128 * i + 128])
     low = 1.0 - r.group[0].astype(F32)
-    keep = r.keep[...].astype(F32)
+    keep = r.keep[...].astype(F32).reshape(1, ROWS)
     middle = lax.broadcasted_iota(jnp.int32, (1, ROWS), 1).astype(F32) + 0.5
     segment = low * jnp.floor(middle * (1.0 / (GRID_LO * GRID_LO))) + (1.0 - low) * jnp.floor(
         middle * (1.0 / SLOTS)
@@ -814,7 +821,7 @@
     second = Exchange(r, spot, r.gp, r.gr, r.gs, r.gc, r.g2_sem, r.stats)
     g_att = Spread(spot, r.gatt, r.ga_sem)
 
-    def halves(acc, arrive, res, sems):
+    def halves(acc, arrive, res, sems, orders):
         rows = acc.shape[0] // 2
         return [
             Reduce(
@@ -822,14 +829,14 @@
                 acc.at[rows * n : rows * n + rows],
                 arrive[n],
                 res.at[rows * n : rows * n + rows],
-                r.groups,
+                orders[n],
                 sems.at[n],
             )
             for n in range(2)
         ]
 
-    down = halves(r.accdn, r.ardn, r.resdn, r.dn_sem)
-    up = halves(r.accup, r.arup, r.resup, r.up_sem)
+    down = halves(r.accdn, r.ardn, r.resdn, r.dn_sem, (r.swapped, r.groups))
+    up = halves(r.accup, r.arup, r.resup, r.up_sem, (r.groups, r.groups))
 
     pieces = down + up
 
@@ -964,7 +971,7 @@
             r.accqkv.at[OWN * n : OWN * n + OWN],
             r.arqkv[n],
             r.resqkv.at[OWN * n : OWN * n + OWN],
-            r.groups if n < 2 else r.turned,
+            r.groups if n < 2 else r.swapped,
             r.qr_sem.at[n],
         )
         for n in range(3)
@@ -974,7 +981,7 @@
     pieces += qkv
     lax.fori_loop(4, CHUNKS, lambda n, carry: (first_part(r, n, first), carry)[1], 0)
     r.accwo[...] = (dot(r.atto[...], r.gatt[...], NT) * r.share[0:1, 0:1]).astype(BF16)
-    out = Reduce(spot, r.accwo, r.arwo, r.reswo, r.turned, r.wr_sem)
+    out = Reduce(spot, r.accwo, r.arwo, r.reswo, r.groups, r.wr_sem)
     out.start()
     pieces.append(out)
 
@@ -998,12 +1005,15 @@
 
     b_down = jnp.sum(r.gout[own, :].astype(F32), axis=1, keepdims=True)
     b_qkv = jnp.sum(r.gproj[0:576, :].astype(F32), axis=1, keepdims=True)
+    turn = (lane_sum(r.sf0), lane_sum(r.sf1))
+    turns = [turn[n][32 * h : 32 * h + 32] for h in range(3) for n in range(2)]
     columns = [
         jnp.sum(r.gpre[...].astype(F32), axis=1, keepdims=True),
-        jnp.concatenate([b_qkv, lane_sum(r.sf0), lane_sum(r.sf1)], axis=0),
         jnp.concatenate([lane_sum(r.sbo), lane_sum(r.sg1), lane_sum(r.sb1), lane_sum(r.sg2)], axis=0),
-        jnp.concatenate([lane_sum(r.sb2), b_down, jnp.zeros((384, 1), F32)], axis=0),
+        jnp.concatenate([lane_sum(r.sb2), b_down] + turns + [jnp.zeros((OWN, 1), F32)], axis=0),
     ]
+    rest = jnp.zeros((D - OWN, 1), F32)
+    columns += [jnp.concatenate([b_qkv[OWN * n : OWN * n + OWN], rest], axis=0) for n in range(3)]
     lane = lax.broadcasted_iota(jnp.int32, (D, 128), 1)
     table = jnp.zeros((D, 128), F32)
     for n, column in enumerate(columns):
@@ -1073,7 +1083,7 @@
     )
 
     groups = [(bit,) for bit in range(dp_bits)]
-    turned = groups[1:] + groups[:1]
+    swapped = groups[1::-1] + groups[2:]
 
     def levels(rows):
         steps = plan((rows, D), groups)
@@ -1174,7 +1184,7 @@
         r.accdn, r.accup, r.accwo = r.wof, r.wupt, r.wdn.at[0:OWN]
         r.wqkvn = r.wot
         r.accqkv = r.wdnt.at[0:576]
-        r.dp_bits, r.groups, r.turned = dp_bits, groups, turned
+        r.dp_bits, r.groups, r.swapped = dp_bits, groups, swapped
         kernel(r, place())
 
     results = pl.pallas_call(
@@ -1220,21 +1230,20 @@
 ):
     row_count, width_loc = tokens.shape
     heads_loc = freqs.shape[1]
-    row = lax.broadcasted_iota(jnp.int32, (8, D), 0)
-    pack = jnp.zeros((8, D), F32)
-    vectors = (b_up, norm1_gain, norm1_bias, norm2_gain, norm2_bias, b_out, b_down)
-    for n, vector in enumerate(vectors):
-        wide = jnp.pad(vector.astype(F32), (0, D - vector.shape[0]))
-        pack = jnp.where(row == n, wide[None, :], pack)
-
     a = run(
         lax.axis_size("dp").bit_length() - 1,
         tok=tokens.T,
         cot=cotangent.T,
-        pack=pack,
+        b_up=b_up,
+        gain1=norm1_gain,
+        bias1=norm1_bias,
+        gain2=norm2_gain,
+        bias2=norm2_bias,
+        b_out=b_out,
+        b_down=b_down,
         bqkv=b_qkv,
         freqs=freqs.transpose(1, 0, 2),
-        keep=keep_mask.reshape(1, row_count),
+        keep=keep_mask,
         coords=coords,
         group=block_group,
         in_wqkv=w_qkv.transpose(1, 2, 0).reshape(3 * width_loc, D),
@@ -1244,23 +1253,23 @@
     )
     sums = a.sums
     grad_qkv = a.resqkv.astype(F32)
-    half = (2, heads_loc, HEAD_DIM // 2)
+    turns = sums[2, 2 * width_loc : 3 * width_loc].reshape(heads_loc, 2, HEAD_DIM // 2)
     return (
         a.out.T,
         a.igrad[:, :row_count].T,
         grad_qkv.reshape(3, width_loc, D).transpose(2, 0, 1),
-        sums[1, : 3 * width_loc].reshape(3, width_loc),
-        sums[1, 3 * width_loc :].reshape(half),
+        sums[3:6, :width_loc],
+        turns.transpose(1, 0, 2),
         a.reswo.astype(F32),
+        sums[1, 0:192],
+        sums[1, 192:384],
+        sums[1, 384:576],
+        sums[1, 576:768],
         sums[2, 0:192],
-        sums[2, 192:384],
-        sums[2, 384:576],
-        sums[2, 576:768],
-        sums[3, 0:192],
         a.resup.astype(F32),
         sums[0],
         a.resdn.astype(F32),
-        sums[3, 192:384],
+        sums[2, 192:384],
     )
 
 

time: 188 us -> 180 us (0.957)
  other arithmetic: 10.1 us -> 6.72 us
  Pallas kernels: 167 us -> 164 us
    pallas_call x1, Pallas kernels: 167 us -> 164 us  [run(): pl.pallas_call(body, out_shape=[jax.ShapeDtypeStruct(shape, dtype) for sh...]
    pad x3 -> x0, other arithmetic: 2.02 us -> none  [local(): wide = jnp.pad(vector.astype(F32), (0, D - vector.shape[0]))]
where the time goes in v7:
time: 180 us; the launch traced here: 179 us
  Pallas kernels  164 us (91%)
  local copies, waits for them, and re-layouts  7.43 us (4%)
  other arithmetic  6.72 us (4%)
    pallas_call x1, Pallas kernels, run(): pl.pallas_call(body, out_shape=[jax.ShapeDtypeStruct(shape, dtype) for sh...  164 us

profile of v7, /device:TPU:0, one launch (start us, length us, event | category | flops | bytes accessed | tf_op | source)
XLA Modules:
  0.0 179.2 jit_solution(6442671557319297500)
XLA Ops:
  1.3 163.7 %shard_map.289 = (bf16[192,1728]{1,0:T(8,128)(2,1)}, f32[192,1792]{1,0:T(8,128)}, bf16[768,768]{1,0:T(8,128)(2,1)}, bf16[768,768]{1,0:T(8,128)(2,1)}, bf16[192,7...) custom-call(bf16[192,1728]{1,0:T(8,128)(2,1)} %bitcast.22, bf16[192,1728]{1,0:T(8,128)(2,1)} %bitcast.23, ...), custom_call_target="tpu_custom_call" | custom-call | tf_op jit(solution)/shard_map/pallas_call | solution.py:1190
  165.0 1.5 fusion
  166.5 0.7 reshape_squeeze.3
  167.2 1.3 slice.31
  168.5 1.3 slice_reduce_fusion
  169.8 0.0 copy-start.1
  169.8 2.9 %convert_element_type.11 = f32[768,768]{1,0:T(8,128)} convert(bf16[768,768]{1,0:T(8,128)(2,1)} %get-tuple-element.27) | non-fusion elementwise | flops 589824 | bytes 3538944 | tf_op jit(solution)/shard_map/convert_element_type | solution.py:1269
  172.8 0.0 copy-done.1
  172.8 0.0 copy-start.2
  172.8 1.6 convert_element_type.12
  174.3 0.0 copy-start
  174.3 0.0 copy-done.2
  174.3 1.4 convert_bitcast_fusion
  175.7 0.6 copy-done
  176.3 0.0 copy-start.4
  176.3 0.0 copy-start.3
  176.3 1.2 slice_bitcast_fusion
  177.5 0.0 copy-done.4
  177.5 0.9 convert_element_type.10
  178.3 0.0 copy-done.3
  178.3 0.8 copy.35
Async XLA Ops:
  169.8 2.9 %copy-start.1 = (bf16[768,768]{1,0:T(8,128)(2,1)S(1)}, bf16[768,768]{1,0:T(8,128)(2,1)}, u32[]{:S(2)}) copy-start(bf16[768,768]{1,0:T(8,128)(2,1)} %get-tuple-element.28) | copy-start | bytes 3538948
  172.8 1.6 copy-start.2
  174.3 2.0 %copy-start = (f32[192,1792]{1,0:T(8,128)S(1)}, f32[192,1792]{1,0:T(8,128)}, u32[]{:S(2)}) copy-start(f32[192,1792]{1,0:T(8,128)} %get-tuple-element.23) | copy-start | bytes 4128772
  176.3 1.2 copy-start.4
  176.3 2.0 %copy-start.3 = (bf16[192,1728]{1,0:T(8,128)(2,1)S(1)}, bf16[192,1728]{1,0:T(8,128)(2,1)}, u32[]{:S(2)}) copy-start(bf16[192,1728]{1,0:T(8,128)(2,1)} %get-tuple-element.22) | copy-start | bytes 1990660

commit v8 on v7

--- a/solution.py
+++ b/solution.py
@@ -32,15 +32,15 @@
 inv_root_two_pi = 0.3989422804014327
 
 
-EARLY = 2
+EARLY = 1
 IN_BACKWARD, BEFORE_TILES, AFTER_TILES, IN_LAST, TAIL = range(5)
 MOVES = (
-    {6: (0, 1,)},
-    {0: (0, 1,), 2: (0,), 3: (2,), 5: (2, 0,), 6: (1,)},
-    {1: (2,), 2: (1, 3,), 3: (0,), 4: (1, 3,)},
-    {0: (3, 2, 0, 1,), 3: (4, 6,), 5: (5, 3,), 6: (2, 7, 4,)},
+    {5: (0, 1,)},
+    {0: (0, 1,), 2: (1,), 3: (3, 0, 2,), 5: (2,)},
+    {1: (0, 2,), 3: (1,), 4: (3, 0,), 5: (1,), 6: (3,)},
+    {0: (0, 2, 1, 3,), 3: (4, 5,), 5: (6, 7, 4,), 6: (2,)},
 )
-IN_TAIL = (6, 9, 5, 9, 9, 9, 9, 9, 9, 3, 7, 4, 2, 6, 8, 5, 7, 8, 4, 6, 3, 5, 7, 4, 8, 6, 5, 7, 4, 6, 5, 7)
+IN_TAIL = (9, 9, 9, 9, 6, 3, 9, 9, 9, 5, 7, 4, 6, 2, 5, 8, 7, 4, 8, 6, 5, 3, 7, 4, 8, 6, 5, 7, 4, 5, 6, 7)
 
 
 def numbered_moves():
@@ -971,7 +971,7 @@
             r.accqkv.at[OWN * n : OWN * n + OWN],
             r.arqkv[n],
             r.resqkv.at[OWN * n : OWN * n + OWN],
-            r.groups if n < 2 else r.swapped,
+            r.swapped if n != 1 else r.groups,
             r.qr_sem.at[n],
         )
         for n in range(3)

time: 180 us -> 182 us (1.011)
  Pallas kernels: 164 us -> 166 us
    pallas_call x1, Pallas kernels: 164 us -> 166 us  [run(): pl.pallas_call(body, out_shape=[jax.ShapeDtypeStruct(shape, dtype) for sh...]
where the time goes in v8:
time: 182 us; the launch traced here: 181 us
  Pallas kernels  166 us (91%)
  local copies, waits for them, and re-layouts  7.43 us (4%)
  other arithmetic  6.72 us (4%)
    pallas_call x1, Pallas kernels, run(): pl.pallas_call(body, out_shape=[jax.ShapeDtypeStruct(shape, dtype) for sh...  166 us

profile of v8, /device:TPU:0, one launch (start us, length us, event | category | flops | bytes accessed | tf_op | source)
XLA Modules:
  0.0 181.5 jit_solution(18213687981513938667)
XLA Ops:
  1.3 166.0 %shard_map.289 = (bf16[192,1728]{1,0:T(8,128)(2,1)}, f32[192,1792]{1,0:T(8,128)}, bf16[768,768]{1,0:T(8,128)(2,1)}, bf16[768,768]{1,0:T(8,128)(2,1)}, bf16[192,7...) custom-call(bf16[192,1728]{1,0:T(8,128)(2,1)} %bitcast.22, bf16[192,1728]{1,0:T(8,128)(2,1)} %bitcast.23, ...), custom_call_target="tpu_custom_call" | custom-call | tf_op jit(solution)/shard_map/pallas_call | solution.py:1190
  167.3 1.5 fusion
  168.8 0.7 reshape_squeeze.3
  169.5 1.3 slice.31
  170.8 1.3 slice_reduce_fusion
  172.1 0.0 copy-start.1
  172.1 2.9 %convert_element_type.11 = f32[768,768]{1,0:T(8,128)} convert(bf16[768,768]{1,0:T(8,128)(2,1)} %get-tuple-element.27) | non-fusion elementwise | flops 589824 | bytes 3538944 | tf_op jit(solution)/shard_map/convert_element_type | solution.py:1269
  175.1 0.0 copy-done.1
  175.1 0.0 copy-start.2
  175.1 1.6 convert_element_type.12
  176.7 0.0 copy-start
  176.7 0.0 copy-done.2
  176.7 1.4 convert_bitcast_fusion
  178.0 0.6 copy-done
  178.6 0.0 copy-start.4
  178.6 0.0 copy-start.3
  178.6 1.2 slice_bitcast_fusion
  179.8 0.0 copy-done.4
  179.8 0.9 convert_element_type.10
  180.6 0.0 copy-done.3
  180.6 0.8 copy.35
Async XLA Ops:
  172.1 2.9 %copy-start.1 = (bf16[768,768]{1,0:T(8,128)(2,1)S(1)}, bf16[768,768]{1,0:T(8,128)(2,1)}, u32[]{:S(2)}) copy-start(bf16[768,768]{1,0:T(8,128)(2,1)} %get-tuple-element.28) | copy-start | bytes 3538948
  175.1 1.6 copy-start.2
  176.7 2.0 %copy-start = (f32[192,1792]{1,0:T(8,128)S(1)}, f32[192,1792]{1,0:T(8,128)}, u32[]{:S(2)}) copy-start(f32[192,1792]{1,0:T(8,128)} %get-tuple-element.23) | copy-start | bytes 4128772
  178.6 1.2 copy-start.4
  178.6 2.0 %copy-start.3 = (bf16[192,1728]{1,0:T(8,128)(2,1)S(1)}, bf16[192,1728]{1,0:T(8,128)(2,1)}, u32[]{:S(2)}) copy-start(bf16[192,1728]{1,0:T(8,128)(2,1)} %get-tuple-element.22) | copy-start | bytes 1990660
